TPU v7x, 32 devices: a whole 2x2x4 slice. The times are simulated.
32 devices in a mesh: dp: 8 (over z, x), seq: 4 (over y, core).
Axes of the slice: x: 2, y: 2, z: 4, core: 2. Of those that a mesh axis runs over, the one named last changes fastest.
Arguments:
- tokens: bfloat16 [12288, 1408], P(('dp', 'seq')), may hold values from -6 to 6
- skip: bfloat16 [12288, 1408], P(('dp', 'seq')), may hold values from -6 to 6
- segment_ids: int32 [8, 1536], P('dp'), may hold values from 0 to 2, as said below
- grid_widths: int32 [8, 3], P('dp'), may hold values from 16 to 32
- clip_lengths: int32 [8, 3], P('dp'), may hold values from 1 to 77
- t5_lengths: int32 [8, 3], P('dp'), may hold values from 1 to 256
- timestep: bfloat16 [8, 3, 1408], P('dp'), may hold values from -6 to 6
- captions: bfloat16 [8, 999, 1024], P('dp'), may hold values from -6 to 6
- ln_gains: float32 [5, 1408], replicated, may hold values from 0.5 to 1.5
- ln_biases: float32 [5, 1408], replicated, may hold values from -1.25 to 1.25
- qk_gains: float32 [2, 88], replicated, may hold values from 0.5 to 1.5
- qk_biases: float32 [2, 88], replicated, may hold values from -1.25 to 1.25
- w_skip: bfloat16 [2816, 1408], P('dp'), may hold values from -0.109375 to 0.109375
- w_mod: bfloat16 [1408, 1408], P('dp'), may hold values from -0.15625 to 0.15625
- w_qkv: bfloat16 [1408, 4224], P('dp'), may hold values from -0.15625 to 0.15625
- w_out: bfloat16 [1408, 1408], P('dp'), may hold values from -3.5 to 3.5
- w_cq: bfloat16 [1408, 1408], P('dp'), may hold values from -0.15625 to 0.15625
- w_ckv: bfloat16 [1024, 2816], P('dp'), may hold values from -0.1875 to 0.1875
- w_co: bfloat16 [1408, 1408], P('dp'), may hold values from -1.5 to 1.5
- w_up: bfloat16 [1408, 6144], P('dp'), may hold values from -0.15625 to 0.15625
- w_down: bfloat16 [6144, 1408], P('dp'), may hold values from -0.078125 to 0.078125
- cotangent: bfloat16 [12288, 1408], P(('dp', 'seq')), may hold values from -6 to 6
Outputs:
- block_out: bfloat16 [12288, 1408], P(('dp', 'seq'))
- grad_tokens: bfloat16 [12288, 1408], P(('dp', 'seq'))
- grad_skip: bfloat16 [12288, 1408], P(('dp', 'seq'))
- grad_ln_gains: float32 [5, 1408], replicated
- grad_ln_biases: float32 [4, 1408], replicated
- grad_ff_bias: float32 [1408], replicated
- grad_qk_gains: float32 [2, 88], replicated
- grad_qk_biases: float32 [2, 88], replicated
- grad_w_skip: float32 [2816, 1408], P('dp')
- grad_w_mod: float32 [1408, 1408], P('dp')
- grad_w_qkv: float32 [1408, 4224], P('dp')
- grad_w_out: float32 [1408, 1408], P('dp')
- grad_w_cq: float32 [1408, 1408], P('dp')
- grad_w_ckv: float32 [1024, 2816], P('dp')
- grad_w_co: float32 [1408, 1408], P('dp')
- grad_w_up: float32 [1408, 6144], P('dp')
- grad_w_down: float32 [6144, 1408], P('dp')
Inputs may be any that keep to these rules, and one draw needn't show every extreme that they name: `segment_ids`: in each bucket the image numbers never fall, every one of the 3 images has at least one token, and each image is one contiguous run.
All inputs are finite; a program needn't handle non-finite values.
Results may differ from a plain program's by a relative error of at most 0.025.
Values may be sent and summed in bfloat16 or wider, within the bound.
No kernel may reach another device: no remote copies, remote signals or barrier semaphores. Data moves between devices by JAX's collectives and lax.ppermute only.
A program may use at most 384 MiB of HBM per device.

v0:
```python
import jax
import jax.numpy as jnp
from jax import lax
from jax.sharding import PartitionSpec as P

HEADS = 16
HEAD = 88
CLIP_TOK = 77
IMGS = 3
CAP = 333


eps_norm = 1e-06
masked_score = -1e30


def matmul(left, right):
    return jnp.dot(left, right, preferred_element_type=jnp.float32)


def layer_norm(values, norm_gain, norm_bias):
    center = values - jnp.mean(values, axis=-1, keepdims=True)
    spread = jnp.mean(center * center, axis=-1, keepdims=True)
    return center * lax.rsqrt(spread + eps_norm) * norm_gain + norm_bias


def gelu_tanh(values):
    return (
        0.5
        * values
        * (1.0 + jnp.tanh(0.7978845608028654 * (values + 0.044715 * values * values * values)))
    )


def silu_gate(values):
    return values * jax.nn.sigmoid(values)


def soft_rows(scores):
    row_max = jnp.max(scores, axis=-1, keepdims=True)
    exp_scores = jnp.exp(scores - row_max)
    return exp_scores / jnp.sum(exp_scores, axis=-1, keepdims=True)


def rotate_half(values, cos_part, sin_part):
    quarter = values.shape[-1] // 2
    front_half = values[..., :quarter]
    back_half = values[..., quarter:]
    return jnp.concatenate(
        [
            front_half * cos_part - back_half * sin_part,
            front_half * sin_part + back_half * cos_part,
        ],
        axis=-1,
    )


def rope_two(values, row_pos, col_pos):
    head_dim = values.shape[-1]
    half_dim = head_dim // 2
    frequency = 10000.0 ** (-(jnp.arange(head_dim // 4, dtype=jnp.float32) * 4.0 / head_dim))
    row_angle = (row_pos[:, None] * frequency[None, :])[:, None, :]
    col_angle = (col_pos[:, None] * frequency[None, :])[:, None, :]
    row_part = rotate_half(values[..., :half_dim], jnp.cos(row_angle), jnp.sin(row_angle))
    col_part = rotate_half(values[..., half_dim:], jnp.cos(col_angle), jnp.sin(col_angle))
    return jnp.concatenate([row_part, col_part], axis=-1)


def head_prep(qkv_pre, qk_gains, qk_biases, row_pos, col_pos):
    head_split = qkv_pre.reshape(qkv_pre.shape[0], 3, HEADS, HEAD)
    queries = rope_two(layer_norm(head_split[:, 0], qk_gains[0], qk_biases[0]), row_pos, col_pos)
    keyset = rope_two(layer_norm(head_split[:, 1], qk_gains[1], qk_biases[1]), row_pos, col_pos)
    return (queries, keyset, head_split[:, 2])


def grid_positions(seg_all, widths, first_tok, tok_count):
    images = jnp.arange(IMGS, dtype=jnp.int32)
    starts = jnp.sum((seg_all[None, :] < images[:, None]).astype(jnp.int32), axis=1)
    seg_part = lax.dynamic_slice_in_dim(seg_all, first_tok, tok_count)
    member = seg_part[:, None] == images[None, :]
    start_tok = jnp.sum(jnp.where(member, starts[None, :], 0), axis=1)
    width_tok = jnp.sum(jnp.where(member, widths[None, :], 0), axis=1)
    in_image = first_tok + jnp.arange(tok_count, dtype=jnp.int32) - start_tok
    return (
        seg_part,
        member,
        (in_image // width_tok).astype(jnp.float32),
        (in_image % width_tok).astype(jnp.float32),
    )


def caption_allowed(seg_part, clip_len, t5_len):
    images = jnp.arange(IMGS, dtype=jnp.int32)
    key_spots = jnp.arange(IMGS * CAP, dtype=jnp.int32)
    key_image = key_spots // CAP
    key_slot = key_spots % CAP
    key_member = key_image[:, None] == images[None, :]
    clip_own = jnp.sum(jnp.where(key_member, clip_len[None, :], 0), axis=1)
    t5_own = jnp.sum(jnp.where(key_member, t5_len[None, :], 0), axis=1)
    key_valid = jnp.where(key_slot < CLIP_TOK, key_slot < clip_own, key_slot - CLIP_TOK < t5_own)
    return (seg_part[:, None] == key_image[None, :]) & key_valid[None, :]


def shards(
    tokens,
    skip,
    segment_ids,
    grid_widths,
    clip_lengths,
    t5_lengths,
    timestep,
    captions,
    ln_gains,
    ln_biases,
    qk_gains,
    qk_biases,
    w_skip,
    w_mod,
    w_qkv,
    w_out,
    w_cq,
    w_ckv,
    w_co,
    w_up,
    w_down,
    cotangent,
):
    full_skip, full_mod, full_qkv, full_out, full_cq, full_ckv, full_co, full_up, full_down = (
        lax.all_gather(w_skip, "dp", axis=0, tiled=True),
        lax.all_gather(w_mod, "dp", axis=0, tiled=True),
        lax.all_gather(w_qkv, "dp", axis=0, tiled=True),
        lax.all_gather(w_out, "dp", axis=0, tiled=True),
        lax.all_gather(w_cq, "dp", axis=0, tiled=True),
        lax.all_gather(w_ckv, "dp", axis=0, tiled=True),
        lax.all_gather(w_co, "dp", axis=0, tiled=True),
        lax.all_gather(w_up, "dp", axis=0, tiled=True),
        lax.all_gather(w_down, "dp", axis=0, tiled=True),
    )
    local_tok = tokens.shape[0]
    model_width = tokens.shape[1]
    seq_count = lax.axis_size("seq")
    bucket_len = local_tok * seq_count
    local_heads = HEADS // seq_count
    score_scale = HEAD ** (-0.5)
    block_rows = min(512, bucket_len)
    block_count = bucket_len // block_rows
    seq_rank = lax.axis_index("seq")
    seg_all = segment_ids[0]
    seg_blocks = seg_all.reshape(block_count, block_rows)
    seg_local, member, row_pos, col_pos = grid_positions(
        seg_all, grid_widths[0], seq_rank * local_tok, local_tok
    )
    joined = jnp.concatenate([tokens, skip], axis=1).astype(jnp.float32)
    h_float, pull_skip = jax.vjp(
        layer_norm, joined, ln_gains[0:2].reshape(-1), ln_biases[0:2].reshape(-1)
    )
    h_zero = h_float.astype(jnp.bfloat16)
    x_one = matmul(h_zero, full_skip)
    time_cond = silu_gate(
        jnp.dot(
            member.astype(jnp.float32),
            timestep[0].astype(jnp.float32),
            precision=lax.Precision.HIGHEST,
        )
    ).astype(jnp.bfloat16)
    time_shift = matmul(time_cond, full_mod)
    n_float, pull_one = jax.vjp(layer_norm, x_one, ln_gains[2], ln_biases[2])
    n_one = (n_float + time_shift).astype(jnp.bfloat16)
    qkv_pre = matmul(n_one, full_qkv)

    def prep_local(pre_rows, gains, biases):
        return head_prep(pre_rows, gains, biases, row_pos, col_pos)

    (queries, keyset, values), pull_heads = jax.vjp(prep_local, qkv_pre, qk_gains, qk_biases)
    packed = (
        jnp.stack([queries, keyset, values]).astype(jnp.bfloat16).reshape(3, local_tok, model_width)
    )
    spread_heads = lax.all_to_all(packed, "seq", split_axis=2, concat_axis=1, tiled=True)
    by_head = spread_heads.reshape(3, bucket_len, local_heads, HEAD).transpose(0, 2, 1, 3)

    def block_scores(query_b, seg_b, key_h):
        return jnp.where(
            seg_b[:, None] == seg_all[None, :], matmul(query_b, key_h.T) * score_scale, masked_score
        )

    def self_forward(head_items):
        query_h, key_h, value_h = head_items

        def forward_block(block_items):
            query_b, seg_b = block_items
            scores = block_scores(query_b, seg_b, key_h)
            row_max = jnp.max(scores, axis=1, keepdims=True)
            exp_scores = jnp.exp(scores - row_max)
            row_sum = jnp.sum(exp_scores, axis=1, keepdims=True)
            attn_probs = (exp_scores / row_sum).astype(jnp.bfloat16)
            return (matmul(attn_probs, value_h).astype(jnp.bfloat16), row_max, row_sum)

        outs, maxes, sums = lax.map(
            forward_block, (query_h.reshape(block_count, block_rows, HEAD), seg_blocks)
        )
        return (outs.reshape(bucket_len, HEAD), maxes, sums)

    head_out, row_maxes, row_sums = lax.map(self_forward, (by_head[0], by_head[1], by_head[2]))
    attn_o = lax.all_to_all(
        head_out.transpose(1, 0, 2).reshape(bucket_len, local_heads * HEAD),
        "seq",
        split_axis=0,
        concat_axis=1,
        tiled=True,
    )
    x_two = x_one + matmul(attn_o, full_out)
    n3_float, pull_three = jax.vjp(layer_norm, x_two, ln_gains[3], ln_biases[3])
    n_three = n3_float.astype(jnp.bfloat16)
    cross_q = matmul(n_three, full_cq).astype(jnp.bfloat16).reshape(local_tok, HEADS, HEAD)
    text_kv = matmul(captions[0], full_ckv)
    cross_k = text_kv[:, :model_width].astype(jnp.bfloat16).reshape(-1, HEADS, HEAD)
    cross_v = text_kv[:, model_width:].astype(jnp.bfloat16).reshape(-1, HEADS, HEAD)
    cross_mask = caption_allowed(seg_local, clip_lengths[0], t5_lengths[0])
    cross_scores = jnp.where(
        cross_mask[None],
        jnp.einsum("thd,khd->htk", cross_q, cross_k, preferred_element_type=jnp.float32)
        * score_scale,
        masked_score,
    )
    cross_probs = soft_rows(cross_scores)
    cross_low = cross_probs.astype(jnp.bfloat16)
    cross_o = (
        jnp.einsum("htk,khd->thd", cross_low, cross_v, preferred_element_type=jnp.float32)
        .astype(jnp.bfloat16)
        .reshape(local_tok, model_width)
    )
    x_three = x_two + matmul(cross_o, full_co)
    n2_float, pull_two = jax.vjp(layer_norm, x_three, ln_gains[4], ln_biases[4])
    n_two = n2_float.astype(jnp.bfloat16)
    up_proj = matmul(n_two, full_up)
    act_float, pull_gelu = jax.vjp(gelu_tanh, up_proj)
    act_low = act_float.astype(jnp.bfloat16)
    block_out = (x_three + matmul(act_low, full_down)).astype(jnp.bfloat16)
    grad_down = matmul(act_low.T, cotangent)
    d_act = matmul(cotangent, full_down.T)
    d_up = pull_gelu(d_act)[0].astype(jnp.bfloat16)
    grad_up = matmul(n_two.T, d_up)
    d_n_two = matmul(d_up, full_up.T)
    back_three_x, gain_four, bias_four = pull_two(d_n_two)
    d_x_three = cotangent.astype(jnp.float32) + back_three_x
    d_co = d_x_three.astype(jnp.bfloat16)
    grad_co = matmul(cross_o.T, d_co)
    d_cross_o = matmul(d_co, full_co.T).astype(jnp.bfloat16).reshape(local_tok, HEADS, HEAD)
    d_cprobs = jnp.einsum("thd,khd->htk", d_cross_o, cross_v, preferred_element_type=jnp.float32)
    d_cscores = (
        cross_probs * (d_cprobs - jnp.sum(d_cprobs * cross_probs, axis=-1, keepdims=True))
    ).astype(jnp.bfloat16)
    d_cross_q = (
        (
            jnp.einsum("htk,khd->thd", d_cscores, cross_k, preferred_element_type=jnp.float32)
            * score_scale
        )
        .astype(jnp.bfloat16)
        .reshape(local_tok, model_width)
    )
    d_cross_k = (
        jnp.einsum("htk,thd->khd", d_cscores, cross_q, preferred_element_type=jnp.float32)
        * score_scale
    )
    d_cross_v = jnp.einsum("htk,thd->khd", cross_low, d_cross_o, preferred_element_type=jnp.float32)
    d_text_kv = jnp.concatenate(
        [d_cross_k.reshape(-1, model_width), d_cross_v.reshape(-1, model_width)], axis=1
    )
    grad_ckv = jnp.dot(
        captions[0].astype(jnp.float32).T,
        d_text_kv,
        precision=lax.Precision.HIGHEST,
        preferred_element_type=jnp.float32,
    )
    grad_cq = matmul(n_three.T, d_cross_q)
    d_n_three = matmul(d_cross_q, full_cq.T)
    back_two_x, gain_three, bias_three = pull_three(d_n_three)
    d_x_two = d_x_three + back_two_x
    d_attn = d_x_two.astype(jnp.bfloat16)
    grad_out = matmul(attn_o.T, d_attn)
    d_attn_o = matmul(d_attn, full_out.T).astype(jnp.bfloat16)
    d_spread = lax.all_to_all(d_attn_o, "seq", split_axis=1, concat_axis=0, tiled=True)
    d_by_head = d_spread.reshape(bucket_len, local_heads, HEAD).transpose(1, 0, 2)

    def self_backward(head_items):
        query_h, key_h, value_h, d_out_h, row_max, row_sum = head_items

        def backward_block(carry, block_items):
            key_total, value_total = carry
            query_b, seg_b, d_out_b, max_b, sum_b = block_items
            scores = block_scores(query_b, seg_b, key_h)
            attn_probs = jnp.exp(scores - max_b) / sum_b
            probs_low = attn_probs.astype(jnp.bfloat16)
            d_probs = matmul(d_out_b, value_h.T)
            d_scores = (
                attn_probs * (d_probs - jnp.sum(d_probs * attn_probs, axis=1, keepdims=True))
            ).astype(jnp.bfloat16)
            d_query = (matmul(d_scores, key_h) * score_scale).astype(jnp.bfloat16)
            key_total = key_total + matmul(d_scores.T, query_b) * score_scale
            value_total = value_total + matmul(probs_low.T, d_out_b)
            return ((key_total, value_total), d_query)

        start = (
            jnp.zeros((bucket_len, HEAD), jnp.float32),
            jnp.zeros((bucket_len, HEAD), jnp.float32),
        )
        (key_total, value_total), d_query_blocks = lax.scan(
            backward_block,
            start,
            (
                query_h.reshape(block_count, block_rows, HEAD),
                seg_blocks,
                d_out_h.reshape(block_count, block_rows, HEAD),
                row_max,
                row_sum,
            ),
        )
        return jnp.stack(
            [
                d_query_blocks.reshape(bucket_len, HEAD),
                key_total.astype(jnp.bfloat16),
                value_total.astype(jnp.bfloat16),
            ]
        )

    d_heads = lax.map(
        self_backward, (by_head[0], by_head[1], by_head[2], d_by_head, row_maxes, row_sums)
    )
    d_packed = d_heads.transpose(1, 2, 0, 3).reshape(3, bucket_len, local_heads * HEAD)
    d_gathered = lax.all_to_all(d_packed, "seq", split_axis=1, concat_axis=2, tiled=True)
    d_parts = d_gathered.astype(jnp.float32).reshape(3, local_tok, HEADS, HEAD)
    d_qkv_float, grad_qk_gain, grad_qk_bias = pull_heads((d_parts[0], d_parts[1], d_parts[2]))
    d_qkv = d_qkv_float.astype(jnp.bfloat16)
    grad_qkv = matmul(n_one.T, d_qkv)
    d_n_one = matmul(d_qkv, full_qkv.T)
    d_shift = d_n_one.astype(jnp.bfloat16)
    grad_mod = matmul(time_cond.T, d_shift)
    back_one_x, gain_one, bias_one = pull_one(d_n_one)
    d_x_one = d_x_two + back_one_x
    d_y = d_x_one.astype(jnp.bfloat16)
    grad_skip_w = matmul(h_zero.T, d_y)
    d_h_zero = matmul(d_y, full_skip.T)
    d_joined, gain_skip, bias_skip = pull_skip(d_h_zero)
    grad_tokens = d_joined[:, :model_width].astype(jnp.bfloat16)
    grad_skip = d_joined[:, model_width:].astype(jnp.bfloat16)
    gain_rows = jnp.stack(
        [gain_skip[:model_width], gain_skip[model_width:], gain_one, gain_three, gain_four]
    )
    bias_rows = jnp.stack([bias_skip[:model_width], bias_skip[model_width:], bias_one, bias_three])
    gain_total, bias_total, ff_bias_total, qk_gain_total, qk_bias_total = lax.psum(
        (gain_rows, bias_rows, bias_four, grad_qk_gain, grad_qk_bias), ("dp", "seq")
    )
    local_grads = (
        grad_skip_w,
        grad_mod,
        grad_qkv,
        grad_out,
        grad_cq,
        grad_ckv,
        grad_co,
        grad_up,
        grad_down,
    )
    row_sums_w = (
        lax.psum_scatter(
            local_grads[0].astype(jnp.bfloat16), "dp", scatter_dimension=0, tiled=True
        ).astype(jnp.float32),
        lax.psum_scatter(
            local_grads[1].astype(jnp.bfloat16), "dp", scatter_dimension=0, tiled=True
        ).astype(jnp.float32),
        lax.psum_scatter(
            local_grads[2].astype(jnp.bfloat16), "dp", scatter_dimension=0, tiled=True
        ).astype(jnp.float32),
        lax.psum_scatter(
            local_grads[3].astype(jnp.bfloat16), "dp", scatter_dimension=0, tiled=True
        ).astype(jnp.float32),
        lax.psum_scatter(
            local_grads[4].astype(jnp.bfloat16), "dp", scatter_dimension=0, tiled=True
        ).astype(jnp.float32),
        lax.psum_scatter(
            local_grads[5].astype(jnp.bfloat16), "dp", scatter_dimension=0, tiled=True
        ).astype(jnp.float32),
        lax.psum_scatter(
            local_grads[6].astype(jnp.bfloat16), "dp", scatter_dimension=0, tiled=True
        ).astype(jnp.float32),
        lax.psum_scatter(
            local_grads[7].astype(jnp.bfloat16), "dp", scatter_dimension=0, tiled=True
        ).astype(jnp.float32),
        lax.psum_scatter(
            local_grads[8].astype(jnp.bfloat16), "dp", scatter_dimension=0, tiled=True
        ).astype(jnp.float32),
    )
    split_sums = (
        lax.psum_scatter(
            row_sums_w[0].astype(jnp.bfloat16), "seq", scatter_dimension=1, tiled=True
        ).astype(jnp.float32),
        lax.psum_scatter(
            row_sums_w[1].astype(jnp.bfloat16), "seq", scatter_dimension=1, tiled=True
        ).astype(jnp.float32),
        lax.psum_scatter(
            row_sums_w[2].astype(jnp.bfloat16), "seq", scatter_dimension=1, tiled=True
        ).astype(jnp.float32),
        lax.psum_scatter(
            row_sums_w[3].astype(jnp.bfloat16), "seq", scatter_dimension=1, tiled=True
        ).astype(jnp.float32),
        lax.psum_scatter(
            row_sums_w[4].astype(jnp.bfloat16), "seq", scatter_dimension=1, tiled=True
        ).astype(jnp.float32),
        lax.psum_scatter(
            row_sums_w[5].astype(jnp.bfloat16), "seq", scatter_dimension=1, tiled=True
        ).astype(jnp.float32),
        lax.psum_scatter(
            row_sums_w[6].astype(jnp.bfloat16), "seq", scatter_dimension=1, tiled=True
        ).astype(jnp.float32),
        lax.psum_scatter(
            row_sums_w[7].astype(jnp.bfloat16), "seq", scatter_dimension=1, tiled=True
        ).astype(jnp.float32),
        lax.psum_scatter(
            row_sums_w[8].astype(jnp.bfloat16), "seq", scatter_dimension=1, tiled=True
        ).astype(jnp.float32),
    )
    reduced = (
        lax.all_gather(split_sums[0].astype(jnp.bfloat16), "seq", axis=1, tiled=True).astype(
            jnp.float32
        ),
        lax.all_gather(split_sums[1].astype(jnp.bfloat16), "seq", axis=1, tiled=True).astype(
            jnp.float32
        ),
        lax.all_gather(split_sums[2].astype(jnp.bfloat16), "seq", axis=1, tiled=True).astype(
            jnp.float32
        ),
        lax.all_gather(split_sums[3].astype(jnp.bfloat16), "seq", axis=1, tiled=True).astype(
            jnp.float32
        ),
        lax.all_gather(split_sums[4].astype(jnp.bfloat16), "seq", axis=1, tiled=True).astype(
            jnp.float32
        ),
        lax.all_gather(split_sums[5].astype(jnp.bfloat16), "seq", axis=1, tiled=True).astype(
            jnp.float32
        ),
        lax.all_gather(split_sums[6].astype(jnp.bfloat16), "seq", axis=1, tiled=True).astype(
            jnp.float32
        ),
        lax.all_gather(split_sums[7].astype(jnp.bfloat16), "seq", axis=1, tiled=True).astype(
            jnp.float32
        ),
        lax.all_gather(split_sums[8].astype(jnp.bfloat16), "seq", axis=1, tiled=True).astype(
            jnp.float32
        ),
    )
    return (
        block_out,
        grad_tokens,
        grad_skip,
        gain_total,
        bias_total,
        ff_bias_total,
        qk_gain_total,
        qk_bias_total,
        reduced[0],
        reduced[1],
        reduced[2],
        reduced[3],
        reduced[4],
        reduced[5],
        reduced[6],
        reduced[7],
        reduced[8],
    )


def solution(mesh):
    in_specs = (
        P(("dp", "seq"), None),
        P(("dp", "seq"), None),
        P("dp", None),
        P("dp", None),
        P("dp", None),
        P("dp", None),
        P("dp", None, None),
        P("dp", None, None),
        P(),
        P(),
        P(),
        P(),
        P("dp", None),
        P("dp", None),
        P("dp", None),
        P("dp", None),
        P("dp", None),
        P("dp", None),
        P("dp", None),
        P("dp", None),
        P("dp", None),
        P(("dp", "seq"), None),
    )
    out_specs = (
        P(("dp", "seq"), None),
        P(("dp", "seq"), None),
        P(("dp", "seq"), None),
        P(),
        P(),
        P(),
        P(),
        P(),
        P("dp", None),
        P("dp", None),
        P("dp", None),
        P("dp", None),
        P("dp", None),
        P("dp", None),
        P("dp", None),
        P("dp", None),
        P("dp", None),
    )
    return jax.shard_map(shards, mesh=mesh, in_specs=in_specs, out_specs=out_specs, check_vma=False)
```

profile of v0, /device:TPU:1, one launch (start us, length us, event | category | flops | bytes accessed | tf_op | source)
XLA Modules:
  0.0 3504.9 jit_solution(7824018569201404117)
XLA Ops:
  19.3 111.8 %all-gather.18.cloned.1.call-done = bf16[2816,1408]{1,0:T(8,128)(2,1)} async-done(((bf16[352,1408]{1,0:T(8,128)(2,1)}), bf16[2816,1408]{1,0:T(8,128)(2,1)}) %all-gather.18.cloned.1.call-update) | async-done | bytes 7929872 | tf_op jit(solution)/shard_map/all_gather | solution.py:129
  140.3 61.0 %all-gather.20.cloned.1.call-done = bf16[1408,1408]{1,0:T(8,128)(2,1)} async-done(((bf16[176,1408]{1,0:T(8,128)(2,1)}), bf16[1408,1408]{1,0:T(8,128)(2,1)}) %all-gather.20.cloned.1.call-update) | async-done | bytes 3964944 | tf_op jit(solution)/shard_map/all_gather | solution.py:130
  207.2 163.5 %all-gather.22.cloned.1.call-done = bf16[1408,4224]{1,0:T(8,128)(2,1)} async-done(((bf16[176,4224]{1,0:T(8,128)(2,1)}), bf16[1408,4224]{1,0:T(8,128)(2,1)}) %all-gather.22.cloned.1.call-update) | async-done | bytes 11894800 | tf_op jit(solution)/shard_map/all_gather | solution.py:131
  410.5 46.8 %all-to-all-done = bf16[3,384,1408]{1,0,2:T(4,128)(2,1)} async-done(((bf16[3,384,1408]{1,0,2:T(4,128)(2,1)}), bf16[3,384,1408]{1,0,2:T(4,128)(2,1)}, u32[]{:S(2)}, u32[]{:S(2)}) %all-to-all-start) | async-done | bytes 3244064 | tf_op jit(solution)/shard_map/all_to_all | solution.py:178
  479.1 44.8 %while.54 = (s32[]{:T(128)}, bf16[4,1536,88]{2,1,0:T(8,128)(2,1)}, f32[4,3,512,1]{2,3,1,0:T(1,128)}, f32[4,3,512,1]{2,3,1,0:T(1,128)}, bf16[4,1536,88]{2,1,0:T(8...) while((s32[]{:T(128)}, bf16[4,1536,88]{2,1,0:T(8,128)(2,1)}, ...), condition=%wide.region_16.17_spmd, body=%wide.region_11.16_spmd.sunk | while | flops 283945984 | bytes 13341066 | solution.py:203
  561.3 43.2 %all-gather.28.cloned.1.call-done = bf16[1408,1408]{1,0:T(8,128)(2,1)} async-done(((bf16[176,1408]{1,0:T(8,128)(2,1)}), bf16[1408,1408]{1,0:T(8,128)(2,1)}) %all-gather.28.cloned.1.call-update) | async-done | bytes 3964944 | tf_op jit(solution)/shard_map/all_gather | solution.py:133
  640.7 34.9 all-gather.30.cloned.1.call-done
  682.3 327.3 %all-gather.34.cloned.1.call-done = bf16[6144,1408]{1,0:T(8,128)(2,1)} async-done(((bf16[768,1408]{1,0:T(8,128)(2,1)}), bf16[6144,1408]{1,0:T(8,128)(2,1)}) %all-gather.34.cloned.1.call-update) | async-done | bytes 17301520 | tf_op jit(solution)/shard_map/all_gather | solution.py:137
  1022.9 321.2 %all-gather.32.cloned.1.call-done = bf16[1408,6144]{1,0:T(8,128)(2,1)} async-done(((bf16[176,6144]{1,0:T(8,128)(2,1)}), bf16[1408,6144]{1,0:T(8,128)(2,1)}) %all-gather.32.cloned.1.call-update) | async-done | bytes 17301520 | tf_op jit(solution)/shard_map/all_gather | solution.py:136
  1344.1 26.4 fusion.44
  1394.4 18.1 multiply_reduce_fusion.1
  1469.2 189.8 %while.56 = (s32[]{:T(128)}, bf16[4,3,1536,88]{2,3,0,1:T(8,128)(2,1)}, bf16[4,1536,88]{2,1,0:T(8,128)(2,1)}, bf16[4,1536,88]{1,2,0:T(8,128)(2,1)}, f32[4,3,512,1...) while((s32[]{:T(128)}, ...), condition=%wide.region_34.35_spmd, body=%wide.region_30.34_spmd.sunk | while | flops 704179712 | bytes 54403672 | solution.py:326
  1477.1 37.0 %while.58 = (s32[]{:T(128)}, f32[1536,88]{0,1:T(8,128)S(1)}, f32[1536,88]{0,1:T(8,128)S(1)}, bf16[3,512,88]{1,2,0:T(8,128)(2,1)}, s32[3,512]{1,0:T(4,128)}, /*in...) while((s32[]{:T(128)}, f32[1536,88]{0,1:T(8,128)S(1)}, ...), condition=%wide.region_33.33_spmd.clone, body=%wide.region_31.32_spmd.clone.sunk | while | flops 701476352 | bytes 47350080 | solution.py:307
  1524.6 37.0 %while.58 = (s32[]{:T(128)}, f32[1536,88]{0,1:T(8,128)S(1)}, f32[1536,88]{0,1:T(8,128)S(1)}, bf16[3,512,88]{1,2,0:T(8,128)(2,1)}, s32[3,512]{1,0:T(4,128)}, /*in...) while((s32[]{:T(128)}, f32[1536,88]{0,1:T(8,128)S(1)}, ...), condition=%wide.region_33.33_spmd.clone, body=%wide.region_31.32_spmd.clone.sunk | while | flops 701476352 | bytes 47350080 | solution.py:307
  1572.0 37.0 %while.58 = (s32[]{:T(128)}, f32[1536,88]{0,1:T(8,128)S(1)}, f32[1536,88]{0,1:T(8,128)S(1)}, bf16[3,512,88]{1,2,0:T(8,128)(2,1)}, s32[3,512]{1,0:T(4,128)}, /*in...) while((s32[]{:T(128)}, f32[1536,88]{0,1:T(8,128)S(1)}, ...), condition=%wide.region_33.33_spmd.clone, body=%wide.region_31.32_spmd.clone.sunk | while | flops 701476352 | bytes 47350080 | solution.py:307
  1619.4 37.0 %while.58 = (s32[]{:T(128)}, f32[1536,88]{0,1:T(8,128)S(1)}, f32[1536,88]{0,1:T(8,128)S(1)}, bf16[3,512,88]{1,2,0:T(8,128)(2,1)}, s32[3,512]{1,0:T(4,128)}, /*in...) while((s32[]{:T(128)}, f32[1536,88]{0,1:T(8,128)S(1)}, ...), condition=%wide.region_33.33_spmd.clone, body=%wide.region_31.32_spmd.clone.sunk | while | flops 701476352 | bytes 47350080 | solution.py:307
  1667.0 59.6 %all_to_all.59 = bf16[3,1536,352]{2,0,1:T(4,128)(2,1)} all-to-all(bf16[3,1536,352]{2,0,1:T(4,128)(2,1)} %copy.176), channel_id=1, replica_groups=mesh['dp'=8,'seq'=4] {'seq'}, dimensions={1} | all-to-all | bytes 6488064 | tf_op jit(solution)/shard_map/all_to_all | solution.py:330
  1871.8 22.5 convert_bitcast_fusion.2
  1915.7 50.4 %reduce-scatter.39.cloned.1.call-done = bf16[176,4224]{1,0:T(8,128)(2,1)} async-done(((bf16[1408,4224]{1,0:T(8,128)(2,1)}), bf16[176,4224]{1,0:T(8,128)(2,1)}) %reduce-scatter.39.cloned.1.call-update) | async-done | bytes 1486864 | tf_op jit(solution)/shard_map/reduce_scatter | solution.py:371
  1970.0 291.7 %reduce-scatter.49.cloned.1.call-done = bf16[176,6144]{1,0:T(8,128)(2,1)} async-done(((bf16[1408,6144]{1,0:T(8,128)(2,1)}), bf16[176,6144]{1,0:T(8,128)(2,1)}) %reduce-scatter.49.cloned.1.call-update) | async-done | bytes 2162704 | tf_op jit(solution)/shard_map/reduce_scatter | solution.py:386
  2261.7 295.9 %reduce-scatter.53.cloned.1.call-done = bf16[768,1408]{1,0:T(8,128)(2,1)} async-done(((bf16[6144,1408]{1,0:T(8,128)(2,1)}), bf16[768,1408]{1,0:T(8,128)(2,1)}) %reduce-scatter.53.cloned.1.call-update) | async-done | bytes 2162704 | tf_op jit(solution)/shard_map/reduce_scatter | solution.py:389
  2561.9 81.3 %reduce-scatter.41.cloned.1.call-done = bf16[176,1408]{1,0:T(8,128)(2,1)} async-done(((bf16[1408,1408]{1,0:T(8,128)(2,1)}), bf16[176,1408]{1,0:T(8,128)(2,1)}) %reduce-scatter.41.cloned.1.call-update) | async-done | bytes 495632 | tf_op jit(solution)/shard_map/reduce_scatter | solution.py:374
  2645.5 83.4 %reduce-scatter.43.cloned.1.call-done = bf16[176,1408]{1,0:T(8,128)(2,1)} async-done(((bf16[1408,1408]{1,0:T(8,128)(2,1)}), bf16[176,1408]{1,0:T(8,128)(2,1)}) %reduce-scatter.43.cloned.1.call-update) | async-done | bytes 495632 | tf_op jit(solution)/shard_map/reduce_scatter | solution.py:377
  2731.2 83.6 %reduce-scatter.47.cloned.1.call-done = bf16[176,1408]{1,0:T(8,128)(2,1)} async-done(((bf16[1408,1408]{1,0:T(8,128)(2,1)}), bf16[176,1408]{1,0:T(8,128)(2,1)}) %reduce-scatter.47.cloned.1.call-update) | async-done | bytes 495632 | tf_op jit(solution)/shard_map/reduce_scatter | solution.py:383
  2817.0 83.6 %reduce-scatter.37.cloned.1.call-done = bf16[176,1408]{1,0:T(8,128)(2,1)} async-done(((bf16[1408,1408]{1,0:T(8,128)(2,1)}), bf16[176,1408]{1,0:T(8,128)(2,1)}) %reduce-scatter.37.cloned.1.call-update) | async-done | bytes 495632 | tf_op jit(solution)/shard_map/reduce_scatter | solution.py:368
  2902.8 111.1 %reduce-scatter.65.cloned.1.call-done = bf16[128,2816]{1,0:T(8,128)(2,1)} async-done(((bf16[1024,2816]{1,0:T(8,128)(2,1)}), bf16[128,2816]{1,0:T(8,128)(2,1)}) %reduce-scatter.65.cloned.1.call-update) | async-done | bytes 720912
  3016.2 142.5 %reduce-scatter.35.cloned.1.call-done = bf16[352,1408]{1,0:T(8,128)(2,1)} async-done(((bf16[2816,1408]{1,0:T(8,128)(2,1)}), bf16[352,1408]{1,0:T(8,128)(2,1)}) %reduce-scatter.35.cloned.1.call-update) | async-done | bytes 991248 | tf_op jit(solution)/shard_map/reduce_scatter | solution.py:365
  3161.1 31.7 reduce-scatter.59.cloned.1.call-done
  3194.9 32.4 reduce-scatter.51.cloned.1.call-done
  3261.9 40.3 %all-reduce.19 = (f32[5,1408]{1,0:T(8,128)}, f32[4,1408]{1,0:T(4,128)}, f32[1408]{0:T(1024)}, f32[2,88]{1,0:T(2,128)}, f32[2,88]{1,0:T(2,128)}) all-reduce(f32[5,1408]{1,0:T(8,128)S(1)} %stack.44, f32[4,1408]{1,0:T(4,128)S(1)} %pad_maximum_fusion.4, f32[1408]{0:T(1024)S(1)} %copy-done.107, ...), channel_id=1, replica_groups=mesh['dp'=8,'seq'=4] {'dp','seq'}, use_global_device_ids=true, to_apply=%region_47.48 | all-reduce | flops 14432 | bytes 115456 | tf_op jit(solution)/shard_map/psum | solution.py:350
  3403.6 18.2 reduce-scatter.55.cloned.1.call-done
  3473.1 20.3 all-gather.38.cloned.1.call-done
  (909 shorter events, 911.3 us)
Async XLA Ops:
  7.2 123.9 %all-gather.18.cloned.1.call-start = ((), (), s32[]{:S(2)}) async-start(), calls=%async_computation.22 | async-start | bytes 8921088 | tf_op jit(solution)/shard_map/all_gather | solution.py:129
  7.9 193.4 %all-gather.20.cloned.1.call-start = ((), (), s32[]{:S(2)}) async-start(), calls=%async_computation.23 | async-start | bytes 4460544 | tf_op jit(solution)/shard_map/all_gather | solution.py:130
  8.7 362.0 %all-gather.22.cloned.1.call-start = ((), (), s32[]{:S(2)}) async-start(), calls=%async_computation.24 | async-start | bytes 13381632 | tf_op jit(solution)/shard_map/all_gather | solution.py:131
  9.5 523.8 %all-gather.26.cloned.1.call-start = ((), (), s32[]{:S(2)}) async-start(), calls=%async_computation.26 | async-start | bytes 6488064 | tf_op jit(solution)/shard_map/all_gather | solution.py:134
  10.0 544.1 %all-gather.24.cloned.1.call-start = ((), (), s32[]{:S(2)}) async-start(), calls=%async_computation.25 | async-start | bytes 4460544 | tf_op jit(solution)/shard_map/all_gather | solution.py:132
  10.6 593.9 %all-gather.28.cloned.1.call-start = ((), (), s32[]{:S(2)}) async-start(), calls=%async_computation.27 | async-start | bytes 4460544 | tf_op jit(solution)/shard_map/all_gather | solution.py:133
  11.2 664.4 %all-gather.30.cloned.1.call-start = ((), (), s32[]{:S(2)}) async-start(), calls=%async_computation.28 | async-start | bytes 4460544 | tf_op jit(solution)/shard_map/all_gather | solution.py:135
  12.0 997.6 %all-gather.34.cloned.1.call-start = ((), (), s32[]{:S(2)}) async-start(), calls=%async_computation.30 | async-start | bytes 19464192 | tf_op jit(solution)/shard_map/all_gather | solution.py:137
  402.5 54.7 %all-to-all-start = ((bf16[3,384,1408]{1,0,2:T(4,128)(2,1)}), bf16[3,384,1408]{1,0,2:T(4,128)(2,1)}, u32[]{:S(2)}, u32[]{:S(2)}) async-start(bf16[3,384,1408]{1,0,2:T(4,128)(2,1)} %copy.157), calls=%async_computation | async-start | bytes 8650752 | tf_op jit(solution)/shard_map/all_to_all | solution.py:178
  408.5 935.6 %all-gather.32.cloned.1.call-start = ((), (), s32[]{:S(2)}) async-start(), calls=%async_computation.29 | async-start | bytes 19464192 | tf_op jit(solution)/shard_map/all_gather | solution.py:136
  528.9 25.3 all-to-all-start.1
  1451.3 514.8 %reduce-scatter.39.cloned.1.call-start = ((), (), s32[]{:S(2)}) async-start(), calls=%async_computation.33 | async-start | bytes 13381632 | tf_op jit(solution)/shard_map/reduce_scatter | solution.py:371
  1768.4 493.2 %reduce-scatter.49.cloned.1.call-start = ((), (), s32[]{:S(2)}) async-start(), calls=%async_computation.38 | async-start | bytes 19464192 | tf_op jit(solution)/shard_map/reduce_scatter | solution.py:386
  1784.7 772.9 %reduce-scatter.53.cloned.1.call-start = ((), (), s32[]{:S(2)}) async-start(), calls=%async_computation.41 | async-start | bytes 19464192 | tf_op jit(solution)/shard_map/reduce_scatter | solution.py:389
  1802.3 840.9 %reduce-scatter.41.cloned.1.call-start = ((), (), s32[]{:S(2)}) async-start(), calls=%async_computation.34 | async-start | bytes 4460544 | tf_op jit(solution)/shard_map/reduce_scatter | solution.py:374
  1809.5 919.5 %reduce-scatter.43.cloned.1.call-start = ((), (), s32[]{:S(2)}) async-start(), calls=%async_computation.35 | async-start | bytes 4460544 | tf_op jit(solution)/shard_map/reduce_scatter | solution.py:377
  1816.8 997.9 %reduce-scatter.47.cloned.1.call-start = ((), (), s32[]{:S(2)}) async-start(), calls=%async_computation.37 | async-start | bytes 4460544 | tf_op jit(solution)/shard_map/reduce_scatter | solution.py:383
  1823.8 1076.8 %reduce-scatter.37.cloned.1.call-start = ((), (), s32[]{:S(2)}) async-start(), calls=%async_computation.32 | async-start | bytes 4460544 | tf_op jit(solution)/shard_map/reduce_scatter | solution.py:368
  1842.5 1171.4 %reduce-scatter.65.cloned.1.call-start = ((), (), s32[]{:S(2)}) async-start(), calls=%async_computation.49 | async-start | bytes 6488064
  1902.7 1256.0 %reduce-scatter.35.cloned.1.call-start = ((), (), s32[]{:S(2)}) async-start(), calls=%async_computation.31 | async-start | bytes 8921088 | tf_op jit(solution)/shard_map/reduce_scatter | solution.py:365
  1915.6 1277.2 %reduce-scatter.59.cloned.1.call-start = ((), (), s32[]{:S(2)}) async-start(), calls=%async_computation.46 | async-start | bytes 2703360
  1969.9 1257.4 %reduce-scatter.51.cloned.1.call-start = ((), (), s32[]{:S(2)}) async-start(), calls=%async_computation.39 | async-start | bytes 2703360 | tf_op jit(solution)/shard_map/reduce_scatter | solution.py:415
  2261.7 1000.1 %reduce-scatter.69.cloned.1.call-start = ((), (), s32[]{:S(2)}) async-start(), calls=%async_computation.51 | async-start | bytes 2703360
  2561.9 744.4 %reduce-scatter.61.cloned.1.call-start = ((), (), s32[]{:S(2)}) async-start(), calls=%async_computation.47 | async-start | bytes 901120
  2645.5 673.5 %reduce-scatter.63.cloned.1.call-start = ((), (), s32[]{:S(2)}) async-start(), calls=%async_computation.48 | async-start | bytes 901120
  2731.1 610.6 %reduce-scatter.67.cloned.1.call-start = ((), (), s32[]{:S(2)}) async-start(), calls=%async_computation.50 | async-start | bytes 901120
  2816.9 550.7 %reduce-scatter.57.cloned.1.call-start = ((), (), s32[]{:S(2)}) async-start(), calls=%async_computation.45 | async-start | bytes 901120
  2902.8 490.8 %reduce-scatter.45.cloned.1.call-start = ((), (), s32[]{:S(2)}) async-start(), calls=%async_computation.36 | async-start | bytes 901120 | tf_op jit(solution)/shard_map/reduce_scatter | solution.py:409
  3016.2 405.6 %reduce-scatter.55.cloned.1.call-start = ((), (), s32[]{:S(2)}) async-start(), calls=%async_computation.44 | async-start | bytes 1351680
  3161.1 283.3 %all-gather.40.cloned.1.call-start = ((), (), s32[]{:S(2)}) async-start(), calls=%async_computation.43 | async-start | bytes 2027520 | tf_op jit(solution)/shard_map/all_gather | solution.py:429
  3194.9 274.1 %all-gather.36.cloned.1.call-start = ((), (), s32[]{:S(2)}) async-start(), calls=%async_computation.40 | async-start | bytes 2703360 | tf_op jit(solution)/shard_map/all_gather | solution.py:444
  3227.4 266.1 %all-gather.38.cloned.1.call-start = ((), (), s32[]{:S(2)}) async-start(), calls=%async_computation.42 | async-start | bytes 2703360 | tf_op jit(solution)/shard_map/all_gather | solution.py:447
  (189 other events, 8316.2 us)
Sparse Core Ops, SparseCore 0:
  10.2 120.8 all-gather.17
  133.3 67.9 all-gather.19
  203.5 167.0 all-gather.21
  372.7 90.5 all-gather.25
  465.3 68.2 all-gather.23
  535.6 68.8 all-gather.27
  606.7 68.8 all-gather.29
  677.1 332.4 all-gather.33
  1011.1 332.9 all-gather.31
  1768.5 197.4 reduce-scatter.38
  1970.0 291.6 reduce-scatter.48
  2265.9 291.6 reduce-scatter.52
  2561.7 81.4 reduce-scatter.40
  2646.7 82.2 reduce-scatter.42
  2732.3 82.3 reduce-scatter.46
  2818.7 81.8 reduce-scatter.36
  2904.1 109.7 reduce-scatter.64
  3017.4 141.2 reduce-scatter.34
  3161.8 30.9 reduce-scatter.58
  3195.4 31.8 reduce-scatter.50
  3229.9 31.8 reduce-scatter.68
  3265.1 22.8 reduce-scatter.60
  3291.1 23.2 reduce-scatter.62
  3317.5 24.0 reduce-scatter.66
  3344.8 22.8 reduce-scatter.56
  3370.8 22.8 reduce-scatter.44
  3396.6 25.1 reduce-scatter.54
  3424.0 20.3 all-gather.39
  3446.0 22.9 all-gather.35
  3470.5 22.9 all-gather.37
where the time goes:
time: 3520 us; the launch traced here: 3500 us
  waiting for transfers between devices  2530 us (72%)
  matrix products  452 us (13%)
  local copies, waits for them, and re-layouts  258 us (7%)
  blocking collectives  151 us (4%)
  other arithmetic  81.5 us (2%)
    dot_general x108, matrix products, matmul(): return jnp.dot(left, right, preferred_element_type=jnp.float32)  351 us
    all_gather x1, waiting for transfers between devices, shards(): lax.all_gather(w_down, 'dp', axis=0, tiled=True)  327 us
    all_gather x1, waiting for transfers between devices, shards(): lax.all_gather(w_up, 'dp', axis=0, tiled=True)  321 us
    reduce_scatter x1, waiting for transfers between devices, shards(): lax.psum_scatter(local_grads[8].astype(jnp.bfloat16), 'dp', scatter_dimen...  296 us
    reduce_scatter x1, waiting for transfers between devices, shards(): lax.psum_scatter(local_grads[7].astype(jnp.bfloat16), 'dp', scatter_dimen...  292 us
    unnamed x38, waiting for transfers between devices  196 us
    all_gather x1, waiting for transfers between devices, shards(): lax.all_gather(w_qkv, 'dp', axis=0, tiled=True)  163 us
    reduce_scatter x1, waiting for transfers between devices, shards(): lax.psum_scatter(local_grads[0].astype(jnp.bfloat16), 'dp', scatter_dimen...  142 us
  transfers between devices with their start and end apart: 33, of which 28 were waited for; matrix products, arithmetic and copies ran while one was open for 12% of the time, Pallas kernels for 0%

commit v1 on v0

--- a/solution.py
+++ b/solution.py
@@ -67,7 +67,7 @@
 
 
 def head_prep(qkv_pre, qk_gains, qk_biases, row_pos, col_pos):
-    head_split = qkv_pre.reshape(qkv_pre.shape[0], 3, HEADS, HEAD)
+    head_split = qkv_pre.reshape(qkv_pre.shape[0], 3, -1, HEAD)
     queries = rope_two(layer_norm(head_split[:, 0], qk_gains[0], qk_biases[0]), row_pos, col_pos)
     keyset = rope_two(layer_norm(head_split[:, 1], qk_gains[1], qk_biases[1]), row_pos, col_pos)
     return (queries, keyset, head_split[:, 2])
@@ -99,6 +99,56 @@
     t5_own = jnp.sum(jnp.where(key_member, t5_len[None, :], 0), axis=1)
     key_valid = jnp.where(key_slot < CLIP_TOK, key_slot < clip_own, key_slot - CLIP_TOK < t5_own)
     return (seg_part[:, None] == key_image[None, :]) & key_valid[None, :]
+
+
+def swap_pairs(count, mask):
+    return [(rank, rank ^ mask) for rank in range(count)]
+
+
+def seq_blocks(block, count):
+    held = {0: block}
+    bit = count // 2
+    while bit:
+        for mask in list(held):
+            held[mask | bit] = lax.ppermute(held[mask], "seq", swap_pairs(count, bit))
+        bit //= 2
+    return [held[mask] for mask in range(count)]
+
+
+def seq_sum(parts, count):
+    held = dict(enumerate(parts))
+    bit = 1
+    while bit < count:
+        for mask in [m for m in held if m & bit]:
+            came = lax.ppermute(
+                held.pop(mask).astype(jnp.bfloat16), "seq", swap_pairs(count, bit)
+            )
+            held[mask ^ bit] = held[mask ^ bit] + came.astype(jnp.float32)
+        bit *= 2
+    return held[0]
+
+
+def seq_exchange(parts, count):
+    return [parts[0]] + [
+        lax.ppermute(parts[mask], "seq", swap_pairs(count, mask)) for mask in range(1, count)
+    ]
+
+
+def gather_rows(weight, seq_count, seq_rank):
+    rows = weight.shape[0]
+    if rows % seq_count:
+        return lax.all_gather(weight, "dp", axis=0, tiled=True)
+    own = lax.dynamic_slice_in_dim(weight, seq_rank * (rows // seq_count), rows // seq_count)
+    return lax.all_gather(own, ("dp", "seq"), axis=0, tiled=True)
+
+
+def scatter_rows(grad, dp_count, seq_count):
+    low = grad.astype(jnp.bfloat16)
+    if (grad.shape[0] // dp_count) % seq_count:
+        total = lax.psum_scatter(low, "dp", scatter_dimension=0, tiled=True)
+        return lax.psum(total, "seq").astype(jnp.float32)
+    total = lax.psum_scatter(low, ("dp", "seq"), scatter_dimension=0, tiled=True)
+    return lax.all_gather(total, "seq", axis=0, tiled=True).astype(jnp.float32)
 
 
 def shards(
@@ -125,58 +175,79 @@
     w_down,
     cotangent,
 ):
-    full_skip, full_mod, full_qkv, full_out, full_cq, full_ckv, full_co, full_up, full_down = (
-        lax.all_gather(w_skip, "dp", axis=0, tiled=True),
-        lax.all_gather(w_mod, "dp", axis=0, tiled=True),
-        lax.all_gather(w_qkv, "dp", axis=0, tiled=True),
-        lax.all_gather(w_out, "dp", axis=0, tiled=True),
-        lax.all_gather(w_cq, "dp", axis=0, tiled=True),
-        lax.all_gather(w_ckv, "dp", axis=0, tiled=True),
-        lax.all_gather(w_co, "dp", axis=0, tiled=True),
-        lax.all_gather(w_up, "dp", axis=0, tiled=True),
-        lax.all_gather(w_down, "dp", axis=0, tiled=True),
-    )
     local_tok = tokens.shape[0]
     model_width = tokens.shape[1]
     seq_count = lax.axis_size("seq")
+    dp_count = lax.axis_size("dp")
+    seq_rank = lax.axis_index("seq")
+    dp_rank = lax.axis_index("dp")
     bucket_len = local_tok * seq_count
     local_heads = HEADS // seq_count
+    head_cols = local_heads * HEAD
+    wide = w_up.shape[1]
+    part = wide // (dp_count * seq_count)
+    local_wide = part * dp_count
+    row_count = w_mod.shape[0]
     score_scale = HEAD ** (-0.5)
     block_rows = min(512, bucket_len)
     block_count = bucket_len // block_rows
-    seq_rank = lax.axis_index("seq")
+    order = seq_rank ^ jnp.arange(seq_count, dtype=jnp.int32)
+
+    full_skip = gather_rows(w_skip, seq_count, seq_rank)
+    own_qkv = lax.dynamic_index_in_dim(
+        w_qkv.reshape(row_count, 3, seq_count, head_cols), seq_rank, 2, keepdims=False
+    ).reshape(row_count, 3 * head_cols)
+    part_qkv = lax.all_gather(own_qkv, "dp", axis=0, tiled=True)
+    pad_rows = -(3 * row_count) % (8 * seq_count)
+    square = jnp.concatenate(
+        [w_out, w_cq, w_co, jnp.zeros((pad_rows, model_width), w_out.dtype)], axis=0
+    )
+    square = gather_rows(square, seq_count, seq_rank).reshape(dp_count, -1, model_width)
+    full_out, full_cq, full_co = (
+        square[:, i * row_count : (i + 1) * row_count].reshape(model_width, model_width)
+        for i in range(3)
+    )
+    full_ckv = gather_rows(w_ckv, seq_count, seq_rank)
+    own_up = lax.dynamic_index_in_dim(
+        w_up.reshape(row_count, dp_count, seq_count, part), seq_rank, 2, keepdims=False
+    ).reshape(row_count, local_wide)
+    part_up = lax.all_gather(own_up, "dp", axis=0, tiled=True)
+    part_down = lax.all_gather(
+        lax.dynamic_slice_in_dim(w_down, seq_rank * part, part), "dp", axis=0, tiled=True
+    )
+
     seg_all = segment_ids[0]
+    seg_local, member, _, _ = grid_positions(seg_all, grid_widths[0], seq_rank * local_tok, local_tok)
+    _, _, row_all, col_all = grid_positions(seg_all, grid_widths[0], 0, bucket_len)
+
+    def reorder(values):
+        return jnp.take(values.reshape(seq_count, local_tok), order, axis=0).reshape(-1)
+
+    row_pos, col_pos, seg_all = reorder(row_all), reorder(col_all), reorder(seg_all)
     seg_blocks = seg_all.reshape(block_count, block_rows)
-    seg_local, member, row_pos, col_pos = grid_positions(
-        seg_all, grid_widths[0], seq_rank * local_tok, local_tok
-    )
+
+    cond = silu_gate(timestep[0].astype(jnp.float32)).astype(jnp.bfloat16)
+    cond_all = lax.all_gather(cond, "dp", axis=0, tiled=True)
+    cond_rows = lax.dynamic_slice_in_dim(cond_all, dp_rank * row_count, row_count, axis=1)
+    shifts = lax.psum_scatter(matmul(cond_rows, w_mod), "dp", scatter_dimension=0, tiled=True)
+    time_shift = jnp.sum(jnp.where(member[:, :, None], shifts[None], 0.0), axis=1)
+
     joined = jnp.concatenate([tokens, skip], axis=1).astype(jnp.float32)
     h_float, pull_skip = jax.vjp(
         layer_norm, joined, ln_gains[0:2].reshape(-1), ln_biases[0:2].reshape(-1)
     )
     h_zero = h_float.astype(jnp.bfloat16)
     x_one = matmul(h_zero, full_skip)
-    time_cond = silu_gate(
-        jnp.dot(
-            member.astype(jnp.float32),
-            timestep[0].astype(jnp.float32),
-            precision=lax.Precision.HIGHEST,
-        )
-    ).astype(jnp.bfloat16)
-    time_shift = matmul(time_cond, full_mod)
     n_float, pull_one = jax.vjp(layer_norm, x_one, ln_gains[2], ln_biases[2])
     n_one = (n_float + time_shift).astype(jnp.bfloat16)
-    qkv_pre = matmul(n_one, full_qkv)
+    n_one_all = jnp.concatenate(seq_blocks(n_one, seq_count), axis=0)
+    qkv_pre = matmul(n_one_all, part_qkv)
 
     def prep_local(pre_rows, gains, biases):
         return head_prep(pre_rows, gains, biases, row_pos, col_pos)
 
     (queries, keyset, values), pull_heads = jax.vjp(prep_local, qkv_pre, qk_gains, qk_biases)
-    packed = (
-        jnp.stack([queries, keyset, values]).astype(jnp.bfloat16).reshape(3, local_tok, model_width)
-    )
-    spread_heads = lax.all_to_all(packed, "seq", split_axis=2, concat_axis=1, tiled=True)
-    by_head = spread_heads.reshape(3, bucket_len, local_heads, HEAD).transpose(0, 2, 1, 3)
+    by_head = jnp.stack([queries, keyset, values]).astype(jnp.bfloat16).transpose(0, 2, 1, 3)
 
     def block_scores(query_b, seg_b, key_h):
         return jnp.where(
@@ -201,13 +272,10 @@
         return (outs.reshape(bucket_len, HEAD), maxes, sums)
 
     head_out, row_maxes, row_sums = lax.map(self_forward, (by_head[0], by_head[1], by_head[2]))
-    attn_o = lax.all_to_all(
-        head_out.transpose(1, 0, 2).reshape(bucket_len, local_heads * HEAD),
-        "seq",
-        split_axis=0,
-        concat_axis=1,
-        tiled=True,
-    )
+
+    out_blocks = head_out.transpose(1, 0, 2).reshape(seq_count, local_tok, head_cols)
+    came = seq_exchange([out_blocks[k] for k in range(seq_count)], seq_count)
+    attn_o = jnp.take(jnp.stack(came), order, axis=0).transpose(1, 0, 2).reshape(local_tok, model_width)
     x_two = x_one + matmul(attn_o, full_out)
     n3_float, pull_three = jax.vjp(layer_norm, x_two, ln_gains[3], ln_biases[3])
     n_three = n3_float.astype(jnp.bfloat16)
@@ -232,15 +300,22 @@
     x_three = x_two + matmul(cross_o, full_co)
     n2_float, pull_two = jax.vjp(layer_norm, x_three, ln_gains[4], ln_biases[4])
     n_two = n2_float.astype(jnp.bfloat16)
-    up_proj = matmul(n_two, full_up)
+
+    n_two_all = jnp.concatenate(seq_blocks(n_two, seq_count), axis=0)
+    cot_all = jnp.concatenate(seq_blocks(cotangent, seq_count), axis=0)
+    up_proj = matmul(n_two_all, part_up)
     act_float, pull_gelu = jax.vjp(gelu_tanh, up_proj)
     act_low = act_float.astype(jnp.bfloat16)
-    block_out = (x_three + matmul(act_low, full_down)).astype(jnp.bfloat16)
-    grad_down = matmul(act_low.T, cotangent)
-    d_act = matmul(cotangent, full_down.T)
+    down_part = matmul(act_low, part_down).reshape(seq_count, local_tok, model_width)
+    block_out = (
+        x_three + seq_sum([down_part[k] for k in range(seq_count)], seq_count)
+    ).astype(jnp.bfloat16)
+    grad_down = matmul(act_low.T, cot_all)
+    d_act = matmul(cot_all, part_down.T)
     d_up = pull_gelu(d_act)[0].astype(jnp.bfloat16)
-    grad_up = matmul(n_two.T, d_up)
-    d_n_two = matmul(d_up, full_up.T)
+    grad_up = matmul(n_two_all.T, d_up)
+    d_two_part = matmul(d_up, part_up.T).reshape(seq_count, local_tok, model_width)
+    d_n_two = seq_sum([d_two_part[k] for k in range(seq_count)], seq_count)
     back_three_x, gain_four, bias_four = pull_two(d_n_two)
     d_x_three = cotangent.astype(jnp.float32) + back_three_x
     d_co = d_x_three.astype(jnp.bfloat16)
@@ -279,8 +354,14 @@
     d_attn = d_x_two.astype(jnp.bfloat16)
     grad_out = matmul(attn_o.T, d_attn)
     d_attn_o = matmul(d_attn, full_out.T).astype(jnp.bfloat16)
-    d_spread = lax.all_to_all(d_attn_o, "seq", split_axis=1, concat_axis=0, tiled=True)
-    d_by_head = d_spread.reshape(bucket_len, local_heads, HEAD).transpose(1, 0, 2)
+
+    d_turned = jnp.take(
+        d_attn_o.reshape(local_tok, seq_count, head_cols).transpose(1, 0, 2), order, axis=0
+    )
+    d_came = seq_exchange([d_turned[k] for k in range(seq_count)], seq_count)
+    d_by_head = (
+        jnp.concatenate(d_came, axis=0).reshape(bucket_len, local_heads, HEAD).transpose(1, 0, 2)
+    )
 
     def self_backward(head_items):
         query_h, key_h, value_h, d_out_h, row_max, row_sum = head_items
@@ -326,15 +407,24 @@
     d_heads = lax.map(
         self_backward, (by_head[0], by_head[1], by_head[2], d_by_head, row_maxes, row_sums)
     )
-    d_packed = d_heads.transpose(1, 2, 0, 3).reshape(3, bucket_len, local_heads * HEAD)
-    d_gathered = lax.all_to_all(d_packed, "seq", split_axis=1, concat_axis=2, tiled=True)
-    d_parts = d_gathered.astype(jnp.float32).reshape(3, local_tok, HEADS, HEAD)
+
+    d_parts = d_heads.transpose(1, 2, 0, 3).astype(jnp.float32)
     d_qkv_float, grad_qk_gain, grad_qk_bias = pull_heads((d_parts[0], d_parts[1], d_parts[2]))
     d_qkv = d_qkv_float.astype(jnp.bfloat16)
-    grad_qkv = matmul(n_one.T, d_qkv)
-    d_n_one = matmul(d_qkv, full_qkv.T)
+    grad_qkv = matmul(n_one_all.T, d_qkv)
+    d_one_part = matmul(d_qkv, part_qkv.T).reshape(seq_count, local_tok, model_width)
+    d_n_one = seq_sum([d_one_part[k] for k in range(seq_count)], seq_count)
     d_shift = d_n_one.astype(jnp.bfloat16)
-    grad_mod = matmul(time_cond.T, d_shift)
+    d_image = matmul(member.astype(jnp.bfloat16).T, d_shift)
+    d_image_all = jnp.sum(lax.all_gather(d_image, ("dp", "seq"), axis=0, tiled=True).reshape(
+        dp_count, seq_count, IMGS, model_width
+    ), axis=1).reshape(dp_count * IMGS, model_width)
+    grad_mod = jnp.dot(
+        cond_rows.astype(jnp.float32).T,
+        d_image_all,
+        precision=lax.Precision.HIGHEST,
+        preferred_element_type=jnp.float32,
+    )
     back_one_x, gain_one, bias_one = pull_one(d_n_one)
     d_x_one = d_x_two + back_one_x
     d_y = d_x_one.astype(jnp.bfloat16)
@@ -350,104 +440,38 @@
     gain_total, bias_total, ff_bias_total, qk_gain_total, qk_bias_total = lax.psum(
         (gain_rows, bias_rows, bias_four, grad_qk_gain, grad_qk_bias), ("dp", "seq")
     )
-    local_grads = (
-        grad_skip_w,
-        grad_mod,
-        grad_qkv,
-        grad_out,
-        grad_cq,
-        grad_ckv,
-        grad_co,
-        grad_up,
-        grad_down,
-    )
-    row_sums_w = (
-        lax.psum_scatter(
-            local_grads[0].astype(jnp.bfloat16), "dp", scatter_dimension=0, tiled=True
-        ).astype(jnp.float32),
-        lax.psum_scatter(
-            local_grads[1].astype(jnp.bfloat16), "dp", scatter_dimension=0, tiled=True
-        ).astype(jnp.float32),
-        lax.psum_scatter(
-            local_grads[2].astype(jnp.bfloat16), "dp", scatter_dimension=0, tiled=True
-        ).astype(jnp.float32),
-        lax.psum_scatter(
-            local_grads[3].astype(jnp.bfloat16), "dp", scatter_dimension=0, tiled=True
-        ).astype(jnp.float32),
-        lax.psum_scatter(
-            local_grads[4].astype(jnp.bfloat16), "dp", scatter_dimension=0, tiled=True
-        ).astype(jnp.float32),
-        lax.psum_scatter(
-            local_grads[5].astype(jnp.bfloat16), "dp", scatter_dimension=0, tiled=True
-        ).astype(jnp.float32),
-        lax.psum_scatter(
-            local_grads[6].astype(jnp.bfloat16), "dp", scatter_dimension=0, tiled=True
-        ).astype(jnp.float32),
-        lax.psum_scatter(
-            local_grads[7].astype(jnp.bfloat16), "dp", scatter_dimension=0, tiled=True
-        ).astype(jnp.float32),
-        lax.psum_scatter(
-            local_grads[8].astype(jnp.bfloat16), "dp", scatter_dimension=0, tiled=True
-        ).astype(jnp.float32),
-    )
-    split_sums = (
-        lax.psum_scatter(
-            row_sums_w[0].astype(jnp.bfloat16), "seq", scatter_dimension=1, tiled=True
-        ).astype(jnp.float32),
-        lax.psum_scatter(
-            row_sums_w[1].astype(jnp.bfloat16), "seq", scatter_dimension=1, tiled=True
-        ).astype(jnp.float32),
-        lax.psum_scatter(
-            row_sums_w[2].astype(jnp.bfloat16), "seq", scatter_dimension=1, tiled=True
-        ).astype(jnp.float32),
-        lax.psum_scatter(
-            row_sums_w[3].astype(jnp.bfloat16), "seq", scatter_dimension=1, tiled=True
-        ).astype(jnp.float32),
-        lax.psum_scatter(
-            row_sums_w[4].astype(jnp.bfloat16), "seq", scatter_dimension=1, tiled=True
-        ).astype(jnp.float32),
-        lax.psum_scatter(
-            row_sums_w[5].astype(jnp.bfloat16), "seq", scatter_dimension=1, tiled=True
-        ).astype(jnp.float32),
-        lax.psum_scatter(
-            row_sums_w[6].astype(jnp.bfloat16), "seq", scatter_dimension=1, tiled=True
-        ).astype(jnp.float32),
-        lax.psum_scatter(
-            row_sums_w[7].astype(jnp.bfloat16), "seq", scatter_dimension=1, tiled=True
-        ).astype(jnp.float32),
-        lax.psum_scatter(
-            row_sums_w[8].astype(jnp.bfloat16), "seq", scatter_dimension=1, tiled=True
-        ).astype(jnp.float32),
-    )
-    reduced = (
-        lax.all_gather(split_sums[0].astype(jnp.bfloat16), "seq", axis=1, tiled=True).astype(
-            jnp.float32
-        ),
-        lax.all_gather(split_sums[1].astype(jnp.bfloat16), "seq", axis=1, tiled=True).astype(
-            jnp.float32
-        ),
-        lax.all_gather(split_sums[2].astype(jnp.bfloat16), "seq", axis=1, tiled=True).astype(
-            jnp.float32
-        ),
-        lax.all_gather(split_sums[3].astype(jnp.bfloat16), "seq", axis=1, tiled=True).astype(
-            jnp.float32
-        ),
-        lax.all_gather(split_sums[4].astype(jnp.bfloat16), "seq", axis=1, tiled=True).astype(
-            jnp.float32
-        ),
-        lax.all_gather(split_sums[5].astype(jnp.bfloat16), "seq", axis=1, tiled=True).astype(
-            jnp.float32
-        ),
-        lax.all_gather(split_sums[6].astype(jnp.bfloat16), "seq", axis=1, tiled=True).astype(
-            jnp.float32
-        ),
-        lax.all_gather(split_sums[7].astype(jnp.bfloat16), "seq", axis=1, tiled=True).astype(
-            jnp.float32
-        ),
-        lax.all_gather(split_sums[8].astype(jnp.bfloat16), "seq", axis=1, tiled=True).astype(
-            jnp.float32
-        ),
-    )
+
+    square_grad = jnp.concatenate(
+        [g.reshape(dp_count, row_count, model_width) for g in (grad_out, grad_cq, grad_co)]
+        + [jnp.zeros((dp_count, pad_rows, model_width), jnp.float32)],
+        axis=1,
+    ).reshape(-1, model_width)
+    square_total = scatter_rows(square_grad, dp_count, seq_count)
+    grad_out, grad_cq, grad_co = (
+        square_total[i * row_count : (i + 1) * row_count] for i in range(3)
+    )
+    total_qkv = lax.psum_scatter(
+        grad_qkv.astype(jnp.bfloat16), "dp", scatter_dimension=0, tiled=True
+    )
+    grad_qkv = (
+        lax.all_gather(total_qkv, "seq", axis=0)
+        .reshape(seq_count, row_count, 3, head_cols)
+        .transpose(1, 2, 0, 3)
+        .reshape(row_count, 3 * model_width)
+        .astype(jnp.float32)
+    )
+    total_up = lax.psum_scatter(grad_up.astype(jnp.bfloat16), "dp", scatter_dimension=0, tiled=True)
+    grad_up = (
+        lax.all_gather(total_up, "seq", axis=0)
+        .reshape(seq_count, row_count, dp_count, part)
+        .transpose(1, 2, 0, 3)
+        .reshape(row_count, wide)
+        .astype(jnp.float32)
+    )
+    total_down = lax.psum_scatter(
+        grad_down.astype(jnp.bfloat16), "dp", scatter_dimension=0, tiled=True
+    )
+    grad_down = lax.all_gather(total_down, "seq", axis=0, tiled=True).astype(jnp.float32)
     return (
         block_out,
         grad_tokens,
@@ -457,15 +481,15 @@
         ff_bias_total,
         qk_gain_total,
         qk_bias_total,
-        reduced[0],
-        reduced[1],
-        reduced[2],
-        reduced[3],
-        reduced[4],
-        reduced[5],
-        reduced[6],
-        reduced[7],
-        reduced[8],
+        scatter_rows(grad_skip_w, dp_count, seq_count),
+        grad_mod,
+        grad_qkv,
+        grad_out,
+        grad_cq,
+        scatter_rows(grad_ckv, dp_count, seq_count),
+        grad_co,
+        grad_up,
+        grad_down,
     )
 
 

time: 3520 us -> 1660 us (0.47)
  waiting for transfers between devices: 2530 us -> 851 us
  matrix products: 452 us -> 324 us
  local copies, waits for them, and re-layouts: 258 us -> 200 us
    all_gather x12 -> x10, waiting for transfers between devices: 1110 us -> 160 us  [the longest x1 57.5 us: shards(): lax.all_gather(lax.dynamic_slice_in_dim(w_down, seq_rank * part, part), '...]
    reduce_scatter x10 -> x4, waiting for transfers between devices: 1160 us -> 335 us  [the longest x1 125 us: scatter_rows(): lax.psum_scatter(low, ('dp', 'seq'), scatter_dimension=0, tiled=True)]
    ppermute x0 -> x24, waiting for transfers between devices: none -> 165 us  [the longest x9 96.1 us: seq_sum(): lax.ppermute(held.pop(mask).astype(jnp.bfloat16), 'seq', swap_pairs(count...]
    dot_general x108, matrix products: 351 us -> 223 us  [matmul(): return jnp.dot(left, right, preferred_element_type=jnp.float32)]
    all_to_all x3 -> x0, waiting for transfers between devices: 60.8 us -> none  [the longest x1 46.8 us: shards(): lax.all_to_all(packed, 'seq', split_axis=2, concat_axis=1, tiled=True)]
    all_to_all x1 -> x0, blocking collectives: 59.6 us -> none  [shards(): lax.all_to_all(d_packed, 'seq', split_axis=1, concat_axis=2, tiled=True)]
    all_gather x6 -> x4, blocking collectives: 51.4 us -> 95.1 us  [the longest x1 42.2 us: shards(): lax.all_gather(d_image, ('dp', 'seq'), axis=0, tiled=True)]
    unnamed x269 -> x287, local copies, waits for them, and re-layouts: 76.3 us -> 41.2 us
  transfers between devices with their start and end apart: 33 -> 41, of which waited for: 28 -> 21; matrix products, arithmetic and copies ran while one was open for 12% -> 25% of each run, Pallas kernels for 0% -> 0%
where the time goes in v1:
time: 1660 us; the launch traced here: 1650 us
  waiting for transfers between devices  851 us (51%)
  matrix products  324 us (20%)
  local copies, waits for them, and re-layouts  200 us (12%)
  blocking collectives  134 us (8%)
  other arithmetic  98.5 us (6%)
  starting transfers between devices  23 us (1%)
  between operations  18.5 us (1%)
    dot_general x108, matrix products, matmul(): return jnp.dot(left, right, preferred_element_type=jnp.float32)  223 us
    unnamed x20, waiting for transfers between devices  191 us
    reduce_scatter x1, waiting for transfers between devices, scatter_rows(): lax.psum_scatter(low, ('dp', 'seq'), scatter_dimension=0, tiled=True)  125 us
    ppermute x9, waiting for transfers between devices, seq_sum(): lax.ppermute(held.pop(mask).astype(jnp.bfloat16), 'seq', swap_pairs(count...  96.1 us
    reduce_scatter x1, waiting for transfers between devices, shards(): lax.psum_scatter(grad_up.astype(jnp.bfloat16), 'dp', scatter_dimension=0,...  93.6 us
    reduce_scatter x1, waiting for transfers between devices, shards(): lax.psum_scatter(grad_down.astype(jnp.bfloat16), 'dp', scatter_dimension=...  93.1 us
    all_gather x1, waiting for transfers between devices, shards(): lax.all_gather(lax.dynamic_slice_in_dim(w_down, seq_rank * part, part), '...  57.5 us
    all_gather x1, waiting for transfers between devices, shards(): part_qkv = lax.all_gather(own_qkv, 'dp', axis=0, tiled=True)  49.4 us
  transfers between devices with their start and end apart: 41, of which 21 were waited for; matrix products, arithmetic and copies ran while one was open for 25% of the time, Pallas kernels for 0%

profile of v1, /device:TPU:1, one launch (start us, length us, event | category | flops | bytes accessed | tf_op | source)
XLA Modules:
  0.0 1651.1 jit_solution(8955638515425974911)
XLA Ops:
  9.0 25.6 %all-gather.2 = bf16[8,3,1408]{2,1,0:T(4,128)(2,1)S(1)} all-gather(bf16[1,3,1408]{2,1,0:T(4,128)(2,1)S(1)} %fusion.98), channel_id=1, replica_groups=mesh['dp'=8,'seq'=4] {'dp'}, dimensions={0}, use_global_device_ids=true | all-gather | bytes 76032 | tf_op jit(solution)/shard_map/all_gather | solution.py:230
  80.9 46.8 %all-reduce.25.cloned.1.call-done = f32[24,1408]{1,0:T(8,128)} async-done(((f32[24,1408]{1,0:T(8,128)}), f32[24,1408]{1,0:T(8,128)}) %all-reduce.25.cloned.1.call-update) | async-done | bytes 135184
  146.5 22.7 %collective-permute-done.1 = bf16[384,1408]{1,0:T(8,128)(2,1)} collective-permute-done((bf16[384,1408]{1,0:T(8,128)(2,1)}, bf16[384,1408]{1,0:T(8,128)(2,1)}, u32[]{:S(2)}, u32[]{:S(2)}) %collective-permute-start.1) | collective-permute-done | bytes 1081376 | tf_op jit(solution)/shard_map/ppermute | solution.py:113
  171.0 27.0 %all-gather.21.cloned.1.call-done = bf16[1024,2816]{1,0:T(8,128)(2,1)} async-done(((bf16[32,2816]{1,0:T(8,128)(2,1)}), bf16[1024,2816]{1,0:T(8,128)(2,1)}) %all-gather.21.cloned.1.call-update) | async-done | bytes 5767184 | tf_op jit(solution)/shard_map/all_gather | solution.py:142
  209.1 49.4 %all-gather.17.cloned.1.call-done = bf16[1408,1056]{1,0:T(8,128)(2,1)} async-done(((bf16[176,1056]{1,0:T(8,128)(2,1)}), bf16[1408,1056]{1,0:T(8,128)(2,1)}) %all-gather.17.cloned.1.call-update) | async-done | bytes 2973712 | tf_op jit(solution)/shard_map/all_gather | solution.py:200
  277.7 42.6 %while.54 = (s32[]{:T(128)}, bf16[4,1536,88]{1,2,0:T(8,128)(2,1)S(1)}, f32[4,3,512,1]{2,3,1,0:T(1,128)}, f32[4,3,512,1]{2,3,1,0:T(1,128)}, bf16[4,1536,88]{2,1,0...) while((s32[]{:T(128)}, ...), condition=%wide.region_18.20_spmd, body=%wide.region_13.19_spmd.sunk | while | flops 283945984 | bytes 13758822 | solution.py:274
  349.7 18.7 %all-gather.19.cloned.1.call-done = bf16[4352,1408]{1,0:T(8,128)(2,1)} async-done(((bf16[136,1408]{1,0:T(8,128)(2,1)}), bf16[4352,1408]{1,0:T(8,128)(2,1)}) %all-gather.19.cloned.1.call-update) | async-done | bytes 12255248 | tf_op jit(solution)/shard_map/all_gather | solution.py:142
  383.0 16.6 %fusion.158 = (f32[16,384]{1,0:T(8,128)S(1)}, f32[16,384,999]{1,2,0:T(8,128)}) fusion(pred[384,999]{0,1:T(8,128)(4,1)S(1)} %copy-done.67, bf16[384,16,88]{0,2,1:T(8,128)(2,1)S(1)} %bitcast.377, bf16[999,16,88]{0,2,1:T(8,128)(2,1)} %bitcast.367), kind=kOutput, calls=%fused_computation.389 | convolution fusion | flops 1104815104 | bytes 28854144 | tf_op jit(solution)/shard_map/sub | solution.py:41
  417.3 24.2 %collective-permute-done.7 = bf16[384,1408]{1,0:T(8,128)(2,1)} collective-permute-done((bf16[384,1408]{1,0:T(8,128)(2,1)}, bf16[384,1408]{1,0:T(8,128)(2,1)}, u32[]{:S(2)}, u32[]{:S(2)}) %collective-permute-start.7) | collective-permute-done | bytes 1081376 | tf_op jit(solution)/shard_map/ppermute | solution.py:113
  448.1 13.2 fusion.84
  461.3 57.5 %all-gather.25.cloned.1.call-done = bf16[1536,1408]{1,0:T(8,128)(2,1)} async-done(((bf16[192,1408]{1,0:T(8,128)(2,1)}), bf16[1536,1408]{1,0:T(8,128)(2,1)}) %all-gather.25.cloned.1.call-update) | async-done | bytes 4325392 | tf_op jit(solution)/shard_map/all_gather | solution.py:215
  518.8 18.8 %fusion.44 = bf16[1536,1536]{1,0:T(8,128)(2,1)S(1)} fusion(f32[1536,1536]{1,0:T(8,128)} %fusion.84, bf16[1536,1408]{1,0:T(8,128)(2,1)} %constant_dynamic-update-slice_fusion.3, bf16[1536,1408]{1,0:T(8,128)(2,1)} %all-gather.25.cloned.1.call-done), kind=kOutput, calls=%fused_computation.90 | convolution fusion | flops 6700400640 | bytes 22806528 | tf_op jit(solution)/shard_map/dot_general | solution.py:18
  565.9 22.4 %collective-permute-done.17 = bf16[384,1408]{1,0:T(8,128)(2,1)S(1)} collective-permute-done((bf16[384,1408]{1,0:T(8,128)(2,1)S(1)}, bf16[384,1408]{1,0:T(8,128)(2,1)S(1)}, u32[]{:S(2)}, u32[]{:S(2)}) %collective-permute-start.17) | collective-permute-done | bytes 1081376 | tf_op jit(solution)/shard_map/ppermute | solution.py:123
  589.9 21.6 %collective-permute-done.11 = bf16[384,1408]{1,0:T(8,128)(2,1)S(1)} collective-permute-done((bf16[384,1408]{1,0:T(8,128)(2,1)S(1)}, bf16[384,1408]{1,0:T(8,128)(2,1)S(1)}, u32[]{:S(2)}, u32[]{:S(2)}) %collective-permute-start.11) | collective-permute-done | bytes 1081376 | tf_op jit(solution)/shard_map/ppermute | solution.py:123
  620.0 21.8 %multiply_reduce_fusion.1 = (f32[16,384]{1,0:T(8,128)S(1)}, f32[16,384,999]{1,2,0:T(8,128)}) fusion(f32[16,384,999]{1,2,0:T(8,128)} %get-tuple-element.643, f32[16,384]{1,0:T(8,128)S(1)} %get-tuple-element.642, bf16[384,16,88]{0,2,1:T(8,128)(2,1)S(1)} %bitcast.395, bf16[999,16,88]{0,2,1:T(8,128)(2,1)} %bitcast.386), kind=kOutput, calls=%fused_computation.69 | convolution fusion | flops 1098670080 | bytes 53046528 | tf_op jit(solution)/shard_map/thd,khd->htk/dot_general | solution.py:324
  641.8 16.4 multiply_convert_fusion.1
  695.7 75.5 %while.56 = (s32[]{:T(128)}, bf16[4,3,1536,88]{2,3,1,0:T(8,128)(2,1)}, bf16[4,1536,88]{2,1,0:T(8,128)(2,1)}, bf16[4,1536,88]{1,2,0:T(8,128)(2,1)}, f32[4,3,512,1...) while((s32[]{:T(128)}, ...), condition=%wide.region_36.39_spmd, body=%wide.region_32.38_spmd.sunk | while | flops 704179712 | bytes 34646480 | solution.py:407
  719.0 13.0 while.58
  737.8 13.0 while.58
  807.5 13.8 convolution_convert_fusion.1
  845.1 23.1 %reduce-scatter.15.cloned.1.call-done = bf16[176,1056]{1,0:T(8,128)(2,1)} async-done(((bf16[1408,1056]{1,0:T(8,128)(2,1)}), bf16[176,1056]{1,0:T(8,128)(2,1)}) %reduce-scatter.15.cloned.1.call-update) | async-done | bytes 371728 | tf_op jit(solution)/shard_map/reduce_scatter | solution.py:453
  868.3 93.6 %reduce-scatter.17.cloned.1.call-done = bf16[176,1536]{1,0:T(8,128)(2,1)} async-done(((bf16[1408,1536]{1,0:T(8,128)(2,1)}), bf16[176,1536]{1,0:T(8,128)(2,1)}) %reduce-scatter.17.cloned.1.call-update) | async-done | bytes 540688 | tf_op jit(solution)/shard_map/reduce_scatter | solution.py:463
  962.0 93.1 %reduce-scatter.19.cloned.1.call-done = bf16[192,1408]{1,0:T(8,128)(2,1)} async-done(((bf16[1536,1408]{1,0:T(8,128)(2,1)}), bf16[192,1408]{1,0:T(8,128)(2,1)}) %reduce-scatter.19.cloned.1.call-update) | async-done | bytes 540688 | tf_op jit(solution)/shard_map/reduce_scatter | solution.py:471
  1055.7 15.5 fusion.47
  1080.9 21.1 %convert_bitcast_fusion.3 = bf16[1024,2816]{0,1:T(8,128)(2,1)} fusion(f32[999,1408]{0,1:T(8,128)} %bitcast.415, f32[999,1408]{0,1:T(8,128)S(1)} %bitcast.373, bf16[1,999,1024]{2,1,0:T(8,128)(2,1)S(1)} %copy-done.131), kind=kOutput, calls=%fused_computation.105 | convolution fusion | flops 34574102528 | bytes 19065856 | tf_op jit(solution)/shard_map/dot_general | solution.py:344
  1125.2 49.5 %collective-permute-done.23 = bf16[384,1408]{1,0:T(8,128)(2,1)S(1)} collective-permute-done((bf16[384,1408]{1,0:T(8,128)(2,1)S(1)}, bf16[384,1408]{1,0:T(8,128)(2,1)S(1)}, u32[]{:S(2)}, u32[]{:S(2)}) %collective-permute-start.23) | collective-permute-done | bytes 1081376 | tf_op jit(solution)/shard_map/ppermute | solution.py:123
  1197.8 42.2 %all-gather.3 = f32[32,3,1408]{2,1,0:T(4,128)S(1)} all-gather(f32[1,3,1408]{2,1,0:T(4,128)S(1)} %convolution_bitcast_fusion), channel_id=1, replica_groups=mesh['dp'=8,'seq'=4] {'dp','seq'}, dimensions={0}, use_global_device_ids=true | all-gather | bytes 557568 | tf_op jit(solution)/shard_map/all_gather | solution.py:419
  1248.3 38.7 %all-reduce.22 = (f32[5,1408]{1,0:T(8,128)}, f32[4,1408]{1,0:T(4,128)}, f32[1408]{0:T(1024)}, f32[2,88]{1,0:T(2,128)}, f32[2,88]{1,0:T(2,128)}) all-reduce(f32[5,1408]{1,0:T(8,128)S(1)} %stack.60, f32[4,1408]{1,0:T(4,128)S(1)} %pad_maximum_fusion.8, f32[1408]{0:T(1024)S(1)} %copy-done.84, ...), channel_id=1, replica_groups=mesh['dp'=8,'seq'=4] {'dp','seq'}, use_global_device_ids=true, to_apply=%region_49.52 | all-reduce | flops 14432 | bytes 115456 | tf_op jit(solution)/shard_map/psum | solution.py:440
  1334.0 124.7 %reduce-scatter.21.cloned.1.call-done = bf16[32,2816]{1,0:T(8,128)(2,1)} async-done(((bf16[1024,2816]{1,0:T(8,128)(2,1)}), bf16[32,2816]{1,0:T(8,128)(2,1)}) %reduce-scatter.21.cloned.1.call-update) | async-done | bytes 180240 | tf_op jit(solution)/shard_map/reduce_scatter | solution.py:150
  1458.7 13.2 all_gather.60
  1473.1 144.2 %reduce-scatter.23.cloned.1.call-done = bf16[88,1408]{1,0:T(8,128)(2,1)} async-done(((bf16[2816,1408]{1,0:T(8,128)(2,1)}), bf16[88,1408]{1,0:T(8,128)(2,1)}) %reduce-scatter.23.cloned.1.call-update) | async-done | bytes 247824
  1617.3 14.1 all_gather.55
  (851 shorter events, 593.8 us)
Async XLA Ops:
  8.0 119.7 %all-reduce.25.cloned.1.call-start = ((), (), s32[]{:S(2)}) async-start(), calls=%async_computation.20 | async-start | bytes 270336
  36.7 93.8 %all-gather.15.cloned.1.call-start = ((), (), s32[]{:S(2)}) async-start(), calls=%async_computation.6 | async-start | bytes 8177664 | tf_op jit(solution)/shard_map/all_gather | solution.py:142
  38.4 159.5 %all-gather.21.cloned.1.call-start = ((), (), s32[]{:S(2)}) async-start(), calls=%async_computation.9 | async-start | bytes 5947392 | tf_op jit(solution)/shard_map/all_gather | solution.py:142
  40.1 218.4 %all-gather.17.cloned.1.call-start = ((), (), s32[]{:S(2)}) async-start(), calls=%async_computation.7 | async-start | bytes 3649536 | tf_op jit(solution)/shard_map/all_gather | solution.py:200
  50.2 318.3 %all-gather.19.cloned.1.call-start = ((), (), s32[]{:S(2)}) async-start(), calls=%async_computation.8 | async-start | bytes 12638208 | tf_op jit(solution)/shard_map/all_gather | solution.py:142
  53.0 395.1 %all-gather.23.cloned.1.call-start = ((), (), s32[]{:S(2)}) async-start(), calls=%async_computation.10 | async-start | bytes 4866048 | tf_op jit(solution)/shard_map/all_gather | solution.py:214
  70.0 448.8 %all-gather.25.cloned.1.call-start = ((), (), s32[]{:S(2)}) async-start(), calls=%async_computation.11 | async-start | bytes 4866048 | tf_op jit(solution)/shard_map/all_gather | solution.py:215
  70.1 346.7 %collective-permute-start.13 = (bf16[384,1408]{1,0:T(8,128)(2,1)}, bf16[384,1408]{1,0:T(8,128)(2,1)}, u32[]{:S(2)}, u32[]{:S(2)}) collective-permute-start(bf16[384,1408]{1,0:T(8,128)(2,1)} %param.55), channel_id=1, source_target_pairs={{0,2},{1,3},{2,0},{3,1},{4,6},{5,7},{6,4},{7,5},{8,10},{9,11},{10,... | collective-permute-start | bytes 3244040 | tf_op jit(solution)/shard_map/ppermute | solution.py:113
  72.3 795.9 %reduce-scatter.15.cloned.1.call-start = ((), (), s32[]{:S(2)}) async-start(), calls=%async_computation.12 | async-start | bytes 3649536 | tf_op jit(solution)/shard_map/reduce_scatter | solution.py:453
  141.7 27.5 %collective-permute-start.1 = (bf16[384,1408]{1,0:T(8,128)(2,1)}, bf16[384,1408]{1,0:T(8,128)(2,1)}, u32[]{:S(2)}, u32[]{:S(2)}) collective-permute-start(bf16[384,1408]{1,0:T(8,128)(2,1)} %add_convert_fusion.5), channel_id=1, source_target_pairs={{0,2},{1,3},{2,0},{3,1},{4,6},{5,7},{6,4},{7,5},{8,10},{9,11},{10,... | collective-permute-start | bytes 3244040 | tf_op jit(solution)/shard_map/ppermute | solution.py:113
  144.6 113.9 %collective-permute-start = (bf16[384,1408]{1,0:T(8,128)(2,1)}, bf16[384,1408]{1,0:T(8,128)(2,1)S(1)}, u32[]{:S(2)}, u32[]{:S(2)}) collective-permute-start(bf16[384,1408]{1,0:T(8,128)(2,1)} %add_convert_fusion.5), channel_id=1, source_target_pairs={{0,1},{1,0},{2,3},{3,2},{4,5},{5,4},{6,7},{7,6},{8,9},{9,8},{10,11... | collective-permute-start | bytes 3244040 | tf_op jit(solution)/shard_map/ppermute | solution.py:113
  169.2 89.2 %collective-permute-start.2 = (bf16[384,1408]{1,0:T(8,128)(2,1)}, bf16[384,1408]{1,0:T(8,128)(2,1)S(1)}, u32[]{:S(2)}, u32[]{:S(2)}) collective-permute-start(bf16[384,1408]{1,0:T(8,128)(2,1)} %collective-permute-done.1), channel_id=1, source_target_pairs={{0,1},{1,0},{2,3},{3,2},{4,5},{5,4},{6,7},{7,6},{8,9},{9,8},{10,11... | collective-permute-start | bytes 3244040 | tf_op jit(solution)/shard_map/ppermute | solution.py:113
  320.4 18.7 %collective-permute-start.5 = (bf16[384,352]{0,1:T(8,128)(2,1)S(1)}, bf16[384,352]{0,1:T(8,128)(2,1)S(1)}, u32[]{:S(2)}, u32[]{:S(2)}) collective-permute-start(bf16[384,352]{0,1:T(8,128)(2,1)S(1)} %bitcast.403), channel_id=1, source_target_pairs={{0,3},{1,2},{2,1},{3,0},{4,7},{5,6},{6,5},{7,4},{8,11},{9,10},{10,... | collective-permute-start | bytes 811016 | tf_op jit(solution)/shard_map/ppermute | solution.py:133
  323.8 24.6 %collective-permute-start.4 = (bf16[384,352]{0,1:T(8,128)(2,1)S(1)}, bf16[384,352]{0,1:T(8,128)(2,1)S(1)}, u32[]{:S(2)}, u32[]{:S(2)}) collective-permute-start(bf16[384,352]{0,1:T(8,128)(2,1)S(1)} %bitcast.401), channel_id=1, source_target_pairs={{0,2},{1,3},{2,0},{3,1},{4,6},{5,7},{6,4},{7,5},{8,10},{9,11},{10,... | collective-permute-start | bytes 811016 | tf_op jit(solution)/shard_map/ppermute | solution.py:133
  324.0 24.5 %collective-permute-start.3 = (bf16[384,352]{0,1:T(8,128)(2,1)S(1)}, bf16[384,352]{0,1:T(8,128)(2,1)S(1)}, u32[]{:S(2)}, u32[]{:S(2)}) collective-permute-start(bf16[384,352]{0,1:T(8,128)(2,1)S(1)} %bitcast.399), channel_id=1, source_target_pairs={{0,1},{1,0},{2,3},{3,2},{4,5},{5,4},{6,7},{7,6},{8,9},{9,8},{10,11... | collective-permute-start | bytes 811016 | tf_op jit(solution)/shard_map/ppermute | solution.py:133
  416.0 25.5 %collective-permute-start.7 = (bf16[384,1408]{1,0:T(8,128)(2,1)}, bf16[384,1408]{1,0:T(8,128)(2,1)}, u32[]{:S(2)}, u32[]{:S(2)}) collective-permute-start(bf16[384,1408]{1,0:T(8,128)(2,1)} %add_convert_fusion.3), channel_id=1, source_target_pairs={{0,2},{1,3},{2,0},{3,1},{4,6},{5,7},{6,4},{7,5},{8,10},{9,11},{10,... | collective-permute-start | bytes 3244040 | tf_op jit(solution)/shard_map/ppermute | solution.py:113
  416.3 27.4 %collective-permute-start.12 = (bf16[384,1408]{1,0:T(8,128)(2,1)S(1)}, bf16[384,1408]{1,0:T(8,128)(2,1)S(1)}, u32[]{:S(2)}, u32[]{:S(2)}) collective-permute-start(bf16[384,1408]{1,0:T(8,128)(2,1)S(1)} %copy-done.26), channel_id=1, source_target_pairs={{0,1},{1,0},{2,3},{3,2},{4,5},{5,4},{6,7},{7,6},{8,9},{9,8},{10,11... | collective-permute-start | bytes 3244040 | tf_op jit(solution)/shard_map/ppermute | solution.py:113
  416.8 30.2 %collective-permute-start.14 = (bf16[384,1408]{1,0:T(8,128)(2,1)}, bf16[384,1408]{1,0:T(8,128)(2,1)S(1)}, u32[]{:S(2)}, u32[]{:S(2)}) collective-permute-start(bf16[384,1408]{1,0:T(8,128)(2,1)} %collective-permute-done.13), channel_id=1, source_target_pairs={{0,1},{1,0},{2,3},{3,2},{4,5},{5,4},{6,7},{7,6},{8,9},{9,8},{10,11... | collective-permute-start | bytes 3244040 | tf_op jit(solution)/shard_map/ppermute | solution.py:113
  416.9 31.2 %collective-permute-start.6 = (bf16[384,1408]{1,0:T(8,128)(2,1)}, bf16[384,1408]{1,0:T(8,128)(2,1)}, u32[]{:S(2)}, u32[]{:S(2)}) collective-permute-start(bf16[384,1408]{1,0:T(8,128)(2,1)} %add_convert_fusion.3), channel_id=1, source_target_pairs={{0,1},{1,0},{2,3},{3,2},{4,5},{5,4},{6,7},{7,6},{8,9},{9,8},{10,11... | collective-permute-start | bytes 3244040 | tf_op jit(solution)/shard_map/ppermute | solution.py:113
  563.3 25.0 %collective-permute-start.17 = (bf16[384,1408]{1,0:T(8,128)(2,1)S(1)}, bf16[384,1408]{1,0:T(8,128)(2,1)S(1)}, u32[]{:S(2)}, u32[]{:S(2)}) collective-permute-start(bf16[384,1408]{1,0:T(8,128)(2,1)S(1)} %fusion.66), channel_id=1, source_target_pairs={{0,2},{1,3},{2,0},{3,1},{4,6},{5,7},{6,4},{7,5},{8,10},{9,11},{10,... | collective-permute-start | bytes 3244040 | tf_op jit(solution)/shard_map/ppermute | solution.py:123
  564.6 25.3 %collective-permute-start.9 = (bf16[384,1408]{1,0:T(8,128)(2,1)S(1)}, bf16[384,1408]{1,0:T(8,128)(2,1)S(1)}, u32[]{:S(2)}, u32[]{:S(2)}) collective-permute-start(bf16[384,1408]{1,0:T(8,128)(2,1)S(1)} %get-tuple-element.580), channel_id=1, source_target_pairs={{0,1},{1,0},{2,3},{3,2},{4,5},{5,4},{6,7},{7,6},{8,9},{9,8},{10,11... | collective-permute-start | bytes 3244040 | tf_op jit(solution)/shard_map/ppermute | solution.py:123
  565.6 45.9 %collective-permute-start.11 = (bf16[384,1408]{1,0:T(8,128)(2,1)S(1)}, bf16[384,1408]{1,0:T(8,128)(2,1)S(1)}, u32[]{:S(2)}, u32[]{:S(2)}) collective-permute-start(bf16[384,1408]{1,0:T(8,128)(2,1)S(1)} %fusion.68), channel_id=1, source_target_pairs={{0,2},{1,3},{2,0},{3,1},{4,6},{5,7},{6,4},{7,5},{8,10},{9,11},{10,... | collective-permute-start | bytes 3244040 | tf_op jit(solution)/shard_map/ppermute | solution.py:123
  795.9 166.0 %reduce-scatter.17.cloned.1.call-start = ((), (), s32[]{:S(2)}) async-start(), calls=%async_computation.14 | async-start | bytes 4866048 | tf_op jit(solution)/shard_map/reduce_scatter | solution.py:463
  807.4 247.7 %reduce-scatter.19.cloned.1.call-start = ((), (), s32[]{:S(2)}) async-start(), calls=%async_computation.15 | async-start | bytes 4866048 | tf_op jit(solution)/shard_map/reduce_scatter | solution.py:471
  821.3 426.8 %reduce-scatter.25.cloned.1.call-start = ((), (), s32[]{:S(2)}) async-start(), calls=%async_computation.22 | async-start | bytes 12638208
  845.1 446.0 %all-gather.31.cloned.1.call-start = ((), (), s32[]{:S(2)}) async-start(), calls=%async_computation.17 | async-start | bytes 2027520 | tf_op jit(solution)/shard_map/all_gather | solution.py:457
  868.2 439.8 %all-gather.33.cloned.1.call-start = ((), (), s32[]{:S(2)}) async-start(), calls=%async_computation.18 | async-start | bytes 2703360 | tf_op jit(solution)/shard_map/all_gather | solution.py:465
  961.9 368.1 %all-gather.29.cloned.1.call-start = ((), (), s32[]{:S(2)}) async-start(), calls=%async_computation.16 | async-start | bytes 2703360 | tf_op jit(solution)/shard_map/all_gather | solution.py:474
  1055.1 403.6 %reduce-scatter.21.cloned.1.call-start = ((), (), s32[]{:S(2)}) async-start(), calls=%async_computation.19 | async-start | bytes 5947392 | tf_op jit(solution)/shard_map/reduce_scatter | solution.py:150
  1110.2 507.1 %reduce-scatter.23.cloned.1.call-start = ((), (), s32[]{:S(2)}) async-start(), calls=%async_computation.21 | async-start | bytes 8177664
  1123.6 51.0 %collective-permute-start.23 = (bf16[384,1408]{1,0:T(8,128)(2,1)S(1)}, bf16[384,1408]{1,0:T(8,128)(2,1)S(1)}, u32[]{:S(2)}, u32[]{:S(2)}) collective-permute-start(bf16[384,1408]{1,0:T(8,128)(2,1)S(1)} %fusion.64), channel_id=1, source_target_pairs={{0,2},{1,3},{2,0},{3,1},{4,6},{5,7},{6,4},{7,5},{8,10},{9,11},{10,... | collective-permute-start | bytes 3244040 | tf_op jit(solution)/shard_map/ppermute | solution.py:123
  1186.9 453.7 %all-gather.27.cloned.1.call-start = ((), (), s32[]{:S(2)}) async-start(), calls=%async_computation.13 | async-start | bytes 1914880 | tf_op jit(solution)/shard_map/all_gather | solution.py:151
  (152 other events, 2967.8 us)
Sparse Core Ops, SparseCore 0:
  36.8 90.9 all-reduce.24
  796.0 72.1 reduce-scatter.14
  872.8 89.0 reduce-scatter.16
  965.3 89.7 reduce-scatter.18
  1057.4 190.5 reduce-scatter.24
  1249.4 18.5 all-gather.30
  1269.6 23.5 all-gather.32
  1294.8 22.9 all-gather.28
  1320.0 138.6 reduce-scatter.20
  1460.9 156.4 reduce-scatter.22
  1619.0 21.5 all-gather.26
Sparse Core Ops, SparseCore 1:
  40.5 84.0 all-gather.14
  127.9 69.9 all-gather.20
  200.5 57.9 all-gather.16
  262.3 106.1 all-gather.18
  371.5 71.3 all-gather.22
  445.8 72.9 all-gather.24

commit v2 on v1

v2 whole, which is shorter than its diff:
```python
import functools
import jax
import jax.numpy as jnp
import numpy as np
from jax import lax
from jax.experimental import pallas as pl
from jax.experimental.pallas import tpu as pltpu
from jax.sharding import PartitionSpec as P

HEADS = 16
HEAD = 88
IMGS = 3
CAP = 333
CLIP_TOK = 77
LANES = 128
LOG2E = 1.4426950408889634
eps_norm = 1e-06
masked_score = -1e30
vmem_bytes = 60 * 1024 * 1024


def dot_nt(left, right):
    return lax.dot_general(
        left, right, (((1,), (1,)), ((), ())), preferred_element_type=jnp.float32
    )


def dot_tn(left, right):
    return lax.dot_general(
        left, right, (((0,), (0,)), ((), ())), preferred_element_type=jnp.float32
    )


def matmul(left, right):
    return jnp.dot(left, right, preferred_element_type=jnp.float32)


def widen(value):
    pad = jnp.zeros((value.shape[0], LANES - HEAD), value.dtype)
    return jnp.concatenate([value, pad], axis=1)


def lane_of(shape):
    return lax.broadcasted_iota(jnp.int32, shape, len(shape) - 1)


def head_norm(value):
    mean = jnp.sum(value, axis=1, keepdims=True) * (1.0 / HEAD)
    center = jnp.where(lane_of(value.shape) < HEAD, value - mean, 0.0)
    spread = jnp.sum(center * center, axis=1, keepdims=True) * (1.0 / HEAD)
    factor = lax.rsqrt(spread + eps_norm)
    return center * factor, factor


def turn(value, cos_t, sin_a, sin_b):
    ahead = pltpu.roll(value, LANES - HEAD // 4, 1)
    behind = pltpu.roll(value, HEAD // 4, 1)
    return value * cos_t + ahead * sin_a + behind * sin_b


def turn_back(value, cos_t, sin_a, sin_b):
    return (
        value * cos_t
        + pltpu.roll(value * sin_a, HEAD // 4, 1)
        + pltpu.roll(value * sin_b, LANES - HEAD // 4, 1)
    )


def prep_kernel(heads, pre_ref, cos_ref, sa_ref, sb_ref, seg_ref, gain_ref, bias_ref, out_ref):
    cos_t, sin_a, sin_b = cos_ref[...], sa_ref[...], sb_ref[...]
    seg = seg_ref[...]
    lane = lane_of(cos_t.shape)
    image = lane - HEAD
    own = jnp.where(image == seg, 1.0, 0.0)
    other = jnp.where((image >= 0) & (image < IMGS) & (image != seg), masked_score, 0.0)
    ones = jnp.where(image == 0, 1.0, 0.0)
    for kind in range(3):
        for head in range(heads):
            at = (kind * heads + head) * LANES
            value = pre_ref[:, at : at + LANES]
            if kind < 2:
                normed, _ = head_norm(value)
                value = normed * gain_ref[kind : kind + 1, :] + bias_ref[kind : kind + 1, :]
                value = turn(value, cos_t, sin_a, sin_b) + (own if kind == 0 else other)
            else:
                value = value + ones
            out_ref[:, at : at + LANES] = value.astype(jnp.bfloat16)


def prep_heads(pre, tables, seg, gains, biases, heads, rows):
    count = pre.shape[0]
    cols = 3 * heads * LANES
    wide = pl.BlockSpec((rows, LANES), lambda i: (i, 0))
    return pl.pallas_call(
        functools.partial(prep_kernel, heads),
        grid=(count // rows,),
        in_specs=[
            pl.BlockSpec((rows, pre.shape[1]), lambda i: (i, 0)),
            wide,
            wide,
            wide,
            pl.BlockSpec((rows, 1), lambda i: (i, 0)),
            pl.BlockSpec((2, LANES), lambda i: (0, 0)),
            pl.BlockSpec((2, LANES), lambda i: (0, 0)),
        ],
        out_specs=pl.BlockSpec((rows, cols), lambda i: (i, 0)),
        out_shape=jax.ShapeDtypeStruct((count, cols), jnp.bfloat16),
        compiler_params=pltpu.CompilerParams(vmem_limit_bytes=vmem_bytes),
        cost_estimate=pl.CostEstimate(
            flops=20 * count * cols, bytes_accessed=8 * count * cols, transcendentals=0
        ),
    )(pre, *tables, seg, gains, biases)


score_shift = 10.0


def self_exp(scores):
    return jnp.exp2(scores * (HEAD ** (-0.5) * LOG2E) - score_shift * LOG2E)


def self_forward_kernel(heads, q_ref, k_ref, v_ref, out_ref, inv_ref):
    outs = []
    invs = []
    for head in range(heads):
        cols = slice(head * LANES, (head + 1) * LANES)
        exps = self_exp(dot_nt(k_ref[:, cols], q_ref[:, cols])).astype(jnp.bfloat16)
        total = dot_tn(v_ref[:, cols], exps)
        inverse = 1.0 / total[HEAD : HEAD + 1, :]
        invs.append(inverse)
        outs.append((total * inverse).T[:, :HEAD].astype(jnp.bfloat16))
    out_ref[...] = jnp.concatenate(outs, axis=1)
    for head in range(heads):
        inv_ref[head : head + 1, :] = invs[head]


def self_forward(packed, heads, rows):
    count = packed.shape[0]
    cols = heads * LANES
    return pl.pallas_call(
        functools.partial(self_forward_kernel, heads),
        grid=(count // rows,),
        in_specs=[
            pl.BlockSpec((rows, cols), lambda i: (i, 0)),
            pl.BlockSpec((count, cols), lambda i: (0, 1)),
            pl.BlockSpec((count, cols), lambda i: (0, 2)),
        ],
        out_specs=[
            pl.BlockSpec((rows, heads * HEAD), lambda i: (i, 0)),
            pl.BlockSpec((heads, rows), lambda i: (0, i)),
        ],
        out_shape=[
            jax.ShapeDtypeStruct((count, heads * HEAD), jnp.bfloat16),
            jax.ShapeDtypeStruct((heads, count), jnp.float32),
        ],
        compiler_params=pltpu.CompilerParams(vmem_limit_bytes=vmem_bytes),
        cost_estimate=pl.CostEstimate(
            flops=4 * count * count * cols,
            bytes_accessed=8 * count * cols,
            transcendentals=count * count * heads,
        ),
    )(packed, packed, packed)


def self_backward_kernel(heads, blocks, q_ref, k_ref, v_ref, d_ref, inv_ref, dq_ref, dk_ref, dv_ref, key_sum, value_sum):
    step = pl.program_id(0)

    @pl.when(step == 0)
    def _():
        key_sum[...] = jnp.zeros_like(key_sum)
        value_sum[...] = jnp.zeros_like(value_sum)

    scale = HEAD ** (-0.5)
    for head in range(heads):
        cols = slice(head * LANES, (head + 1) * LANES)
        d_out = widen(d_ref[:, head * HEAD : (head + 1) * HEAD])
        query, key = q_ref[:, cols], k_ref[:, cols]
        probs = self_exp(dot_nt(key, query)) * inv_ref[head : head + 1, :]
        d_probs = dot_nt(v_ref[:, cols], d_out)
        weight = jnp.sum(probs * d_probs, axis=0, keepdims=True)
        d_scores = (probs * (d_probs - weight)).astype(jnp.bfloat16)
        value_sum[:, cols] += matmul(probs.astype(jnp.bfloat16), d_out)
        key_sum[:, cols] += matmul(d_scores, query)
        dq_ref[:, cols] = (dot_tn(d_scores, key) * scale).astype(jnp.bfloat16)

    @pl.when(step == blocks - 1)
    def _():
        dk_ref[...] = (key_sum[...] * scale).astype(jnp.bfloat16)
        dv_ref[...] = value_sum[...].astype(jnp.bfloat16)


def self_backward(packed, d_out, inverse, heads, rows):
    count = packed.shape[0]
    cols = heads * LANES
    blocks = count // rows
    whole = pl.BlockSpec((count, cols), lambda i: (0, 0))
    return pl.pallas_call(
        functools.partial(self_backward_kernel, heads, blocks),
        grid=(blocks,),
        in_specs=[
            pl.BlockSpec((rows, cols), lambda i: (i, 0)),
            pl.BlockSpec((count, cols), lambda i: (0, 1)),
            pl.BlockSpec((count, cols), lambda i: (0, 2)),
            pl.BlockSpec((rows, heads * HEAD), lambda i: (i, 0)),
            pl.BlockSpec((heads, rows), lambda i: (0, i)),
        ],
        out_specs=[pl.BlockSpec((rows, cols), lambda i: (i, 0)), whole, whole],
        out_shape=[jax.ShapeDtypeStruct((count, cols), jnp.bfloat16)] * 3,
        scratch_shapes=[pltpu.VMEM((count, cols), jnp.float32)] * 2,
        compiler_params=pltpu.CompilerParams(vmem_limit_bytes=vmem_bytes),
        cost_estimate=pl.CostEstimate(
            flops=10 * count * count * cols,
            bytes_accessed=14 * count * cols,
            transcendentals=count * count * heads,
        ),
    )(packed, packed, packed, d_out, inverse)


def prep_back_kernel(heads, pre_ref, dq_ref, dk_ref, dv_ref, cos_ref, sa_ref, sb_ref, gain_ref, out_ref, dg_ref, db_ref):
    step = pl.program_id(0)

    @pl.when(step == 0)
    def _():
        dg_ref[...] = jnp.zeros_like(dg_ref)
        db_ref[...] = jnp.zeros_like(db_ref)

    cos_t, sin_a, sin_b = cos_ref[...], sa_ref[...], sb_ref[...]
    live = lane_of(cos_t.shape) < HEAD
    for kind, d_ref in enumerate((dq_ref, dk_ref)):
        gain = gain_ref[kind : kind + 1, :]
        gain_sum = jnp.zeros((1, LANES), jnp.float32)
        bias_sum = jnp.zeros((1, LANES), jnp.float32)
        for head in range(heads):
            at = (kind * heads + head) * LANES
            normed, factor = head_norm(pre_ref[:, at : at + LANES])
            given = jnp.where(live, d_ref[:, head * LANES : (head + 1) * LANES].astype(jnp.float32), 0.0)
            d_normed = turn_back(given, cos_t, sin_a, sin_b)
            gain_sum = gain_sum + jnp.sum(d_normed * normed, axis=0, keepdims=True)
            bias_sum = bias_sum + jnp.sum(d_normed, axis=0, keepdims=True)
            scaled = d_normed * gain
            mean = jnp.sum(scaled, axis=1, keepdims=True) * (1.0 / HEAD)
            slope = jnp.sum(scaled * normed, axis=1, keepdims=True) * (1.0 / HEAD)
            result = jnp.where(live, factor * (scaled - mean - normed * slope), 0.0)
            out_ref[:, at : at + LANES] = result.astype(jnp.bfloat16)
        dg_ref[kind : kind + 1, :] += gain_sum
        db_ref[kind : kind + 1, :] += bias_sum
    out_ref[:, 2 * heads * LANES :] = dv_ref[...]


def prep_back(pre, d_query, d_key, d_value, tables, gains, heads, rows):
    count = pre.shape[0]
    cols = heads * LANES
    wide = pl.BlockSpec((rows, LANES), lambda i: (i, 0))
    headed = pl.BlockSpec((rows, cols), lambda i: (i, 0))
    small = pl.BlockSpec((2, LANES), lambda i: (0, 0))
    return pl.pallas_call(
        functools.partial(prep_back_kernel, heads),
        grid=(count // rows,),
        in_specs=[
            pl.BlockSpec((rows, pre.shape[1]), lambda i: (i, 0)),
            headed,
            headed,
            headed,
            wide,
            wide,
            wide,
            small,
        ],
        out_specs=[pl.BlockSpec((rows, pre.shape[1]), lambda i: (i, 0)), small, small],
        out_shape=[
            jax.ShapeDtypeStruct(pre.shape, jnp.bfloat16),
            jax.ShapeDtypeStruct((2, LANES), jnp.float32),
            jax.ShapeDtypeStruct((2, LANES), jnp.float32),
        ],
        compiler_params=pltpu.CompilerParams(vmem_limit_bytes=vmem_bytes),
        cost_estimate=pl.CostEstimate(
            flops=60 * count * cols, bytes_accessed=30 * count * cols, transcendentals=0
        ),
    )(pre, d_query, d_key, d_value, *tables, gains)


def cross_key(kv_ref, first, head, keys, penalty):
    key = widen(kv_ref[pl.ds(first, keys), head * HEAD : (head + 1) * HEAD])
    return jnp.where(lane_of(key.shape) == HEAD, penalty, key)


def cross_value(kv_ref, first, head, keys, width):
    at = width + head * HEAD
    value = widen(kv_ref[pl.ds(first, keys), at : at + HEAD])
    return jnp.where(lane_of(value.shape) == HEAD, jnp.bfloat16(1), value)


def cross_query(q_ref, head):
    query = widen(q_ref[:, head * HEAD : (head + 1) * HEAD])
    return jnp.where(lane_of(query.shape) == HEAD, jnp.bfloat16(1), query)


cross_factor = HEAD ** (-0.5) * LOG2E


def cross_forward_kernel(heads, keys, span_ref, q_ref, kv_ref, pen_ref, seg_ref, out_ref, top_ref, inv_ref, turned):
    width = heads * HEAD

    def image(index, carry):
        first = pl.multiple_of(index * keys, 16)
        penalty = pen_ref[pl.ds(first, keys), :]
        member = seg_ref[...] == index
        for head in range(heads):
            key = cross_key(kv_ref, first, head, keys, penalty)
            scores = dot_nt(key, cross_query(q_ref, head)) * cross_factor
            top = jnp.max(scores, axis=0, keepdims=True)
            exps = jnp.exp2(scores - top).astype(jnp.bfloat16)
            total = dot_tn(cross_value(kv_ref, first, head, keys, width), exps)
            inverse = 1.0 / total[HEAD : HEAD + 1, :]
            at = slice(head * LANES, (head + 1) * LANES)
            turned[at, :] = jnp.where(member, total * inverse, turned[at, :])
            top_ref[head : head + 1, :] = jnp.where(member, top, top_ref[head : head + 1, :])
            inv_ref[head : head + 1, :] = jnp.where(member, inverse, inv_ref[head : head + 1, :])
        return carry

    lax.fori_loop(span_ref[0], span_ref[1] + 1, image, 0)
    out_ref[...] = jnp.concatenate(
        [
            turned[head * LANES : (head + 1) * LANES, :].T[:, :HEAD].astype(jnp.bfloat16)
            for head in range(heads)
        ],
        axis=1,
    )


def cross_forward(query, text_kv, penalty, seg_row, span):
    count, width = query.shape
    heads = width // HEAD
    keys = text_kv.shape[0] // IMGS
    vmem = pl.BlockSpec(memory_space=pltpu.VMEM)
    return pl.pallas_call(
        functools.partial(cross_forward_kernel, heads, keys),
        in_specs=[pl.BlockSpec(memory_space=pltpu.SMEM)] + [vmem] * 4,
        out_specs=[vmem] * 3,
        out_shape=[
            jax.ShapeDtypeStruct((count, width), jnp.bfloat16),
            jax.ShapeDtypeStruct((heads, count), jnp.float32),
            jax.ShapeDtypeStruct((heads, count), jnp.float32),
        ],
        scratch_shapes=[pltpu.VMEM((heads * LANES, count), jnp.float32)],
        compiler_params=pltpu.CompilerParams(vmem_limit_bytes=vmem_bytes),
        cost_estimate=pl.CostEstimate(
            flops=8 * count * keys * heads * LANES,
            bytes_accessed=2 * text_kv.size + 8 * query.size,
            transcendentals=2 * count * keys * heads,
        ),
    )(span, query, text_kv, penalty, seg_row)


def cross_backward_kernel(heads, keys, span_ref, q_ref, kv_ref, pen_ref, seg_ref, top_ref, inv_ref, d_ref, dq_ref, dkv_ref, turned):
    width = heads * HEAD
    scale = HEAD ** (-0.5)
    turned[...] = jnp.zeros_like(turned)
    dkv_ref[...] = jnp.zeros_like(dkv_ref)

    def image(index, carry):
        first = pl.multiple_of(index * keys, 16)
        penalty = pen_ref[pl.ds(first, keys), :]
        member = seg_ref[...] == index
        d_keys, d_values = [], []
        for head in range(heads):
            key = cross_key(kv_ref, first, head, keys, penalty)
            query = cross_query(q_ref, head)
            d_out = widen(d_ref[:, head * HEAD : (head + 1) * HEAD])
            top = jnp.where(member, top_ref[head : head + 1, :], -masked_score)
            scores = dot_nt(key, query) * cross_factor
            probs = jnp.exp2(scores - top) * inv_ref[head : head + 1, :]
            d_probs = dot_nt(cross_value(kv_ref, first, head, keys, width), d_out)
            weight = jnp.sum(probs * d_probs, axis=0, keepdims=True)
            d_scores = (probs * (d_probs - weight)).astype(jnp.bfloat16)
            d_values.append(matmul(probs.astype(jnp.bfloat16), d_out)[:, :HEAD].astype(jnp.bfloat16))
            d_keys.append((matmul(d_scores, query) * scale)[:, :HEAD].astype(jnp.bfloat16))
            at = slice(head * LANES, (head + 1) * LANES)
            turned[at, :] += dot_tn(key, d_scores)
        dkv_ref[pl.ds(first, keys), :] = jnp.concatenate(d_keys + d_values, axis=1)
        return carry

    lax.fori_loop(span_ref[0], span_ref[1] + 1, image, 0)
    dq_ref[...] = jnp.concatenate(
        [
            (turned[head * LANES : (head + 1) * LANES, :] * scale).T[:, :HEAD].astype(jnp.bfloat16)
            for head in range(heads)
        ],
        axis=1,
    )


def cross_backward(query, text_kv, penalty, seg_row, span, top, inverse, d_out):
    count, width = query.shape
    heads = width // HEAD
    keys = text_kv.shape[0] // IMGS
    vmem = pl.BlockSpec(memory_space=pltpu.VMEM)
    return pl.pallas_call(
        functools.partial(cross_backward_kernel, heads, keys),
        in_specs=[pl.BlockSpec(memory_space=pltpu.SMEM)] + [vmem] * 7,
        out_specs=[vmem] * 2,
        out_shape=[
            jax.ShapeDtypeStruct((count, width), jnp.bfloat16),
            jax.ShapeDtypeStruct(text_kv.shape, jnp.bfloat16),
        ],
        scratch_shapes=[pltpu.VMEM((heads * LANES, count), jnp.float32)],
        compiler_params=pltpu.CompilerParams(vmem_limit_bytes=vmem_bytes),
        cost_estimate=pl.CostEstimate(
            flops=20 * count * keys * heads * LANES,
            bytes_accessed=4 * text_kv.size + 8 * query.size,
            transcendentals=2 * count * keys * heads,
        ),
    )(span, query, text_kv, penalty, seg_row, top, inverse, d_out)


def layer_norm(values, norm_gain, norm_bias):
    center = values - jnp.mean(values, axis=-1, keepdims=True)
    spread = jnp.mean(center * center, axis=-1, keepdims=True)
    return center * lax.rsqrt(spread + eps_norm) * norm_gain + norm_bias


def gelu_tanh(values):
    return (
        0.5
        * values
        * (1.0 + jnp.tanh(0.7978845608028654 * (values + 0.044715 * values * values * values)))
    )


def silu_gate(values):
    return values * jax.nn.sigmoid(values)


def grid_positions(seg_all, widths, first_tok, tok_count):
    images = jnp.arange(IMGS, dtype=jnp.int32)
    starts = jnp.sum((seg_all[None, :] < images[:, None]).astype(jnp.int32), axis=1)
    seg_part = lax.dynamic_slice_in_dim(seg_all, first_tok, tok_count)
    member = seg_part[:, None] == images[None, :]
    start_tok = jnp.sum(jnp.where(member, starts[None, :], 0), axis=1)
    width_tok = jnp.sum(jnp.where(member, widths[None, :], 0), axis=1)
    in_image = first_tok + jnp.arange(tok_count, dtype=jnp.int32) - start_tok
    return (
        seg_part,
        member,
        (in_image // width_tok).astype(jnp.float32),
        (in_image % width_tok).astype(jnp.float32),
    )


def swap(value, axis, mask):
    count = lax.axis_size(axis)
    return lax.ppermute(value, axis, [(rank, rank ^ mask) for rank in range(count)])


def blocks_of(block, axis):
    count = lax.axis_size(axis)
    held = {0: block}
    bit = count // 2
    while bit:
        for mask in list(held):
            held[mask | bit] = swap(held[mask], axis, bit)
        bit //= 2
    return [held[mask] for mask in range(count)]


def sum_parts(parts, axis, kind):
    count = lax.axis_size(axis)
    held = dict(enumerate(parts))
    bit = 1
    while bit < count:
        for mask in [m for m in held if m & bit]:
            came = swap(held.pop(mask).astype(kind), axis, bit)
            held[mask ^ bit] = held[mask ^ bit] + came.astype(jnp.float32)
        bit *= 2
    return held[0]


def gather_small(value, axis):
    bit = 1
    while bit < lax.axis_size(axis):
        value = jnp.concatenate([value, swap(value, axis, bit)])
        bit *= 2
    return value


def scatter_small(value, axis):
    bit = lax.axis_size(axis) // 2
    while bit:
        half = value.shape[0] // 2
        value = value[:half] + swap(value[half:], axis, bit)
        bit //= 2
    return value


def sum_all(value, axis):
    bit = 1
    while bit < lax.axis_size(axis):
        value = value + swap(value, axis, bit)
        bit *= 2
    return value


def exchange(parts, axis):
    return [parts[0]] + [swap(parts[mask], axis, mask) for mask in range(1, len(parts))]


def in_order(blocks, rank):
    stacked = jnp.stack(blocks)
    return [
        lax.dynamic_index_in_dim(stacked, rank ^ place, 0, keepdims=False)
        for place in range(len(blocks))
    ]


def share_of(rows, seq_count):
    if rows >= 16 * seq_count:
        return -(-rows // (16 * seq_count)) * 16
    return -(-rows // seq_count)


def rope_tables(row_pos, col_pos):
    lane = np.arange(LANES)
    half, quarter = HEAD // 2, HEAD // 4
    live = lane < HEAD
    index = lane % half % quarter
    frequency = np.where(live, 10000.0 ** (-(index * 4.0 / HEAD)), 0.0).astype(np.float32)
    front = live & (lane % half < quarter)
    back = live & (lane % half >= quarter)
    angle = jnp.where((lane < half)[None], row_pos[:, None], col_pos[:, None]) * frequency[None]
    sine = jnp.sin(angle)
    return (
        jnp.where(live[None], jnp.cos(angle), 0.0),
        jnp.where(front[None], -sine, 0.0),
        jnp.where(back[None], sine, 0.0),
    )


def caption_penalty(clip_len, t5_len, keys):
    slot = jnp.arange(keys, dtype=jnp.int32)[None]
    clip_live = (slot < CLIP_TOK) & (slot < clip_len[:, None])
    t5_live = (slot >= CLIP_TOK) & (slot < CAP) & (slot - CLIP_TOK < t5_len[:, None])
    return (
        jnp.where(clip_live | t5_live, 0.0, masked_score).astype(jnp.bfloat16).reshape(-1, 1)
    )


def piece_kernel(heads, ranks_ref, *refs):
    out = refs[-1]
    for mask, piece in enumerate(refs[:-1]):

        @pl.when(pl.program_id(0) == mask)
        def _(piece=piece):
            if not heads:
                out[...] = piece[...]
            for head in range(heads):
                out[:, head * LANES : (head + 1) * LANES] = widen(
                    piece[:, head * HEAD : (head + 1) * HEAD]
                )


def place_pieces(pieces, ranks, heads=0):
    count = len(pieces)
    rows, cols = pieces[0].shape
    out_cols = heads * LANES if heads else cols
    return pl.pallas_call(
        functools.partial(piece_kernel, heads),
        grid_spec=pltpu.PrefetchScalarGridSpec(
            num_scalar_prefetch=1,
            grid=(count,),
            in_specs=[pl.BlockSpec((rows, cols), lambda i, ranks: (0, 0))] * count,
            out_specs=pl.BlockSpec((rows, out_cols), lambda i, ranks: (ranks[0] ^ i, 0)),
        ),
        out_shape=jax.ShapeDtypeStruct((count * rows, out_cols), pieces[0].dtype),
        compiler_params=pltpu.CompilerParams(vmem_limit_bytes=vmem_bytes),
        cost_estimate=pl.CostEstimate(
            flops=0, bytes_accessed=4 * count * rows * out_cols, transcendentals=0
        ),
    )(ranks, *pieces)


def pick_kernel(moves, ranks_ref, source, out):
    for place, moved in enumerate(moves):

        @pl.when(ranks_ref[1] == place)
        def _(moved=moved):
            for first, at, size in moved:
                out[:, at : at + size] = source[:, first : first + size]


def pick_columns(weight, ranks, moves):
    cols = sum(size for _, _, size in moves[0])
    vmem = pl.BlockSpec(memory_space=pltpu.VMEM)
    return pl.pallas_call(
        functools.partial(pick_kernel, moves),
        in_specs=[pl.BlockSpec(memory_space=pltpu.SMEM), vmem],
        out_specs=vmem,
        out_shape=jax.ShapeDtypeStruct((weight.shape[0], cols), weight.dtype),
        compiler_params=pltpu.CompilerParams(vmem_limit_bytes=vmem_bytes),
    )(ranks, weight)


def put_kernel(moves, ranks_ref, *refs):
    out = refs[-1]
    for mask, block in enumerate(refs[:-1]):
        for place, moved in enumerate(moves):

            @pl.when((ranks_ref[1] ^ mask) == place)
            def _(block=block, moved=moved):
                for first, at, size in moved:
                    out[:, at : at + size] = block[:, first : first + size].astype(out.dtype)


def put_columns(blocks, ranks, moves, cols, kind):
    vmem = pl.BlockSpec(memory_space=pltpu.VMEM)
    return pl.pallas_call(
        functools.partial(put_kernel, moves),
        in_specs=[pl.BlockSpec(memory_space=pltpu.SMEM)] + [vmem] * len(blocks),
        out_specs=vmem,
        out_shape=jax.ShapeDtypeStruct((blocks[0].shape[0], cols), kind),
        compiler_params=pltpu.CompilerParams(vmem_limit_bytes=vmem_bytes),
    )(ranks, *blocks)


def quarter_kernel(row_counts, shares, ranks_ref, *refs):
    outs = refs[-len(row_counts) :]
    quarters = refs[: -len(row_counts)]
    seq_count = len(quarters) * (quarters[0].shape[1] // sum(shares))
    for mask in range(seq_count):
        quarter = quarters[mask % len(quarters)]
        base = mask // len(quarters) * sum(shares)
        for place in range(seq_count):

            @pl.when((ranks_ref[1] ^ mask) == place)
            def _(quarter=quarter, place=place, base=base):
                first = base
                for out, rows, share in zip(outs, row_counts, shares):
                    size = min(share, rows - place * share)
                    if size > 0:
                        at = place * share
                        out[at : at + size, :] = quarter[0, first : first + size, :]
                    first += share


def place_quarters(quarters, ranks, row_counts, shares):
    dp_count, held, cols = quarters[0].shape
    return pl.pallas_call(
        functools.partial(quarter_kernel, row_counts, shares),
        grid_spec=pltpu.PrefetchScalarGridSpec(
            num_scalar_prefetch=1,
            grid=(dp_count,),
            in_specs=[pl.BlockSpec((1, held, cols), lambda i, ranks: (i, 0, 0))] * len(quarters),
            out_specs=[
                pl.BlockSpec((rows, cols), lambda i, ranks: (ranks[0] ^ i, 0))
                for rows in row_counts
            ],
        ),
        out_shape=[
            jax.ShapeDtypeStruct((dp_count * rows, cols), quarters[0].dtype)
            for rows in row_counts
        ],
        compiler_params=pltpu.CompilerParams(vmem_limit_bytes=vmem_bytes),
        cost_estimate=pl.CostEstimate(
            flops=0, bytes_accessed=4 * dp_count * sum(row_counts) * cols, transcendentals=0
        ),
    )(ranks, *quarters)


def bits_below(count):
    return [1 << place for place in reversed(range(count.bit_length() - 1))]


class Gather:
    def __init__(self, own, stages):
        self.stages = list(stages)
        self.start(own)

    def start(self, own):
        self.axis, bits = self.stages.pop(0)
        self.masks = [0]
        for bit in reversed(bits):
            self.masks += [mask | bit for mask in self.masks]
        self.held, self.came, self.level = {0: own}, None, 0
        self.send()

    def send(self):
        self.level += 1
        masks = [m for m in self.masks if bin(m).count("1") == self.level]
        if masks:
            self.came = {
                m: swap(self.held[m & (m - 1)], self.axis, m & -m)
                for m in sorted(masks, key=lambda m: (m & -m, m), reverse=True)
            }
        elif self.stages:
            self.start(jnp.stack([self.held[m] for m in self.masks]))

    def step(self):
        if self.came is None:
            return
        self.held.update(self.came)
        self.came = None
        self.send()

    def finish(self):
        while self.came is not None:
            self.came = lax.optimization_barrier(self.came)
            self.step()
        return [self.held[m] for m in self.masks]


def own_shares(weights, ranks):
    seq_count = lax.axis_size("seq")
    shares = [share_of(w.shape[0], seq_count) for w in weights]
    return jnp.concatenate(
        [
            lax.dynamic_slice_in_dim(
                jnp.pad(w, ((0, share * seq_count - w.shape[0]), (0, 0))), ranks[1] * share, share
            )
            for w, share in zip(weights, shares)
        ]
    )


def aligned(rows):
    return rows % 16 == 0 and rows >= 16 * lax.axis_size("seq")


def widen_heads(whole, heads):
    return jnp.pad(
        whole.reshape(-1, heads, HEAD), ((0, 0), (0, 0), (0, LANES - HEAD))
    ).reshape(-1, heads * LANES)


def gather_seq(total, rank):
    return in_order(blocks_of(total, "seq"), rank)


class Scatter:
    def __init__(self, grad, ranks, last=0, shared=True):
        dp_count, seq_count = lax.axis_size("dp"), lax.axis_size("seq")
        self.rows = grad.shape[0] // dp_count
        self.ranks = ranks
        low = grad.astype(jnp.bfloat16).reshape(dp_count, self.rows, -1)
        if shared:
            share = share_of(self.rows, seq_count)
            low = jnp.pad(low, ((0, 0), (0, share * seq_count - self.rows), (0, 0)))
            self.held = low.reshape(dp_count, seq_count, share, -1)
        else:
            self.held = low[:, None]
        over_seq, over_dp = [], []
        bit = 1
        while shared and bit < seq_count:
            over_seq.append(("seq", bit, ranks[1], 1))
            bit *= 2
        bit = 1
        while bit < dp_count:
            over_dp.append(("dp", bit, ranks[0], 0))
            bit *= 2
        first = len(over_seq) - last
        self.todo = over_seq[:first] + over_dp + over_seq[first:]
        self.came = None
        self.send()

    def send(self):
        if not self.todo:
            return
        axis, bit, rank, dim = self.todo.pop(0)
        shape = self.held.shape
        split = self.held.reshape(shape[:dim] + (shape[dim] // 2, 2) + shape[dim + 1 :])
        mine = (rank // bit) % 2
        self.held = lax.dynamic_index_in_dim(split, mine, dim + 1, keepdims=False)
        give = lax.dynamic_index_in_dim(split, 1 - mine, dim + 1, keepdims=False)
        self.came = swap(give, axis, bit)

    def step(self):
        if self.came is None:
            return
        total = self.held.astype(jnp.float32) + self.came.astype(jnp.float32)
        self.held, self.came = total.astype(jnp.bfloat16), None
        self.send()

    def total(self):
        while self.came is not None:
            self.step()
        return self.held.reshape(self.held.shape[2:])

    def finish(self):
        blocks = gather_seq(self.total(), self.ranks[1])
        return jnp.concatenate(blocks, axis=0)[: self.rows].astype(jnp.float32)


def advance(value, scatters):
    active = [s for s in scatters if s.came is not None]
    value, came = lax.optimization_barrier((value, [s.came for s in active]))
    for scatter, arrived in zip(active, came):
        scatter.came = arrived
        scatter.step()
    return value


def shards(
    tokens,
    skip,
    segment_ids,
    grid_widths,
    clip_lengths,
    t5_lengths,
    timestep,
    captions,
    ln_gains,
    ln_biases,
    qk_gains,
    qk_biases,
    w_skip,
    w_mod,
    w_qkv,
    w_out,
    w_cq,
    w_ckv,
    w_co,
    w_up,
    w_down,
    cotangent,
):
    local_tok = tokens.shape[0]
    model_width = tokens.shape[1]
    seq_count = lax.axis_size("seq")
    dp_count = lax.axis_size("dp")
    seq_rank = lax.axis_index("seq")
    dp_rank = lax.axis_index("dp")
    ranks = jnp.stack([dp_rank, seq_rank])
    bucket_len = local_tok * seq_count
    local_heads = HEADS // seq_count
    head_cols = local_heads * HEAD
    wide = w_up.shape[1]
    part = wide // (dp_count * seq_count)
    local_wide = part * dp_count
    row_count = w_mod.shape[0]
    skip_rows = w_skip.shape[0]
    order = seq_rank ^ jnp.arange(seq_count, dtype=jnp.int32)
    seq_range = range(seq_count)

    up_moves = [
        [(r * seq_count * part + j * part, r * part, part) for r in range(dp_count)]
        for j in seq_range
    ]
    qkv_moves = [
        [(kind * model_width + j * head_cols, kind * head_cols, head_cols) for kind in range(3)]
        for j in seq_range
    ]
    own_skip = lax.dynamic_slice_in_dim(w_skip, seq_rank * head_cols, head_cols, axis=1)
    dp_bits, seq_bits = bits_below(dp_count), bits_below(seq_count)
    skip_way = Gather(own_skip, [("dp", dp_bits)]) if aligned(skip_rows) else None
    joined = jnp.concatenate([tokens, skip], axis=1).astype(jnp.float32)
    h_float, pull_skip = jax.vjp(
        layer_norm, joined, ln_gains[0:2].reshape(-1), ln_biases[0:2].reshape(-1)
    )
    h_zero = h_float.astype(jnp.bfloat16)
    own_qkv = pick_columns(w_qkv, ranks, qkv_moves)
    own_square = own_shares([w_out, w_cq, w_co], ranks)
    own_ckv = own_shares([w_ckv], ranks)
    first_ways = [] if skip_way is None else [skip_way]
    h_zero, own_qkv, own_square, own_ckv = advance(
        (h_zero, own_qkv, own_square, own_ckv), first_ways
    )
    own_up = pick_columns(w_up, ranks, up_moves)
    h_way = Gather(h_zero, [("seq", seq_bits)])
    ways = []
    if aligned(row_count):
        qkv_way = Gather(own_qkv, [("dp", dp_bits)])
        square_way = Gather(own_square, [("dp", dp_bits), ("seq", seq_bits)])
        ways = [qkv_way, square_way]
    if aligned(w_ckv.shape[0]):
        ckv_way = Gather(
            own_ckv, [("seq", seq_bits[:-1]), ("dp", dp_bits), ("seq", seq_bits[-1:])]
        )
        ways.append(ckv_way)
    pieces = skip_way.finish() if skip_way else []
    pieces, own_up = advance((pieces, own_up), [h_way] + ways)
    if skip_way:
        part_skip = place_pieces(pieces, ranks)
    else:
        part_skip = lax.all_gather(own_skip, "dp", axis=0, tiled=True)
    h_all = jnp.concatenate(h_way.finish(), axis=0)
    x_cols = matmul(h_all, part_skip).astype(jnp.bfloat16).reshape(seq_count, local_tok, head_cols)
    x_one = jnp.concatenate(
        in_order(exchange([x_cols[k] for k in seq_range], "seq"), seq_rank), axis=1
    ).astype(jnp.float32)

    seg_all = segment_ids[0]
    seg_local, member, _, _ = grid_positions(
        seg_all, grid_widths[0], seq_rank * local_tok, local_tok
    )
    _, _, row_all, col_all = grid_positions(seg_all, grid_widths[0], 0, bucket_len)

    def reorder(values):
        return jnp.take(values.reshape(seq_count, local_tok), order, axis=0).reshape(-1)

    tables = rope_tables(reorder(row_all), reorder(col_all))
    seg_column = reorder(seg_all)[:, None]
    lane_pad = ((0, 0), (0, LANES - HEAD))
    head_gains, head_biases = jnp.pad(qk_gains, lane_pad), jnp.pad(qk_biases, lane_pad)

    cond = silu_gate(timestep[0].astype(jnp.float32)).astype(jnp.bfloat16)
    cond_all = gather_small(cond, "dp")
    cond_rows = lax.dynamic_slice_in_dim(cond_all, dp_rank * row_count, row_count, axis=1)
    shifts = scatter_small(matmul(cond_rows, w_mod), "dp")
    time_shift = jnp.sum(jnp.where(member[:, :, None], shifts[None], 0.0), axis=1)

    keys = -(-CAP // 16) * 16
    caption_rows = jnp.pad(
        captions[0].reshape(IMGS, CAP, -1), ((0, 0), (0, keys - CAP), (0, 0))
    ).reshape(IMGS * keys, -1)
    penalty = caption_penalty(clip_lengths[0], t5_lengths[0], keys)
    x_one, tables, seg_column, caption_rows, penalty, time_shift = advance(
        (x_one, tables, seg_column, caption_rows, penalty, time_shift), ways
    )
    n_float, pull_one = jax.vjp(layer_norm, x_one, ln_gains[2], ln_biases[2])
    n_one = (n_float + time_shift).astype(jnp.bfloat16)
    n_one_blocks, own_up, w_down = advance((blocks_of(n_one, "seq"), own_up, w_down), ways)
    part_up = lax.all_gather(own_up, "dp", axis=0, tiled=True)
    own_down = lax.dynamic_slice_in_dim(w_down, seq_rank * part, part)
    part_down = lax.all_gather(own_down, "dp", axis=0, tiled=True)
    if ways:
        part_qkv = place_pieces(qkv_way.finish(), ranks, 3 * local_heads)
    else:
        part_qkv = widen_heads(lax.all_gather(own_qkv, "dp", axis=0, tiled=True), 3 * local_heads)
    n_one_all = jnp.concatenate(n_one_blocks, axis=0)
    qkv_pre = matmul(n_one_all, part_qkv)
    packed = prep_heads(qkv_pre, tables, seg_column, head_gains, head_biases, local_heads, 256)
    head_out, inverse = self_forward(packed, local_heads, 256)
    head_out = advance(head_out, ways)
    out_blocks = head_out.reshape(seq_count, local_tok, head_cols)
    attn_o = jnp.concatenate(
        in_order(exchange([out_blocks[k] for k in seq_range], "seq"), seq_rank), axis=1
    )
    attn_o, part_up = advance((attn_o, part_up), ways)
    if aligned(w_ckv.shape[0]):
        ckv_rows = w_ckv.shape[0]
        quarters = [q.reshape(dp_count, -1, w_ckv.shape[1]) for q in ckv_way.finish()]
        (full_ckv,) = place_quarters(quarters, ranks, [ckv_rows], [share_of(ckv_rows, seq_count)])
    else:
        full_ckv = lax.all_gather(w_ckv, "dp", axis=0, tiled=True)
    if ways:
        full_out, full_cq, full_co = place_quarters(
            square_way.finish(), ranks, [row_count] * 3, [share_of(row_count, seq_count)] * 3
        )
    else:
        full_out, full_cq, full_co = (
            lax.all_gather(w, "dp", axis=0, tiled=True) for w in (w_out, w_cq, w_co)
        )
    x_two = x_one + matmul(attn_o, full_out)
    n3_float, pull_three = jax.vjp(layer_norm, x_two, ln_gains[3], ln_biases[3])
    n_three = n3_float.astype(jnp.bfloat16)
    n_three, cotangent = lax.optimization_barrier((n_three, cotangent))
    cross_q = matmul(n_three, full_cq).astype(jnp.bfloat16)
    text_kv = matmul(caption_rows, full_ckv).astype(jnp.bfloat16)
    seg_row = seg_local[None]
    span = jnp.stack([seg_local[0], seg_local[-1]])
    cross_o, cross_top, cross_inv = cross_forward(cross_q, text_kv, penalty, seg_row, span)
    cross_o, cot_blocks = lax.optimization_barrier((cross_o, blocks_of(cotangent, "seq")))
    x_three = x_two + matmul(cross_o, full_co)
    n2_float, pull_two = jax.vjp(layer_norm, x_three, ln_gains[4], ln_biases[4])
    n_two = n2_float.astype(jnp.bfloat16)
    n_two_blocks, part_skip, part_down = lax.optimization_barrier(
        (blocks_of(n_two, "seq"), part_skip, part_down)
    )
    n_two_all = jnp.concatenate(n_two_blocks, axis=0)
    cot_all = jnp.concatenate(cot_blocks, axis=0)
    skip_blocks = blocks_of(part_skip, "seq")
    up_proj = matmul(n_two_all, part_up)
    act_float, pull_gelu = jax.vjp(gelu_tanh, up_proj)
    act_low = act_float.astype(jnp.bfloat16)
    down_part = matmul(act_low, part_down).astype(jnp.bfloat16)

    grad_down = matmul(act_low.T, cot_all).astype(jnp.bfloat16)
    total_down = lax.psum_scatter(grad_down, "dp", scatter_dimension=0, tiled=True)
    d_act = matmul(cot_all, part_down.T)
    d_up = pull_gelu(d_act)[0].astype(jnp.bfloat16)
    d_two_part = matmul(d_up, part_up.T).astype(jnp.bfloat16)
    d_two_part, skip_blocks = lax.optimization_barrier((d_two_part, skip_blocks))
    d_two_part = d_two_part.reshape(seq_count, local_tok, model_width)
    grad_up = matmul(n_two_all.T, d_up).astype(jnp.bfloat16)
    total_up = lax.psum_scatter(grad_up, "dp", scatter_dimension=0, tiled=True)
    d_n_two = sum_parts([d_two_part[k] for k in seq_range], "seq", jnp.bfloat16)
    d_n_two, down_part = lax.optimization_barrier((d_n_two, down_part))
    down_part = down_part.reshape(seq_count, local_tok, model_width)
    block_out = (
        x_three + sum_parts([down_part[k] for k in seq_range], "seq", jnp.bfloat16)
    ).astype(jnp.bfloat16)
    back_three_x, gain_four, bias_four = pull_two(d_n_two)
    d_x_three = cotangent.astype(jnp.float32) + back_three_x
    d_co = d_x_three.astype(jnp.bfloat16)
    scatters = [Scatter(matmul(cross_o.T, d_co), ranks, 1)]
    d_cross_o = matmul(d_co, full_co.T).astype(jnp.bfloat16)
    d_cross_q, d_text_kv = cross_backward(
        cross_q, text_kv, penalty, seg_row, span, cross_top, cross_inv, d_cross_o
    )
    d_cross_q = advance(d_cross_q, scatters)
    d_n_three = matmul(d_cross_q, full_cq.T)
    back_two_x, gain_three, bias_three = pull_three(d_n_three)
    d_x_two = d_x_three + back_two_x
    d_attn = d_x_two.astype(jnp.bfloat16)
    d_attn_o = matmul(d_attn, full_out.T).astype(jnp.bfloat16)
    d_turned = in_order(jnp.split(d_attn_o, seq_count, axis=1), seq_rank)
    d_heads = jnp.concatenate(exchange(d_turned, "seq"), axis=0)
    scatters += [
        Scatter(matmul(n_three.T, d_cross_q), ranks, 1),
        Scatter(matmul(caption_rows.T, d_text_kv), ranks),
    ]
    d_heads = advance(d_heads, scatters)
    scatters.append(Scatter(matmul(attn_o.T, d_attn), ranks, 1))
    d_query, d_key, d_value = self_backward(packed, d_heads, inverse, local_heads, 256)
    d_query = advance(d_query, scatters)
    d_qkv, gain_qk, bias_qk = prep_back(
        qkv_pre, d_query, d_key, d_value, tables, head_gains, local_heads, 256
    )
    d_one_part = matmul(d_qkv, part_qkv.T).astype(jnp.bfloat16).reshape(seq_count, local_tok, model_width)
    grad_qkv = matmul(n_one_all.T, d_qkv).astype(jnp.bfloat16)
    total_qkv = lax.psum_scatter(grad_qkv, "dp", scatter_dimension=0, tiled=True)
    d_n_one = sum_parts([d_one_part[k] for k in seq_range], "seq", jnp.bfloat16)
    d_n_one = advance(d_n_one, scatters)
    back_one_x, gain_one, bias_one = pull_one(d_n_one)
    d_x_one = d_x_two + back_one_x
    d_y = d_x_one.astype(jnp.bfloat16)
    y_blocks = in_order(jnp.split(d_y, seq_count, axis=1), seq_rank)
    y_cols = jnp.concatenate(exchange(y_blocks, "seq"), axis=0)
    grad_skip_w = matmul(h_all.T, y_cols).astype(jnp.bfloat16)
    down_blocks, up_blocks = blocks_of(total_down, "seq"), blocks_of(total_up, "seq")
    grad_skip_w, d_n_one, y_blocks, down_blocks, up_blocks = advance(
        (grad_skip_w, d_n_one, y_blocks, down_blocks, up_blocks), scatters
    )
    skip_scatter = Scatter(grad_skip_w, ranks, shared=False)

    d_shift = d_n_one.astype(jnp.bfloat16)
    d_image = matmul(member.astype(jnp.bfloat16).T, d_shift)
    d_image_all = gather_small(sum_all(d_image, "seq"), "dp")
    grad_mod = jnp.dot(
        cond_rows.astype(jnp.float32).T,
        d_image_all,
        precision=lax.Precision.HIGHEST,
        preferred_element_type=jnp.float32,
    )
    d_h_zero = sum(dot_nt(y, w) for y, w in zip(y_blocks, skip_blocks))
    moving = scatters + [skip_scatter]
    d_joined, gain_skip, bias_skip = advance(pull_skip(d_h_zero), moving)
    grad_tokens = d_joined[:, :model_width].astype(jnp.bfloat16)
    grad_skip = d_joined[:, model_width:].astype(jnp.bfloat16)
    qk_cols = 4 * HEAD
    small = jnp.concatenate(
        [
            jnp.stack([gain_skip[:model_width], gain_skip[model_width:]]),
            jnp.stack([gain_one, gain_three, gain_four]),
            jnp.stack([bias_skip[:model_width], bias_skip[model_width:]]),
            jnp.stack([bias_one, bias_three, bias_four]),
            jnp.pad(
                jnp.concatenate([gain_qk[:, :HEAD], bias_qk[:, :HEAD]]).reshape(1, qk_cols),
                ((0, 0), (0, model_width - qk_cols)),
            ),
        ]
    )
    small = sum_all(sum_all(small, "seq"), "dp")
    qk_total = small[10, :qk_cols].reshape(4, HEAD)

    grad_down = jnp.concatenate(in_order(down_blocks, seq_rank), axis=0).astype(jnp.float32)
    grad_up = put_columns(
        up_blocks, ranks, [[(at, first, size) for first, at, size in m] for m in up_moves], wide, jnp.float32
    )
    grad_down, grad_up, grad_mod = advance((grad_down, grad_up, grad_mod), moving)
    grad_co, grad_cq, grad_ckv, grad_out = (s.finish() for s in scatters)
    back_moves = [
        [
            (
                (kind * local_heads + head) * LANES,
                kind * model_width + j * head_cols + head * HEAD,
                HEAD,
            )
            for kind in range(3)
            for head in range(local_heads)
        ]
        for j in seq_range
    ]
    grad_qkv = put_columns(
        blocks_of(total_qkv, "seq"), ranks, back_moves, 3 * model_width, jnp.float32
    )
    skip_moves = [[(0, j * head_cols, head_cols)] for j in seq_range]
    grad_w_skip = put_columns(
        blocks_of(skip_scatter.total(), "seq"), ranks, skip_moves, model_width, jnp.float32
    )
    return (
        block_out,
        grad_tokens,
        grad_skip,
        small[0:5],
        small[5:9],
        small[9],
        qk_total[0:2],
        qk_total[2:4],
        grad_w_skip,
        grad_mod,
        grad_qkv,
        grad_out,
        grad_cq,
        grad_ckv,
        grad_co,
        grad_up,
        grad_down,
    )


def solution(mesh):
    in_specs = (
        P(("dp", "seq"), None),
        P(("dp", "seq"), None),
        P("dp", None),
        P("dp", None),
        P("dp", None),
        P("dp", None),
        P("dp", None, None),
        P("dp", None, None),
        P(),
        P(),
        P(),
        P(),
        P("dp", None),
        P("dp", None),
        P("dp", None),
        P("dp", None),
        P("dp", None),
        P("dp", None),
        P("dp", None),
        P("dp", None),
        P("dp", None),
        P(("dp", "seq"), None),
    )
    out_specs = (
        P(("dp", "seq"), None),
        P(("dp", "seq"), None),
        P(("dp", "seq"), None),
        P(),
        P(),
        P(),
        P(),
        P(),
        P("dp", None),
        P("dp", None),
        P("dp", None),
        P("dp", None),
        P("dp", None),
        P("dp", None),
        P("dp", None),
        P("dp", None),
        P("dp", None),
    )
    return jax.shard_map(shards, mesh=mesh, in_specs=in_specs, out_specs=out_specs, check_vma=False)
```

time: 1660 us -> 1140 us (0.69)
  waiting for transfers between devices: 851 us -> 334 us
  Pallas kernels: 0 us -> 168 us
  matrix products: 324 us -> 186 us
  blocking collectives: 134 us -> 0 us
  starting transfers between devices: 23 us -> 154 us
  local copies, waits for them, and re-layouts: 200 us -> 170 us
    reduce_scatter x4 -> x3, waiting for transfers between devices: 335 us -> 0.01 us  [the longest x1 0.01 us: shards(): total_up = lax.psum_scatter(grad_up, 'dp', scatter_dimension=0, tiled=True)]
    unnamed x20 -> x5, waiting for transfers between devices: 191 us -> 0.08 us
    ppermute x24 -> x132, waiting for transfers between devices: 165 us -> 334 us  [swap(): lax.ppermute(value, axis, [(rank, rank ^ mask) for rank in range(count)])]
    pallas_call x0 -> x15, Pallas kernels: none -> 168 us  [the longest x1 37.6 us: self_backward(): pl.pallas_call(functools.partial(self_backward_kernel, heads, blocks), gr...]
    all_gather x9 -> x1, waiting for transfers between devices: 160 us -> 0.01 us  [shards(): part_down = lax.all_gather(own_down, 'dp', axis=0, tiled=True)]
    ppermute x24 -> x132, starting transfers between devices: 21.2 us -> 153 us  [swap(): lax.ppermute(value, axis, [(rank, rank ^ mask) for rank in range(count)])]
    all_gather x4 -> x0, blocking collectives: 95.1 us -> none  [the longest x1 42.2 us: shards(): lax.all_gather(d_image, ('dp', 'seq'), axis=0, tiled=True)]
    dot_general x6 -> x4, matrix products: 82.3 us -> 6.17 us  [dot_nt(): lax.dot_general(left, right, (((1,), (1,)), ((), ())), preferred_element_...]
  transfers between devices with their start and end apart: 41 -> 137, of which waited for: 21 -> 39; matrix products, arithmetic and copies ran while one was open for 25% -> 38% of each run, Pallas kernels for 0% -> 14%
where the time goes in v2:
time: 1140 us; the launch traced here: 1130 us
  waiting for transfers between devices  334 us (29%)
  matrix products  186 us (16%)
  local copies, waits for them, and re-layouts  170 us (15%)
  Pallas kernels  168 us (15%)
  starting transfers between devices  154 us (14%)
  other arithmetic  104 us (9%)
  between operations  16.7 us (1%)
    ppermute x132, waiting for transfers between devices, swap(): lax.ppermute(value, axis, [(rank, rank ^ mask) for rank in range(count)])  334 us
    dot_general x24, matrix products, matmul(): return jnp.dot(left, right, preferred_element_type=jnp.float32)  177 us
    ppermute x132, starting transfers between devices, swap(): lax.ppermute(value, axis, [(rank, rank ^ mask) for rank in range(count)])  153 us
    unnamed x370, local copies, waits for them, and re-layouts  74.8 us
    pallas_call x1, Pallas kernels, self_backward(): pl.pallas_call(functools.partial(self_backward_kernel, heads, blocks), gr...  37.6 us
    convert_element_type x18, other arithmetic, step(): self.held, self.came = (total.astype(jnp.bfloat16), None)  23.9 us
  transfers between devices with their start and end apart: 137, of which 39 were waited for; matrix products, arithmetic and copies ran while one was open for 38% of the time, Pallas kernels for 14%

profile of v2, /device:TPU:1, one launch (start us, length us, event | category | flops | bytes accessed | tf_op | source)
XLA Modules:
  0.0 1131.5 jit_solution(2003608042765374437)
XLA Ops:
  44.8 43.1 %collective-permute-done.15 = bf16[32,2816]{1,0:T(8,128)(2,1)} collective-permute-done((bf16[32,2816]{1,0:T(8,128)(2,1)S(1)}, bf16[32,2816]{1,0:T(8,128)(2,1)}, u32[]{:S(2)}, u32[]{:S(2)}) %collective-permute-start.15) | collective-permute-done | bytes 180256 | tf_op jit(solution)/shard_map/ppermute | solution.py:452
  94.2 13.9 %collective-permute-done.11.refs_4_ = bf16[176,1056]{1,0:T(8,128)(2,1)} collective-permute-done((bf16[176,1056]{1,0:T(8,128)(2,1)}, bf16[176,1056]{1,0:T(8,128)(2,1)}, u32[]{:S(2)}, u32[]{:S(2)}) %collective-permute-start.11) | collective-permute-done | bytes 371744 | tf_op jit(solution)/shard_map/ppermute | solution.py:452
  111.1 16.6 %collective-permute-done.14 = bf16[144,1408]{1,0:T(8,128)(2,1)} collective-permute-done((bf16[144,1408]{1,0:T(8,128)(2,1)S(1)}, bf16[144,1408]{1,0:T(8,128)(2,1)}, u32[]{:S(2)}, u32[]{:S(2)}) %collective-permute-start.14) | collective-permute-done | bytes 405536 | tf_op jit(solution)/shard_map/ppermute | solution.py:452
  165.2 10.1 convolution_convert_fusion.15
  224.6 15.0 %collective-permute-done.36 = bf16[384,1408]{1,0:T(8,128)(2,1)} collective-permute-done((bf16[384,1408]{1,0:T(8,128)(2,1)S(1)}, bf16[384,1408]{1,0:T(8,128)(2,1)}, u32[]{:S(2)}, u32[]{:S(2)}) %collective-permute-start.36) | collective-permute-done | bytes 1081376 | tf_op jit(solution)/shard_map/ppermute | solution.py:452
  258.4 8.7 collective-permute-done.39
  287.0 12.9 %fusion.104.pre_ref = f32[1536,1536]{1,0:T(8,128)} fusion(bf16[1536,1408]{1,0:T(8,128)(2,1)} %constant_dynamic-update-slice_fusion, bf16[1408,1536]{1,0:T(8,128)(2,1)} %shard_map.389), kind=kOutput, calls=%fused_computation.394 | convolution fusion | flops 6643777536 | bytes 18087936 | tf_op jit(solution)/shard_map/dot_general | solution.py:35
  299.8 15.3 %shard_map.390.q_ref.k_ref.v_ref = bf16[1536,1536]{1,0:T(8,128)(2,1)} custom-call(f32[1536,1536]{1,0:T(8,128)} %fusion.104.pre_ref, f32[1536,128]{1,0:T(8,128)} %get-tuple-element.204.cos_ref, f32[1536,128]{1,0:T(8,128)} %get-tuple-element.205.sa_ref, f32[1536,128]{1,0:T(8,128)} %get-tuple-element.206.sb_ref, s32[1536,1]{1,0:T(8,128)} %copy.96.seg_ref, ...), custom_call_target="tpu_custom_call" | custom-call | flops 47185920 | bytes 18874368 | tf_op jit(solution)/shard_map/pallas_call | solution.py:94
  322.2 18.7 %shard_map.391 = (bf16[1536,352]{1,0:T(8,128)(2,1)}, f32[4,1536]{1,0:T(4,128)}) custom-call(bf16[1536,1536]{1,0:T(8,128)(2,1)} %shard_map.390.q_ref.k_ref.v_ref, bf16[1536,1536]{1,0:T(8,128)(2,1)} %shard_map.390.q_ref.k_ref.v_ref, bf16[1536,1536]{1,0:T(8,128)(2,1)} %shard_map.390.q_ref.k_ref.v_ref), custom_call_target="tpu_custom_call" | custom-call | flops 4831838208 | bytes 6291456 | tf_op jit(solution)/shard_map/pallas_call | solution.py:140
  368.0 12.4 %shard_map.392 = (bf16[1408,1408]{1,0:T(8,128)(2,1)}, bf16[1408,1408]{1,0:T(8,128)(2,1)}, bf16[1408,1408]{1,0:T(8,128)(2,1)}) custom-call(s32[2]{0:T(128)} %pad_add_fusion.ranks_ref, bf16[8,144,1408]{2,1,0:T(8,128)(2,1)} %bitcast_dynamic-update-slice_fusion.refs_0_, bf16[8,144,1408]{2,1,0:T(8,128)(2,1)} %collective-permute-done.43.refs_1_, ...), custom_call_target="tpu_custom_call" | custom-call | bytes 23789568 | tf_op jit(solution)/shard_map/pallas_call | solution.py:646
  394.6 8.7 shard_map.393
  413.2 10.4 convolution_convert_fusion.10.kv_ref
  426.6 11.1 shard_map.394
  451.6 23.6 %collective-permute-done.55 = bf16[384,1408]{1,0:T(8,128)(2,1)} collective-permute-done((bf16[384,1408]{1,0:T(8,128)(2,1)}, bf16[384,1408]{1,0:T(8,128)(2,1)}, u32[]{:S(2)}, u32[]{:S(2)}) %collective-permute-start.55) | collective-permute-done | bytes 1081376 | tf_op jit(solution)/shard_map/ppermute | solution.py:452
  496.1 12.0 %fusion.105 = f32[1536,1536]{1,0:T(8,128)} fusion(bf16[1536,1408]{1,0:T(8,128)(2,1)S(1)} %constant_dynamic-update-slice_fusion.4, bf16[1408,1536]{1,0:T(8,128)(2,1)} %all-gather.3.cloned.1.call-done), kind=kOutput, calls=%fused_computation.395 | convolution fusion | flops 6643777536 | bytes 18087936 | tf_op jit(solution)/shard_map/dot_general | solution.py:35
  508.1 21.0 %fusion.3 = bf16[1536,1536]{1,0:T(8,128)(2,1)} fusion(f32[1536,1536]{1,0:T(8,128)} %fusion.105, bf16[1536,1408]{1,0:T(8,128)(2,1)} %constant_dynamic-update-slice_fusion.8, bf16[1536,1408]{1,0:T(8,128)(2,1)S(1)} %bitcast.413), kind=kOutput, calls=%fused_computation.10 | convolution fusion | flops 6700400640 | bytes 22806528 | tf_op jit(solution)/shard_map/dot_general | solution.py:35
  535.1 9.6 convolution_convert_fusion.5
  548.6 8.8 convolution_convert_fusion.1
  560.8 11.9 %convolution_convert_fusion.4 = bf16[1536,1408]{1,0:T(8,128)(2,1)S(1)} fusion(bf16[1536,1408]{1,0:T(8,128)(2,1)} %all-gather.5.cloned.1.call-done, f32[1536,1536]{1,0:T(8,128)} %fusion.105), kind=kOutput, calls=%fused_computation.19 | convolution fusion | flops 6667173888 | bytes 18087936 | tf_op jit(solution)/shard_map/dot_general | solution.py:35
  572.7 12.9 %collective-permute-done.62 = bf16[384,1408]{1,0:T(8,128)(2,1)S(1)} collective-permute-done((bf16[384,1408]{1,0:T(8,128)(2,1)S(1)}, bf16[384,1408]{1,0:T(8,128)(2,1)S(1)}, u32[]{:S(2)}, u32[]{:S(2)}) %collective-permute-start.62) | collective-permute-done | bytes 1081376 | tf_op jit(solution)/shard_map/ppermute | solution.py:452
  597.1 13.6 %convolution_convert_fusion.2 = bf16[1536,1408]{1,0:T(8,128)(2,1)} fusion(bf16[1536,1408]{1,0:T(8,128)(2,1)} %constant_dynamic-update-slice_fusion.8, f32[1536,1536]{1,0:T(8,128)} %fusion.105), kind=kOutput, calls=%fused_computation.17 | convolution fusion | flops 6667173888 | bytes 18087936 | tf_op jit(solution)/shard_map/dot_general | solution.py:35
  638.0 15.7 %shard_map.395 = (bf16[384,1408]{1,0:T(8,128)(2,1)}, bf16[1008,2816]{1,0:T(8,128)(2,1)}) custom-call(s32[2]{0:T(128)} %pad_add_fusion.1.span_ref, bf16[384,1408]{1,0:T(8,128)(2,1)} %convolution_convert_fusion.14.q_ref, bf16[1008,2816]{1,0:T(8,128)(2,1)} %convolution_convert_fusion.10.kv_ref, bf16[1008,1]{1,0:T(8,128)(2,1)} %copy.97.pen_ref, ...), custom_call_target="tpu_custom_call" | custom-call | flops 5284823040 | bytes 15679488 | tf_op jit(solution)/shard_map/pallas_call | solution.py:398
  653.7 9.3 convolution_convert_fusion.9
  736.1 37.6 %shard_map.396 = (bf16[1536,512]{1,0:T(8,128)(2,1)}, bf16[1536,512]{1,0:T(8,128)(2,1)}, bf16[1536,512]{1,0:T(8,128)(2,1)}) custom-call(bf16[1536,1536]{1,0:T(8,128)(2,1)} %shard_map.390.q_ref.k_ref.v_ref, bf16[1536,1536]{1,0:T(8,128)(2,1)} %shard_map.390.q_ref.k_ref.v_ref, bf16[1536,1536]{1,0:T(8,128)(2,1)} %shard_map.390.q_ref.k_ref.v_ref, ...), custom_call_target="tpu_custom_call" | custom-call | flops 12079595520 | bytes 11010048 | tf_op jit(solution)/shard_map/pallas_call | solution.py:197
  773.8 18.5 %shard_map.397 = (bf16[1536,1536]{1,0:T(8,128)(2,1)}, f32[2,128]{1,0:T(2,128)}, f32[2,128]{1,0:T(2,128)}) custom-call(f32[1536,1536]{1,0:T(8,128)} %fusion.104.pre_ref, bf16[1536,512]{1,0:T(8,128)(2,1)} %get-tuple-element.261.dq_ref, bf16[1536,512]{1,0:T(8,128)(2,1)} %get-tuple-element.262.dk_ref, bf16[1536,512]{1,0:T(8,128)(2,1)} %get-tuple-element.263.dv_ref, ...), custom_call_target="tpu_custom_call" | custom-call | flops 47185920 | bytes 23592960 | tf_op jit(solution)/shard_map/pallas_call | solution.py:256
  793.7 11.1 convolution_convert_fusion.3
  811.5 11.4 %convolution_convert_fusion = bf16[1408,1536]{1,0:T(8,128)(2,1)} fusion(bf16[1536,1408]{1,0:T(8,128)(2,1)} %constant_dynamic-update-slice_fusion, bf16[1536,1536]{1,0:T(8,128)(2,1)S(1)} %copy-done.155), kind=kOutput, calls=%fused_computation.15 | convolution fusion | flops 6645940224 | bytes 13369344 | tf_op jit(solution)/shard_map/dot_general | solution.py:35
  841.5 18.2 %collective-permute-done.79 = bf16[384,1408]{1,0:T(8,128)(2,1)} collective-permute-done((bf16[384,1408]{1,0:T(8,128)(2,1)}, bf16[384,1408]{1,0:T(8,128)(2,1)}, u32[]{:S(2)}, u32[]{:S(2)}) %collective-permute-start.79) | collective-permute-done | bytes 1081376 | tf_op jit(solution)/shard_map/ppermute | solution.py:452
  866.0 32.3 %collective-permute-done.81 = bf16[2,2,48,1408]{3,2,1,0:T(8,128)(2,1)S(1)} collective-permute-done((bf16[2,2,48,1408]{3,2,1,0:T(8,128)(2,1)S(1)}, bf16[2,2,48,1408]{3,2,1,0:T(8,128)(2,1)S(1)}, u32[]{:S(2)}, u32[]{:S(2)}) %collective-permute-start.81) | collective-permute-done | bytes 540704 | tf_op jit(solution)/shard_map/ppermute | solution.py:452
  937.7 15.5 %collective-permute-done.95 = bf16[2,1,32,2816]{3,2,0,1:T(8,128)(2,1)S(1)} collective-permute-done((bf16[2,1,32,2816]{3,2,0,1:T(8,128)(2,1)S(1)}, bf16[2,1,32,2816]{3,2,0,1:T(8,128)(2,1)S(1)}, u32[]{:S(2)}, u32[]{:S(2)}) %collective-permute-start.95) | collective-permute-done | bytes 360480 | tf_op jit(solution)/shard_map/ppermute | solution.py:452
  953.1 13.8 %collective-permute-done.96 = bf16[2,2,48,1408]{3,2,1,0:T(8,128)(2,1)S(1)} collective-permute-done((bf16[2,2,48,1408]{3,2,1,0:T(8,128)(2,1)S(1)}, bf16[2,2,48,1408]{3,2,1,0:T(8,128)(2,1)S(1)}, u32[]{:S(2)}, u32[]{:S(2)}) %collective-permute-start.96) | collective-permute-done | bytes 540704 | tf_op jit(solution)/shard_map/ppermute | solution.py:452
  1038.2 10.9 collective-permute-done.99
  (892 shorter events, 610.3 us)
Async XLA Ops:
  7.2 360.8 %all-gather.3.cloned.1.call-start = ((), (), s32[]{:S(2)}) async-start(), calls=%async_computation.3 | async-start | bytes 4866048 | tf_op jit(solution)/shard_map/all_gather | solution.py:920
  33.4 54.7 %collective-permute-start.3 = (bf16[352,352]{1,0:T(8,128)(2,1)}, bf16[352,352]{1,0:T(8,128)(2,1)}, u32[]{:S(2)}, u32[]{:S(2)}) collective-permute-start(bf16[352,352]{1,0:T(8,128)(2,1)} %collective-permute-done.1.refs_2_), channel_id=1, source_target_pairs={{0,4},{4,0},{8,12},{12,8},{16,20},{20,16},{24,28},{28,24},{1,5},{5... | collective-permute-start | bytes 743432 | tf_op jit(solution)/shard_map/ppermute | solution.py:452
  38.9 99.5 %collective-permute-start.8 = (bf16[384,2816]{1,0:T(8,128)(2,1)}, bf16[384,2816]{1,0:T(8,128)(2,1)}, u32[]{:S(2)}, u32[]{:S(2)}) collective-permute-start(bf16[384,2816]{1,0:T(8,128)(2,1)} %fusion.16), channel_id=1, source_target_pairs={{0,2},{1,3},{2,0},{3,1},{4,6},{5,7},{6,4},{7,5},{8,10},{9,11},{10,... | collective-permute-start | bytes 6488072 | tf_op jit(solution)/shard_map/ppermute | solution.py:452
  40.1 98.3 %collective-permute-start.7 = (bf16[384,2816]{1,0:T(8,128)(2,1)}, bf16[384,2816]{1,0:T(8,128)(2,1)}, u32[]{:S(2)}, u32[]{:S(2)}) collective-permute-start(bf16[384,2816]{1,0:T(8,128)(2,1)} %fusion.16), channel_id=1, source_target_pairs={{0,1},{1,0},{2,3},{3,2},{4,5},{5,4},{6,7},{7,6},{8,9},{9,8},{10,11... | collective-permute-start | bytes 6488072 | tf_op jit(solution)/shard_map/ppermute | solution.py:452
  44.2 43.6 %collective-permute-start.15 = (bf16[32,2816]{1,0:T(8,128)(2,1)S(1)}, bf16[32,2816]{1,0:T(8,128)(2,1)}, u32[]{:S(2)}, u32[]{:S(2)}) collective-permute-start(bf16[32,2816]{1,0:T(8,128)(2,1)S(1)} %constant_dynamic-slice_fusion.18), channel_id=1, source_target_pairs={{0,2},{1,3},{2,0},{3,1},{4,6},{5,7},{6,4},{7,5},{8,10},{9,11},{10,... | collective-permute-start | bytes 540680 | tf_op jit(solution)/shard_map/ppermute | solution.py:452
  44.5 48.1 %collective-permute-start.5 = (bf16[352,352]{1,0:T(8,128)(2,1)}, bf16[352,352]{1,0:T(8,128)(2,1)S(1)}, u32[]{:S(2)}, u32[]{:S(2)}) collective-permute-start(bf16[352,352]{1,0:T(8,128)(2,1)} %collective-permute-done.2.refs_4_), channel_id=1, source_target_pairs={{0,8},{4,12},{8,0},{12,4},{16,24},{20,28},{24,16},{28,20},{1,9},{5... | collective-permute-start | bytes 743432 | tf_op jit(solution)/shard_map/ppermute | solution.py:452
  208.8 39.6 %collective-permute-start.42 = (bf16[2,32,2816]{2,1,0:T(8,128)(2,1)}, bf16[2,32,2816]{2,1,0:T(8,128)(2,1)}, u32[]{:S(2)}, u32[]{:S(2)}) collective-permute-start(bf16[2,32,2816]{2,1,0:T(8,128)(2,1)} %collective-permute-done.34), channel_id=1, source_target_pairs={{0,8},{4,12},{8,0},{12,4},{16,24},{20,28},{24,16},{28,20},{1,9},{5... | collective-permute-start | bytes 1081352 | tf_op jit(solution)/shard_map/ppermute | solution.py:452
  209.4 41.0 %collective-permute-start.41 = (bf16[2,32,2816]{2,1,0:T(8,128)(2,1)}, bf16[2,32,2816]{2,1,0:T(8,128)(2,1)}, u32[]{:S(2)}, u32[]{:S(2)}) collective-permute-start(bf16[2,32,2816]{2,1,0:T(8,128)(2,1)} %collective-permute-done.34), channel_id=1, source_target_pairs={{0,4},{4,0},{8,12},{12,8},{16,20},{20,16},{24,28},{28,24},{1,5},{5... | collective-permute-start | bytes 1081352 | tf_op jit(solution)/shard_map/ppermute | solution.py:452
  216.9 50.2 %collective-permute-start.35 = (bf16[384,1408]{1,0:T(8,128)(2,1)S(1)}, bf16[384,1408]{1,0:T(8,128)(2,1)}, u32[]{:S(2)}, u32[]{:S(2)}) collective-permute-start(bf16[384,1408]{1,0:T(8,128)(2,1)S(1)} %add_convert_fusion.8), channel_id=1, source_target_pairs={{0,1},{1,0},{2,3},{3,2},{4,5},{5,4},{6,7},{7,6},{8,9},{9,8},{10,11... | collective-permute-start | bytes 3244040 | tf_op jit(solution)/shard_map/ppermute | solution.py:452
  267.9 73.0 %collective-permute-start.44 = (bf16[8,144,1408]{2,1,0:T(8,128)(2,1)}, bf16[8,144,1408]{2,1,0:T(8,128)(2,1)}, u32[]{:S(2)}, u32[]{:S(2)}) collective-permute-start(bf16[8,144,1408]{2,1,0:T(8,128)(2,1)} %bitcast_dynamic-update-slice_fusion.refs_0_), channel_id=1, source_target_pairs={{0,2},{1,3},{2,0},{3,1},{4,6},{5,7},{6,4},{7,5},{8,10},{9,11},{10,... | collective-permute-start | bytes 9732104 | tf_op jit(solution)/shard_map/ppermute | solution.py:452
  268.8 72.2 %collective-permute-start.43 = (bf16[8,144,1408]{2,1,0:T(8,128)(2,1)}, bf16[8,144,1408]{2,1,0:T(8,128)(2,1)}, u32[]{:S(2)}, u32[]{:S(2)}) collective-permute-start(bf16[8,144,1408]{2,1,0:T(8,128)(2,1)} %bitcast_dynamic-update-slice_fusion.refs_0_), channel_id=1, source_target_pairs={{0,1},{1,0},{2,3},{3,2},{4,5},{5,4},{6,7},{7,6},{8,9},{9,8},{10,11... | collective-permute-start | bytes 9732104 | tf_op jit(solution)/shard_map/ppermute | solution.py:452
  269.9 214.9 %all-gather.5.cloned.1.call-start = ((), (), s32[]{:S(2)}) async-start(), calls=%async_computation.4 | async-start | bytes 4866048 | tf_op jit(solution)/shard_map/all_gather | solution.py:922
  270.3 70.6 %collective-permute-start.45 = (bf16[2,32,2816]{2,1,0:T(8,128)(2,1)}, bf16[2,32,2816]{2,1,0:T(8,128)(2,1)S(1)}, u32[]{:S(2)}, u32[]{:S(2)}) collective-permute-start(bf16[2,32,2816]{2,1,0:T(8,128)(2,1)} %collective-permute-done.42), channel_id=1, source_target_pairs={{0,4},{4,0},{8,12},{12,8},{16,20},{20,16},{24,28},{28,24},{1,5},{5... | collective-permute-start | bytes 1081352 | tf_op jit(solution)/shard_map/ppermute | solution.py:452
  351.0 356.3 %reduce-scatter.6.cloned.1.call-start = ((), (), s32[]{:S(2)}) async-start(), calls=%async_computation.6 | async-start | bytes 4866048 | tf_op jit(solution)/shard_map/reduce_scatter | solution.py:983
  393.4 44.3 %collective-permute-start.51 = (bf16[384,1408]{1,0:T(8,128)(2,1)S(1)}, bf16[384,1408]{1,0:T(8,128)(2,1)}, u32[]{:S(2)}, u32[]{:S(2)}) collective-permute-start(bf16[384,1408]{1,0:T(8,128)(2,1)S(1)} %copy-done.23), channel_id=1, source_target_pairs={{0,1},{1,0},{2,3},{3,2},{4,5},{5,4},{6,7},{7,6},{8,9},{9,8},{10,11... | collective-permute-start | bytes 3244040 | tf_op jit(solution)/shard_map/ppermute | solution.py:452
  489.3 45.0 %collective-permute-start.58 = (bf16[2816,352]{0,1:T(8,128)(2,1)}, bf16[2816,352]{0,1:T(8,128)(2,1)S(1)}, u32[]{:S(2)}, u32[]{:S(2)}) collective-permute-start(bf16[2816,352]{0,1:T(8,128)(2,1)} %copy.98), channel_id=1, source_target_pairs={{0,2},{1,3},{2,0},{3,1},{4,6},{5,7},{6,4},{7,5},{8,10},{9,11},{10,... | collective-permute-start | bytes 5947400 | tf_op jit(solution)/shard_map/ppermute | solution.py:452
  490.0 54.6 %collective-permute-start.57 = (bf16[2816,352]{0,1:T(8,128)(2,1)}, bf16[2816,352]{0,1:T(8,128)(2,1)S(1)}, u32[]{:S(2)}, u32[]{:S(2)}) collective-permute-start(bf16[2816,352]{0,1:T(8,128)(2,1)} %copy.98), channel_id=1, source_target_pairs={{0,1},{1,0},{2,3},{3,2},{4,5},{5,4},{6,7},{7,6},{8,9},{9,8},{10,11... | collective-permute-start | bytes 5947400 | tf_op jit(solution)/shard_map/ppermute | solution.py:452
  557.4 307.5 %reduce-scatter.4.cloned.1.call-start = ((), (), s32[]{:S(2)}) async-start(), calls=%async_computation.5 | async-start | bytes 4866048 | tf_op jit(solution)/shard_map/reduce_scatter | solution.py:976
  610.7 481.5 %reduce-scatter.8.cloned.1.call-start = ((), (), s32[]{:S(2)}) async-start(), calls=%async_computation.7 | async-start | bytes 4866048 | tf_op jit(solution)/shard_map/reduce_scatter | solution.py:1019
  667.0 47.0 %collective-permute-start.72 = (bf16[8,2,32,2816]{3,2,0,1:T(8,128)(2,1)}, bf16[8,2,32,2816]{3,2,0,1:T(8,128)(2,1)}, u32[]{:S(2)}, u32[]{:S(2)}) collective-permute-start(bf16[8,2,32,2816]{3,2,0,1:T(8,128)(2,1)} %bitcast.339), channel_id=1, source_target_pairs={{0,1},{1,0},{2,3},{3,2},{4,5},{5,4},{6,7},{7,6},{8,9},{9,8},{10,11... | collective-permute-start | bytes 8650760 | tf_op jit(solution)/shard_map/ppermute | solution.py:452
  711.4 152.4 %collective-permute-start.91 = (bf16[176,1536]{1,0:T(8,128)(2,1)}, bf16[176,1536]{1,0:T(8,128)(2,1)}, u32[]{:S(2)}, u32[]{:S(2)}) collective-permute-start(bf16[176,1536]{1,0:T(8,128)(2,1)} %reduce-scatter.6.cloned.1.call-done.refs_0_), channel_id=1, source_target_pairs={{0,2},{1,3},{2,0},{3,1},{4,6},{5,7},{6,4},{7,5},{8,10},{9,11},{10,... | collective-permute-start | bytes 1622024 | tf_op jit(solution)/shard_map/ppermute | solution.py:452
  711.8 62.0 %collective-permute-start.76 = (bf16[8,2,48,1408]{3,2,1,0:T(8,128)(2,1)}, bf16[8,2,48,1408]{3,2,1,0:T(8,128)(2,1)}, u32[]{:S(2)}, u32[]{:S(2)}) collective-permute-start(bf16[8,2,48,1408]{3,2,1,0:T(8,128)(2,1)} %dynamic-slice_bitcast_fusion), channel_id=1, source_target_pairs={{0,1},{1,0},{2,3},{3,2},{4,5},{5,4},{6,7},{7,6},{8,9},{9,8},{10,11... | collective-permute-start | bytes 6488072 | tf_op jit(solution)/shard_map/ppermute | solution.py:452
  727.2 46.6 %collective-permute-start.75 = (bf16[8,1,32,2816]{3,2,0,1:T(8,128)(2,1)}, bf16[8,1,32,2816]{3,2,0,1:T(8,128)(2,1)}, u32[]{:S(2)}, u32[]{:S(2)}) collective-permute-start(bf16[8,1,32,2816]{3,2,0,1:T(8,128)(2,1)} %constant_dynamic-slice_fusion.12), channel_id=1, source_target_pairs={{0,2},{1,3},{2,0},{3,1},{4,6},{5,7},{6,4},{7,5},{8,10},{9,11},{10,... | collective-permute-start | bytes 4325384 | tf_op jit(solution)/shard_map/ppermute | solution.py:452
  734.5 39.3 %collective-permute-start.73 = (bf16[2,2,48,1408]{3,2,1,0:T(8,128)(2,1)}, bf16[2,2,48,1408]{3,2,1,0:T(8,128)(2,1)S(1)}, u32[]{:S(2)}, u32[]{:S(2)}) collective-permute-start(bf16[2,2,48,1408]{3,2,1,0:T(8,128)(2,1)} %dynamic-slice_bitcast_fusion.14), channel_id=1, source_target_pairs={{0,8},{4,12},{8,0},{12,4},{16,24},{20,28},{24,16},{28,20},{1,9},{5... | collective-permute-start | bytes 1622024 | tf_op jit(solution)/shard_map/ppermute | solution.py:452
  823.8 75.5 %collective-permute-start.82 = (bf16[4,1,32,2816]{3,2,0,1:T(8,128)(2,1)}, bf16[4,1,32,2816]{3,2,0,1:T(8,128)(2,1)}, u32[]{:S(2)}, u32[]{:S(2)}) collective-permute-start(bf16[4,1,32,2816]{3,2,0,1:T(8,128)(2,1)} %dynamic-slice_bitcast_fusion.6), channel_id=1, source_target_pairs={{0,4},{4,0},{8,12},{12,8},{16,20},{20,16},{24,28},{28,24},{1,5},{5... | collective-permute-start | bytes 2162696 | tf_op jit(solution)/shard_map/ppermute | solution.py:452
  828.6 70.7 %collective-permute-start.83 = (bf16[4,2,48,1408]{3,2,1,0:T(8,128)(2,1)}, bf16[4,2,48,1408]{3,2,1,0:T(8,128)(2,1)}, u32[]{:S(2)}, u32[]{:S(2)}) collective-permute-start(bf16[4,2,48,1408]{3,2,1,0:T(8,128)(2,1)} %dynamic-slice_bitcast_fusion.3), channel_id=1, source_target_pairs={{0,4},{4,0},{8,12},{12,8},{16,20},{20,16},{24,28},{28,24},{1,5},{5... | collective-permute-start | bytes 3244040 | tf_op jit(solution)/shard_map/ppermute | solution.py:452
  863.8 45.2 %collective-permute-start.90 = (bf16[176,1536]{1,0:T(8,128)(2,1)}, bf16[176,1536]{1,0:T(8,128)(2,1)}, u32[]{:S(2)}, u32[]{:S(2)}) collective-permute-start(bf16[176,1536]{1,0:T(8,128)(2,1)} %reduce-scatter.6.cloned.1.call-done.refs_0_), channel_id=1, source_target_pairs={{0,1},{1,0},{2,3},{3,2},{4,5},{5,4},{6,7},{7,6},{8,9},{9,8},{10,11... | collective-permute-start | bytes 1622024 | tf_op jit(solution)/shard_map/ppermute | solution.py:452
  864.9 44.6 %collective-permute-start.88 = (bf16[192,1408]{1,0:T(8,128)(2,1)}, bf16[192,1408]{1,0:T(8,128)(2,1)S(1)}, u32[]{:S(2)}, u32[]{:S(2)}) collective-permute-start(bf16[192,1408]{1,0:T(8,128)(2,1)} %reduce-scatter.4.cloned.1.call-done), channel_id=1, source_target_pairs={{0,2},{1,3},{2,0},{3,1},{4,6},{5,7},{6,4},{7,5},{8,10},{9,11},{10,... | collective-permute-start | bytes 1622024 | tf_op jit(solution)/shard_map/ppermute | solution.py:452
  923.3 43.7 %collective-permute-start.96 = (bf16[2,2,48,1408]{3,2,1,0:T(8,128)(2,1)S(1)}, bf16[2,2,48,1408]{3,2,1,0:T(8,128)(2,1)S(1)}, u32[]{:S(2)}, u32[]{:S(2)}) collective-permute-start(bf16[2,2,48,1408]{3,2,1,0:T(8,128)(2,1)S(1)} %dynamic-slice_bitcast_fusion.12), channel_id=1, source_target_pairs={{0,8},{4,12},{8,0},{12,4},{16,24},{20,28},{24,16},{28,20},{1,9},{5... | collective-permute-start | bytes 1622024 | tf_op jit(solution)/shard_map/ppermute | solution.py:452
  967.6 60.0 %collective-permute-start.130 = (bf16[48,1408]{1,0:T(8,128)(2,1)}, bf16[48,1408]{1,0:T(8,128)(2,1)}, u32[]{:S(2)}, u32[]{:S(2)}) collective-permute-start(bf16[48,1408]{1,0:T(8,128)(2,1)} %get-tuple-element.409), channel_id=1, source_target_pairs={{0,2},{1,3},{2,0},{3,1},{4,6},{5,7},{6,4},{7,5},{8,10},{9,11},{10,... | collective-permute-start | bytes 405512 | tf_op jit(solution)/shard_map/ppermute | solution.py:452
  968.5 64.8 %collective-permute-start.129 = (bf16[48,1408]{1,0:T(8,128)(2,1)}, bf16[48,1408]{1,0:T(8,128)(2,1)}, u32[]{:S(2)}, u32[]{:S(2)}) collective-permute-start(bf16[48,1408]{1,0:T(8,128)(2,1)} %get-tuple-element.409), channel_id=1, source_target_pairs={{0,1},{1,0},{2,3},{3,2},{4,5},{5,4},{6,7},{7,6},{8,9},{9,8},{10,11... | collective-permute-start | bytes 405512 | tf_op jit(solution)/shard_map/ppermute | solution.py:452
  971.4 66.8 %collective-permute-start.97 = (bf16[1,1,48,1408]{3,2,1,0:T(8,128)(2,1)}, bf16[1,1,48,1408]{3,2,1,0:T(8,128)(2,1)}, u32[]{:S(2)}, u32[]{:S(2)}) collective-permute-start(bf16[1,1,48,1408]{3,2,1,0:T(8,128)(2,1)} %constant_dynamic-slice_fusion.8), channel_id=1, source_target_pairs={{0,2},{1,3},{2,0},{3,1},{4,6},{5,7},{6,4},{7,5},{8,10},{9,11},{10,... | collective-permute-start | bytes 405512 | tf_op jit(solution)/shard_map/ppermute | solution.py:452
  (276 other events, 4571.5 us)
Sparse Core Ops, SparseCore 0:
  270.0 73.6 all-gather.2
  351.1 72.7 all-gather.4
  557.5 89.4 reduce-scatter.5
  650.9 111.2 reduce-scatter.3
  835.6 124.4 reduce-scatter.7

commit v3 on v2

--- a/solution.py
+++ b/solution.py
@@ -544,41 +544,9 @@
     )
 
 
-def piece_kernel(heads, ranks_ref, *refs):
-    out = refs[-1]
-    for mask, piece in enumerate(refs[:-1]):
-
-        @pl.when(pl.program_id(0) == mask)
-        def _(piece=piece):
-            if not heads:
-                out[...] = piece[...]
-            for head in range(heads):
-                out[:, head * LANES : (head + 1) * LANES] = widen(
-                    piece[:, head * HEAD : (head + 1) * HEAD]
-                )
-
-
-def place_pieces(pieces, ranks, heads=0):
-    count = len(pieces)
-    rows, cols = pieces[0].shape
-    out_cols = heads * LANES if heads else cols
-    return pl.pallas_call(
-        functools.partial(piece_kernel, heads),
-        grid_spec=pltpu.PrefetchScalarGridSpec(
-            num_scalar_prefetch=1,
-            grid=(count,),
-            in_specs=[pl.BlockSpec((rows, cols), lambda i, ranks: (0, 0))] * count,
-            out_specs=pl.BlockSpec((rows, out_cols), lambda i, ranks: (ranks[0] ^ i, 0)),
-        ),
-        out_shape=jax.ShapeDtypeStruct((count * rows, out_cols), pieces[0].dtype),
-        compiler_params=pltpu.CompilerParams(vmem_limit_bytes=vmem_bytes),
-        cost_estimate=pl.CostEstimate(
-            flops=0, bytes_accessed=4 * count * rows * out_cols, transcendentals=0
-        ),
-    )(ranks, *pieces)
-
-
 def pick_kernel(moves, ranks_ref, source, out):
+    if sum(size for _, _, size in moves[0]) < out.shape[1]:
+        out[...] = jnp.zeros_like(out)
     for place, moved in enumerate(moves):
 
         @pl.when(ranks_ref[1] == place)
@@ -587,8 +555,7 @@
                 out[:, at : at + size] = source[:, first : first + size]
 
 
-def pick_columns(weight, ranks, moves):
-    cols = sum(size for _, _, size in moves[0])
+def pick_columns(weight, ranks, moves, cols):
     vmem = pl.BlockSpec(memory_space=pltpu.VMEM)
     return pl.pallas_call(
         functools.partial(pick_kernel, moves),
@@ -641,8 +608,12 @@
                     first += share
 
 
-def place_quarters(quarters, ranks, row_counts, shares):
+def place_quarters(quarters, ranks, row_counts, shares, bits):
     dp_count, held, cols = quarters[0].shape
+
+    def rank_at(i, ranks):
+        return ranks[0] ^ sum(bit * ((i >> place) & 1) for place, bit in enumerate(bits))
+
     return pl.pallas_call(
         functools.partial(quarter_kernel, row_counts, shares),
         grid_spec=pltpu.PrefetchScalarGridSpec(
@@ -650,7 +621,7 @@
             grid=(dp_count,),
             in_specs=[pl.BlockSpec((1, held, cols), lambda i, ranks: (i, 0, 0))] * len(quarters),
             out_specs=[
-                pl.BlockSpec((rows, cols), lambda i, ranks: (ranks[0] ^ i, 0))
+                pl.BlockSpec((rows, cols), lambda i, ranks: (rank_at(i, ranks), 0))
                 for rows in row_counts
             ],
         ),
@@ -675,14 +646,21 @@
         self.start(own)
 
     def start(self, own):
-        self.axis, bits = self.stages.pop(0)
+        self.axis, bits, self.joined = self.stages.pop(0)
+        self.bits = list(bits)
         self.masks = [0]
         for bit in reversed(bits):
             self.masks += [mask | bit for mask in self.masks]
-        self.held, self.came, self.level = {0: own}, None, 0
+        self.held, self.came, self.level = own[None] if self.joined else {0: own}, None, 0
         self.send()
 
     def send(self):
+        if self.joined:
+            if self.bits:
+                self.came = swap(self.held, self.axis, self.bits.pop(0))
+            elif self.stages:
+                self.start(self.held)
+            return
         self.level += 1
         masks = [m for m in self.masks if bin(m).count("1") == self.level]
         if masks:
@@ -690,13 +668,14 @@
                 m: swap(self.held[m & (m - 1)], self.axis, m & -m)
                 for m in sorted(masks, key=lambda m: (m & -m, m), reverse=True)
             }
-        elif self.stages:
-            self.start(jnp.stack([self.held[m] for m in self.masks]))
 
     def step(self):
         if self.came is None:
             return
-        self.held.update(self.came)
+        if self.joined:
+            self.held = jnp.concatenate([self.held, self.came])
+        else:
+            self.held.update(self.came)
         self.came = None
         self.send()
 
@@ -724,31 +703,83 @@
     return rows % 16 == 0 and rows >= 16 * lax.axis_size("seq")
 
 
-def widen_heads(whole, heads):
-    return jnp.pad(
-        whole.reshape(-1, heads, HEAD), ((0, 0), (0, 0), (0, LANES - HEAD))
-    ).reshape(-1, heads * LANES)
-
-
-def gather_seq(total, rank):
-    return in_order(blocks_of(total, "seq"), rank)
+def split_kernel(ranks_ref, source, *outs):
+    width = outs[0].shape[1]
+    for mask, out in enumerate(outs):
+        for place in range(len(outs)):
+
+            @pl.when((ranks_ref[1] ^ mask) == place)
+            def _(out=out, place=place):
+                out[...] = source[:, place * width : (place + 1) * width]
+
+
+def split_columns(value, ranks):
+    count = lax.axis_size("seq")
+    vmem = pl.BlockSpec(memory_space=pltpu.VMEM)
+    block = jax.ShapeDtypeStruct((value.shape[0], value.shape[1] // count), value.dtype)
+    return pl.pallas_call(
+        split_kernel,
+        in_specs=[pl.BlockSpec(memory_space=pltpu.SMEM), vmem],
+        out_specs=[vmem] * count,
+        out_shape=[block] * count,
+        compiler_params=pltpu.CompilerParams(vmem_limit_bytes=vmem_bytes),
+    )(ranks, value)
+
+
+def join_columns(blocks, ranks, kind):
+    width = blocks[0].shape[1]
+    moves = [[(0, j * width, width)] for j in range(len(blocks))]
+    return put_columns(blocks, ranks, moves, len(blocks) * width, kind)
+
+
+def put_rows_kernel(shares, ranks_ref, *refs):
+    outs = refs[-len(shares) :]
+    blocks = refs[: -len(shares)]
+    for mask, block in enumerate(blocks):
+        for place in range(len(blocks)):
+
+            @pl.when((ranks_ref[1] ^ mask) == place)
+            def _(block=block, place=place):
+                first = 0
+                for out, share in zip(outs, shares):
+                    size = min(share, out.shape[0] - place * share)
+                    width = block.shape[1]
+                    for half in range(out.shape[1] // width):
+                        if size > 0:
+                            out[place * share : place * share + size, half * width : (half + 1) * width] = block[
+                                first : first + size, :
+                            ].astype(out.dtype)
+                        first += share
+
+
+def put_rows(blocks, ranks, shapes, shares):
+    vmem = pl.BlockSpec(memory_space=pltpu.VMEM)
+    return pl.pallas_call(
+        functools.partial(put_rows_kernel, shares),
+        in_specs=[pl.BlockSpec(memory_space=pltpu.SMEM)] + [vmem] * len(blocks),
+        out_specs=[vmem] * len(shapes),
+        out_shape=[jax.ShapeDtypeStruct(shape, jnp.float32) for shape in shapes],
+        compiler_params=pltpu.CompilerParams(vmem_limit_bytes=vmem_bytes),
+    )(ranks, *blocks)
+
+
+def shared_rows(grad, group=1):
+    dp_count, seq_count = lax.axis_size("dp"), lax.axis_size("seq")
+    low = grad.astype(jnp.bfloat16).reshape(dp_count, -1, grad.shape[1])
+    rows = low.shape[1]
+    share = share_of(rows, seq_count)
+    low = jnp.pad(low, ((0, 0), (0, share * seq_count - rows), (0, 0)))
+    low = low.reshape(dp_count, seq_count, share, -1)
+    return jnp.concatenate(jnp.split(low, group, axis=3), axis=2)
 
 
 class Scatter:
-    def __init__(self, grad, ranks, last=0, shared=True):
+    def __init__(self, held, ranks, last=0):
         dp_count, seq_count = lax.axis_size("dp"), lax.axis_size("seq")
-        self.rows = grad.shape[0] // dp_count
-        self.ranks = ranks
-        low = grad.astype(jnp.bfloat16).reshape(dp_count, self.rows, -1)
-        if shared:
-            share = share_of(self.rows, seq_count)
-            low = jnp.pad(low, ((0, 0), (0, share * seq_count - self.rows), (0, 0)))
-            self.held = low.reshape(dp_count, seq_count, share, -1)
-        else:
-            self.held = low[:, None]
+        self.held = held
         over_seq, over_dp = [], []
         bit = 1
-        while shared and bit < seq_count:
+        while bit < seq_count:
             over_seq.append(("seq", bit, ranks[1], 1))
             bit *= 2
         bit = 1
@@ -783,9 +814,72 @@
             self.step()
         return self.held.reshape(self.held.shape[2:])
 
-    def finish(self):
-        blocks = gather_seq(self.total(), self.ranks[1])
-        return jnp.concatenate(blocks, axis=0)[: self.rows].astype(jnp.float32)
+
+def halves_kernel(summed, ranks_ref, *refs):
+    if summed:
+        keep, came, other, other_came, out, give = refs
+        out[...] = (keep[...].astype(jnp.float32) + came[...].astype(jnp.float32)).astype(out.dtype)
+        give[...] = (
+            other[...].astype(jnp.float32) + other_came[...].astype(jnp.float32)
+        ).astype(give.dtype)
+    else:
+        keep, other, out, give = refs
+        out[...] = keep[...]
+        give[...] = other[...]
+
+
+def halves(held, came, ranks, bit):
+    count, rows, cols = held.shape
+
+    def mine(i, ranks):
+        return (2 * i + (ranks[0] // bit) % 2, 0, 0)
+
+    def others(i, ranks):
+        return (2 * i + 1 - (ranks[0] // bit) % 2, 0, 0)
+
+    block = (1, rows, cols)
+    specs = [pl.BlockSpec(block, mine)] * (1 if came is None else 2)
+    specs += [pl.BlockSpec(block, others)] * (1 if came is None else 2)
+    operands = [held] * 2 if came is None else [held, came, held, came]
+    out = jax.ShapeDtypeStruct((count // 2, rows, cols), held.dtype)
+    return pl.pallas_call(
+        functools.partial(halves_kernel, came is not None),
+        grid_spec=pltpu.PrefetchScalarGridSpec(
+            num_scalar_prefetch=1,
+            grid=(count // 2,),
+            in_specs=specs,
+            out_specs=[pl.BlockSpec(block, lambda i, ranks: (i, 0, 0))] * 2,
+        ),
+        out_shape=[out, out],
+        compiler_params=pltpu.CompilerParams(vmem_limit_bytes=vmem_bytes),
+        cost_estimate=pl.CostEstimate(
+            flops=0, bytes_accessed=6 * held.size, transcendentals=0
+        ),
+    )(ranks, *operands)
+
+
+class PartScatter:
+    def __init__(self, grad, ranks):
+        count = lax.axis_size("dp")
+        self.ranks, self.bit = ranks, 1
+        self.held, give = halves(grad.reshape(count, -1, grad.shape[1]), None, ranks, 1)
+        self.came = swap(give, "dp", 1)
+
+    def step(self):
+        if self.came is None:
+            return
+        if self.held.shape[0] > 1:
+            self.bit *= 2
+            self.held, give = halves(self.held, self.came, self.ranks, self.bit)
+            self.came = swap(give, "dp", self.bit)
+        else:
+            total = self.held.astype(jnp.float32) + self.came.astype(jnp.float32)
+            self.held, self.came = total.astype(self.held.dtype), None
+
+    def total(self):
+        while self.came is not None:
+            self.step()
+        return self.held[0]
 
 
 def advance(value, scatters):
@@ -844,47 +938,48 @@
         for j in seq_range
     ]
     qkv_moves = [
-        [(kind * model_width + j * head_cols, kind * head_cols, head_cols) for kind in range(3)]
+        [
+            (
+                kind * model_width + j * head_cols + head * HEAD,
+                (kind * local_heads + head) * LANES,
+                HEAD,
+            )
+            for kind in range(3)
+            for head in range(local_heads)
+        ]
         for j in seq_range
     ]
     own_skip = lax.dynamic_slice_in_dim(w_skip, seq_rank * head_cols, head_cols, axis=1)
+    part_skip = lax.all_gather(own_skip, "dp", axis=0, tiled=True)
+    own_qkv = pick_columns(w_qkv, ranks, qkv_moves, 3 * local_heads * LANES)
+    part_qkv = lax.all_gather(own_qkv, "dp", axis=0, tiled=True)
     dp_bits, seq_bits = bits_below(dp_count), bits_below(seq_count)
-    skip_way = Gather(own_skip, [("dp", dp_bits)]) if aligned(skip_rows) else None
     joined = jnp.concatenate([tokens, skip], axis=1).astype(jnp.float32)
     h_float, pull_skip = jax.vjp(
         layer_norm, joined, ln_gains[0:2].reshape(-1), ln_biases[0:2].reshape(-1)
     )
     h_zero = h_float.astype(jnp.bfloat16)
-    own_qkv = pick_columns(w_qkv, ranks, qkv_moves)
     own_square = own_shares([w_out, w_cq, w_co], ranks)
     own_ckv = own_shares([w_ckv], ranks)
-    first_ways = [] if skip_way is None else [skip_way]
-    h_zero, own_qkv, own_square, own_ckv = advance(
-        (h_zero, own_qkv, own_square, own_ckv), first_ways
-    )
-    own_up = pick_columns(w_up, ranks, up_moves)
-    h_way = Gather(h_zero, [("seq", seq_bits)])
+    own_up = pick_columns(w_up, ranks, up_moves, local_wide)
+    h_zero, own_square, own_ckv, own_qkv = lax.optimization_barrier(
+        (h_zero, own_square, own_ckv, own_qkv)
+    )
+    h_way = Gather(h_zero, [("seq", seq_bits, False)])
     ways = []
     if aligned(row_count):
-        qkv_way = Gather(own_qkv, [("dp", dp_bits)])
-        square_way = Gather(own_square, [("dp", dp_bits), ("seq", seq_bits)])
-        ways = [qkv_way, square_way]
+        square_way = Gather(own_square, [("dp", dp_bits, True), ("seq", seq_bits, False)])
+        ways.append(square_way)
     if aligned(w_ckv.shape[0]):
         ckv_way = Gather(
-            own_ckv, [("seq", seq_bits[:-1]), ("dp", dp_bits), ("seq", seq_bits[-1:])]
+            own_ckv,
+            [("seq", seq_bits[:-1], True), ("dp", dp_bits, True), ("seq", seq_bits[-1:], False)],
         )
         ways.append(ckv_way)
-    pieces = skip_way.finish() if skip_way else []
-    pieces, own_up = advance((pieces, own_up), [h_way] + ways)
-    if skip_way:
-        part_skip = place_pieces(pieces, ranks)
-    else:
-        part_skip = lax.all_gather(own_skip, "dp", axis=0, tiled=True)
+    own_up = advance(own_up, [h_way] + ways)
     h_all = jnp.concatenate(h_way.finish(), axis=0)
     x_cols = matmul(h_all, part_skip).astype(jnp.bfloat16).reshape(seq_count, local_tok, head_cols)
-    x_one = jnp.concatenate(
-        in_order(exchange([x_cols[k] for k in seq_range], "seq"), seq_rank), axis=1
-    ).astype(jnp.float32)
+    x_one = join_columns(exchange([x_cols[k] for k in seq_range], "seq"), ranks, jnp.float32)
 
     seg_all = segment_ids[0]
     seg_local, member, _, _ = grid_positions(
@@ -916,33 +1011,33 @@
     )
     n_float, pull_one = jax.vjp(layer_norm, x_one, ln_gains[2], ln_biases[2])
     n_one = (n_float + time_shift).astype(jnp.bfloat16)
-    n_one_blocks, own_up, w_down = advance((blocks_of(n_one, "seq"), own_up, w_down), ways)
+    n_one_blocks, w_down = advance((blocks_of(n_one, "seq"), w_down), ways)
     part_up = lax.all_gather(own_up, "dp", axis=0, tiled=True)
     own_down = lax.dynamic_slice_in_dim(w_down, seq_rank * part, part)
     part_down = lax.all_gather(own_down, "dp", axis=0, tiled=True)
-    if ways:
-        part_qkv = place_pieces(qkv_way.finish(), ranks, 3 * local_heads)
-    else:
-        part_qkv = widen_heads(lax.all_gather(own_qkv, "dp", axis=0, tiled=True), 3 * local_heads)
     n_one_all = jnp.concatenate(n_one_blocks, axis=0)
     qkv_pre = matmul(n_one_all, part_qkv)
     packed = prep_heads(qkv_pre, tables, seg_column, head_gains, head_biases, local_heads, 256)
     head_out, inverse = self_forward(packed, local_heads, 256)
     head_out = advance(head_out, ways)
     out_blocks = head_out.reshape(seq_count, local_tok, head_cols)
-    attn_o = jnp.concatenate(
-        in_order(exchange([out_blocks[k] for k in seq_range], "seq"), seq_rank), axis=1
-    )
+    attn_o = join_columns(exchange([out_blocks[k] for k in seq_range], "seq"), ranks, jnp.bfloat16)
     attn_o, part_up = advance((attn_o, part_up), ways)
     if aligned(w_ckv.shape[0]):
         ckv_rows = w_ckv.shape[0]
         quarters = [q.reshape(dp_count, -1, w_ckv.shape[1]) for q in ckv_way.finish()]
-        (full_ckv,) = place_quarters(quarters, ranks, [ckv_rows], [share_of(ckv_rows, seq_count)])
+        (full_ckv,) = place_quarters(
+            quarters, ranks, [ckv_rows], [share_of(ckv_rows, seq_count)], dp_bits
+        )
     else:
         full_ckv = lax.all_gather(w_ckv, "dp", axis=0, tiled=True)
-    if ways:
+    if aligned(row_count):
         full_out, full_cq, full_co = place_quarters(
-            square_way.finish(), ranks, [row_count] * 3, [share_of(row_count, seq_count)] * 3
+            square_way.finish(),
+            ranks,
+            [row_count] * 3,
+            [share_of(row_count, seq_count)] * 3,
+            dp_bits,
         )
     else:
         full_out, full_cq, full_co = (
@@ -973,16 +1068,16 @@
     down_part = matmul(act_low, part_down).astype(jnp.bfloat16)
 
     grad_down = matmul(act_low.T, cot_all).astype(jnp.bfloat16)
-    total_down = lax.psum_scatter(grad_down, "dp", scatter_dimension=0, tiled=True)
     d_act = matmul(cot_all, part_down.T)
     d_up = pull_gelu(d_act)[0].astype(jnp.bfloat16)
     d_two_part = matmul(d_up, part_up.T).astype(jnp.bfloat16)
-    d_two_part, skip_blocks = lax.optimization_barrier((d_two_part, skip_blocks))
+    total_down = lax.psum_scatter(grad_down, "dp", scatter_dimension=0, tiled=True)
+    d_two_part, skip_blocks, _ = lax.optimization_barrier((d_two_part, skip_blocks, grad_down))
     d_two_part = d_two_part.reshape(seq_count, local_tok, model_width)
     grad_up = matmul(n_two_all.T, d_up).astype(jnp.bfloat16)
+    d_n_two = sum_parts([d_two_part[k] for k in seq_range], "seq", jnp.bfloat16)
     total_up = lax.psum_scatter(grad_up, "dp", scatter_dimension=0, tiled=True)
-    d_n_two = sum_parts([d_two_part[k] for k in seq_range], "seq", jnp.bfloat16)
-    d_n_two, down_part = lax.optimization_barrier((d_n_two, down_part))
+    d_n_two, down_part, _ = lax.optimization_barrier((d_n_two, down_part, grad_up))
     down_part = down_part.reshape(seq_count, local_tok, model_width)
     block_out = (
         x_three + sum_parts([down_part[k] for k in seq_range], "seq", jnp.bfloat16)
@@ -990,7 +1085,7 @@
     back_three_x, gain_four, bias_four = pull_two(d_n_two)
     d_x_three = cotangent.astype(jnp.float32) + back_three_x
     d_co = d_x_three.astype(jnp.bfloat16)
-    scatters = [Scatter(matmul(cross_o.T, d_co), ranks, 1)]
+    scatters = [Scatter(shared_rows(matmul(cross_o.T, d_co)), ranks, 1)]
     d_cross_o = matmul(d_co, full_co.T).astype(jnp.bfloat16)
     d_cross_q, d_text_kv = cross_backward(
         cross_q, text_kv, penalty, seg_row, span, cross_top, cross_inv, d_cross_o
@@ -1001,14 +1096,18 @@
     d_x_two = d_x_three + back_two_x
     d_attn = d_x_two.astype(jnp.bfloat16)
     d_attn_o = matmul(d_attn, full_out.T).astype(jnp.bfloat16)
-    d_turned = in_order(jnp.split(d_attn_o, seq_count, axis=1), seq_rank)
+    d_turned = split_columns(d_attn_o, ranks)
     d_heads = jnp.concatenate(exchange(d_turned, "seq"), axis=0)
-    scatters += [
-        Scatter(matmul(n_three.T, d_cross_q), ranks, 1),
-        Scatter(matmul(caption_rows.T, d_text_kv), ranks),
-    ]
+    grad_cross = jnp.concatenate(
+        [
+            shared_rows(matmul(n_three.T, d_cross_q)),
+            shared_rows(matmul(caption_rows.T, d_text_kv), 2),
+        ],
+        axis=2,
+    )
+    scatters.append(Scatter(grad_cross, ranks))
     d_heads = advance(d_heads, scatters)
-    scatters.append(Scatter(matmul(attn_o.T, d_attn), ranks, 1))
+    scatters.append(Scatter(shared_rows(matmul(attn_o.T, d_attn)), ranks, 1))
     d_query, d_key, d_value = self_backward(packed, d_heads, inverse, local_heads, 256)
     d_query = advance(d_query, scatters)
     d_qkv, gain_qk, bias_qk = prep_back(
@@ -1022,14 +1121,19 @@
     back_one_x, gain_one, bias_one = pull_one(d_n_one)
     d_x_one = d_x_two + back_one_x
     d_y = d_x_one.astype(jnp.bfloat16)
-    y_blocks = in_order(jnp.split(d_y, seq_count, axis=1), seq_rank)
+    y_blocks = split_columns(d_y, ranks)
     y_cols = jnp.concatenate(exchange(y_blocks, "seq"), axis=0)
     grad_skip_w = matmul(h_all.T, y_cols).astype(jnp.bfloat16)
+    grad_skip_w, d_n_one, y_blocks, total_down, total_up = lax.optimization_barrier(
+        (grad_skip_w, d_n_one, y_blocks, total_down, total_up)
+    )
+    moving = scatters
+    if aligned(skip_rows):
+        skip_scatter = PartScatter(grad_skip_w, ranks)
+        moving = [skip_scatter] + scatters
+    else:
+        total_skip = lax.psum_scatter(grad_skip_w, "dp", scatter_dimension=0, tiled=True)
     down_blocks, up_blocks = blocks_of(total_down, "seq"), blocks_of(total_up, "seq")
-    grad_skip_w, d_n_one, y_blocks, down_blocks, up_blocks = advance(
-        (grad_skip_w, d_n_one, y_blocks, down_blocks, up_blocks), scatters
-    )
-    skip_scatter = Scatter(grad_skip_w, ranks, shared=False)
 
     d_shift = d_n_one.astype(jnp.bfloat16)
     d_image = matmul(member.astype(jnp.bfloat16).T, d_shift)
@@ -1041,7 +1145,7 @@
         preferred_element_type=jnp.float32,
     )
     d_h_zero = sum(dot_nt(y, w) for y, w in zip(y_blocks, skip_blocks))
-    moving = scatters + [skip_scatter]
+    d_h_zero = advance(d_h_zero, moving)
     d_joined, gain_skip, bias_skip = advance(pull_skip(d_h_zero), moving)
     grad_tokens = d_joined[:, :model_width].astype(jnp.bfloat16)
     grad_skip = d_joined[:, model_width:].astype(jnp.bfloat16)
@@ -1061,31 +1165,33 @@
     small = sum_all(sum_all(small, "seq"), "dp")
     qk_total = small[10, :qk_cols].reshape(4, HEAD)
 
-    grad_down = jnp.concatenate(in_order(down_blocks, seq_rank), axis=0).astype(jnp.float32)
+    (grad_down,) = put_rows(down_blocks, ranks, [(seq_count * part, model_width)], [part])
     grad_up = put_columns(
-        up_blocks, ranks, [[(at, first, size) for first, at, size in m] for m in up_moves], wide, jnp.float32
+        up_blocks,
+        ranks,
+        [[(at, first, size) for first, at, size in m] for m in up_moves],
+        wide,
+        jnp.float32,
     )
     grad_down, grad_up, grad_mod = advance((grad_down, grad_up, grad_mod), moving)
-    grad_co, grad_cq, grad_ckv, grad_out = (s.finish() for s in scatters)
-    back_moves = [
-        [
-            (
-                (kind * local_heads + head) * LANES,
-                kind * model_width + j * head_cols + head * HEAD,
-                HEAD,
-            )
-            for kind in range(3)
-            for head in range(local_heads)
-        ]
-        for j in seq_range
-    ]
+    if aligned(skip_rows):
+        total_skip = skip_scatter.total()
+    share, ckv_share = share_of(row_count, seq_count), share_of(w_ckv.shape[0], seq_count)
+    square = (row_count, model_width)
+    grad_co, grad_cq, grad_ckv, grad_out = put_rows(
+        blocks_of(jnp.concatenate([s.total() for s in scatters]), "seq"),
+        ranks,
+        [square, square, w_ckv.shape, square],
+        [share, share, ckv_share, share],
+    )
     grad_qkv = put_columns(
-        blocks_of(total_qkv, "seq"), ranks, back_moves, 3 * model_width, jnp.float32
-    )
-    skip_moves = [[(0, j * head_cols, head_cols)] for j in seq_range]
-    grad_w_skip = put_columns(
-        blocks_of(skip_scatter.total(), "seq"), ranks, skip_moves, model_width, jnp.float32
-    )
+        blocks_of(total_qkv, "seq"),
+        ranks,
+        [[(at, first, size) for first, at, size in m] for m in qkv_moves],
+        3 * model_width,
+        jnp.float32,
+    )
+    grad_w_skip = join_columns(blocks_of(total_skip, "seq"), ranks, jnp.float32)
     return (
         block_out,
         grad_tokens,

time: 1140 us -> 1120 us (0.982)
  local copies, waits for them, and re-layouts: 170 us -> 106 us
  waiting for transfers between devices: 334 us -> 381 us
  starting transfers between devices: 154 us -> 131 us
  Pallas kernels: 168 us -> 186 us
    ppermute x132 -> x96, waiting for transfers between devices: 334 us -> 380 us  [swap(): lax.ppermute(value, axis, [(rank, rank ^ mask) for rank in range(count)])]
    unnamed x370 -> x312, local copies, waits for them, and re-layouts: 74.8 us -> 42.1 us
    ppermute x132 -> x96, starting transfers between devices: 153 us -> 130 us  [swap(): lax.ppermute(value, axis, [(rank, rank ^ mask) for rank in range(count)])]
    concatenate x0 -> x10, other arithmetic: none -> 18.5 us  [the longest x8 17.6 us: step(): self.held = jnp.concatenate([self.held, self.came])]
    pallas_call x2 -> x7, Pallas kernels: 12.7 us -> 24.8 us  [the longest x3 10.6 us: halves(): pl.pallas_call(functools.partial(halves_kernel, came is not None), grid_s...]
    convert_element_type x18 -> x12, other arithmetic: 23.9 us -> 21.2 us  [step(): self.held, self.came = (total.astype(jnp.bfloat16), None)]
  transfers between devices with their start and end apart: 137 -> 103, of which waited for: 39 -> 38; matrix products, arithmetic and copies ran while one was open for 38% -> 32% of each run, Pallas kernels for 14% -> 16%
where the time goes in v3:
time: 1120 us; the launch traced here: 1110 us
  waiting for transfers between devices  381 us (34%)
  matrix products  188 us (17%)
  Pallas kernels  186 us (17%)
  starting transfers between devices  131 us (12%)
  local copies, waits for them, and re-layouts  106 us (9%)
  other arithmetic  103 us (9%)
  between operations  16.4 us (1%)
    ppermute x96, waiting for transfers between devices, swap(): lax.ppermute(value, axis, [(rank, rank ^ mask) for rank in range(count)])  380 us
    dot_general x24, matrix products, matmul(): return jnp.dot(left, right, preferred_element_type=jnp.float32)  174 us
    ppermute x96, starting transfers between devices, swap(): lax.ppermute(value, axis, [(rank, rank ^ mask) for rank in range(count)])  130 us
    unnamed x312, local copies, waits for them, and re-layouts  42.1 us
    pallas_call x1, Pallas kernels, self_backward(): pl.pallas_call(functools.partial(self_backward_kernel, heads, blocks), gr...  37.9 us
  transfers between devices with their start and end apart: 103, of which 38 were waited for; matrix products, arithmetic and copies ran while one was open for 32% of the time, Pallas kernels for 16%

profile of v3, /device:TPU:1, one launch (start us, length us, event | category | flops | bytes accessed | tf_op | source)
XLA Modules:
  0.0 1111.0 jit_solution(13277343583101322227)
XLA Ops:
  43.8 32.2 %collective-permute-done.3 = bf16[1,32,2816]{2,1,0:T(8,128)(2,1)} collective-permute-done((bf16[1,32,2816]{2,1,0:T(8,128)(2,1)S(1)}, bf16[1,32,2816]{2,1,0:T(8,128)(2,1)}, u32[]{:S(2)}, u32[]{:S(2)}) %collective-permute-start.3) | collective-permute-done | bytes 180256 | tf_op jit(solution)/shard_map/ppermute | solution.py:452
  105.8 9.6 convolution_convert_fusion.12
  141.2 16.9 %collective-permute-done.14 = bf16[2,144,1408]{2,1,0:T(8,128)(2,1)} collective-permute-done((bf16[2,144,1408]{2,1,0:T(8,128)(2,1)}, bf16[2,144,1408]{2,1,0:T(8,128)(2,1)}, u32[]{:S(2)}, u32[]{:S(2)}) %collective-permute-start.14) | collective-permute-done | bytes 811040 | tf_op jit(solution)/shard_map/ppermute | solution.py:452
  175.1 12.0 %collective-permute-done.17 = bf16[384,1408]{1,0:T(8,128)(2,1)} collective-permute-done((bf16[384,1408]{1,0:T(8,128)(2,1)}, bf16[384,1408]{1,0:T(8,128)(2,1)}, u32[]{:S(2)}, u32[]{:S(2)}) %collective-permute-start.17) | collective-permute-done | bytes 1081376 | tf_op jit(solution)/shard_map/ppermute | solution.py:452
  195.7 23.6 %collective-permute-done.20 = bf16[2,2,32,2816]{3,2,1,0:T(8,128)(2,1)S(1)} collective-permute-done((bf16[2,2,32,2816]{3,2,1,0:T(8,128)(2,1)}, bf16[2,2,32,2816]{3,2,1,0:T(8,128)(2,1)S(1)}, u32[]{:S(2)}, u32[]{:S(2)}) %collective-permute-start.20) | collective-permute-done | bytes 720928 | tf_op jit(solution)/shard_map/ppermute | solution.py:452
  226.9 9.2 collective-permute-start.23
  245.4 12.9 %fusion.95.pre_ref = f32[1536,1536]{1,0:T(8,128)} fusion(bf16[1536,1408]{1,0:T(8,128)(2,1)} %constant_dynamic-update-slice_fusion, bf16[1408,1536]{1,0:T(8,128)(2,1)} %all-gather.7.cloned.1.call-done), kind=kOutput, calls=%fused_computation.285 | convolution fusion | flops 6643777536 | bytes 18087936 | tf_op jit(solution)/shard_map/dot_general | solution.py:35
  258.3 15.3 %shard_map.389.q_ref.k_ref.v_ref = bf16[1536,1536]{1,0:T(8,128)(2,1)} custom-call(f32[1536,1536]{1,0:T(8,128)} %fusion.95.pre_ref, f32[1536,128]{1,0:T(8,128)} %get-tuple-element.157.cos_ref, f32[1536,128]{1,0:T(8,128)} %get-tuple-element.158.sa_ref, f32[1536,128]{1,0:T(8,128)} %get-tuple-element.159.sb_ref, s32[1536,1]{1,0:T(8,128)} %copy.90.seg_ref, ...), custom_call_target="tpu_custom_call" | custom-call | flops 47185920 | bytes 18874368 | tf_op jit(solution)/shard_map/pallas_call | solution.py:94
  273.6 18.7 %shard_map.390 = (bf16[1536,352]{1,0:T(8,128)(2,1)}, f32[4,1536]{1,0:T(4,128)}) custom-call(bf16[1536,1536]{1,0:T(8,128)(2,1)} %shard_map.389.q_ref.k_ref.v_ref, bf16[1536,1536]{1,0:T(8,128)(2,1)} %shard_map.389.q_ref.k_ref.v_ref, bf16[1536,1536]{1,0:T(8,128)(2,1)} %shard_map.389.q_ref.k_ref.v_ref), custom_call_target="tpu_custom_call" | custom-call | flops 4831838208 | bytes 6291456 | tf_op jit(solution)/shard_map/pallas_call | solution.py:140
  321.5 12.4 %shard_map.392 = (bf16[1408,1408]{1,0:T(8,128)(2,1)}, bf16[1408,1408]{1,0:T(8,128)(2,1)}, bf16[1408,1408]{1,0:T(8,128)(2,1)}) custom-call(s32[2]{0:T(128)} %pad_add_fusion.ranks_ref, bf16[8,144,1408]{2,1,0:T(8,128)(2,1)} %pad_maximum_fusion.2.refs_0_, bf16[8,144,1408]{2,1,0:T(8,128)(2,1)} %collective-permute-done.21.refs_1_, ...), custom_call_target="tpu_custom_call" | custom-call | bytes 23789568 | tf_op jit(solution)/shard_map/pallas_call | solution.py:617
  356.5 9.1 collective-permute-done.30
  366.6 10.5 convolution_convert_fusion.10.kv_ref
  380.0 11.1 %shard_map.394 = (bf16[384,1408]{1,0:T(8,128)(2,1)}, f32[16,384]{1,0:T(8,128)}, f32[16,384]{1,0:T(8,128)}) custom-call(s32[2]{0:T(128)} %pad_add_fusion.1.span_ref, bf16[384,1408]{1,0:T(8,128)(2,1)} %convolution_convert_fusion.15.q_ref, bf16[1008,2816]{1,0:T(8,128)(2,1)} %convolution_convert_fusion.10.kv_ref, bf16[1008,1]{1,0:T(8,128)(2,1)} %copy.91.pen_ref, ...), custom_call_target="tpu_custom_call" | custom-call | flops 2113929216 | bytes 10002432 | tf_op jit(solution)/shard_map/pallas_call | solution.py:336
  404.6 23.8 %collective-permute-done.33 = bf16[384,1408]{1,0:T(8,128)(2,1)} collective-permute-done((bf16[384,1408]{1,0:T(8,128)(2,1)}, bf16[384,1408]{1,0:T(8,128)(2,1)}, u32[]{:S(2)}, u32[]{:S(2)}) %collective-permute-start.33) | collective-permute-done | bytes 1081376 | tf_op jit(solution)/shard_map/ppermute | solution.py:452
  451.4 11.9 %fusion.96 = f32[1536,1536]{1,0:T(8,128)} fusion(bf16[1536,1408]{1,0:T(8,128)(2,1)S(1)} %constant_dynamic-update-slice_fusion.4, bf16[1408,1536]{1,0:T(8,128)(2,1)} %all-gather.9.cloned.1.call-done), kind=kOutput, calls=%fused_computation.286 | convolution fusion | flops 6643777536 | bytes 18087936 | tf_op jit(solution)/shard_map/dot_general | solution.py:35
  463.3 16.9 %fusion.4 = bf16[1536,1536]{1,0:T(8,128)(2,1)S(1)} fusion(f32[1536,1536]{1,0:T(8,128)} %fusion.96, bf16[1536,1408]{1,0:T(8,128)(2,1)} %constant_dynamic-update-slice_fusion.8, bf16[1536,1408]{1,0:T(8,128)(2,1)S(1)} %bitcast.194), kind=kOutput, calls=%fused_computation.13 | convolution fusion | flops 6700400640 | bytes 22806528 | tf_op jit(solution)/shard_map/dot_general | solution.py:35
  489.4 13.9 %convolution_convert_fusion.4 = bf16[1536,1408]{1,0:T(8,128)(2,1)} fusion(bf16[1536,1408]{1,0:T(8,128)(2,1)} %constant_dynamic-update-slice_fusion.8, f32[1536,1536]{1,0:T(8,128)} %fusion.96), kind=kOutput, calls=%fused_computation.22 | convolution fusion | flops 6667173888 | bytes 18087936 | tf_op jit(solution)/shard_map/dot_general | solution.py:35
  506.4 13.3 %convolution_convert_fusion.3 = bf16[1536,1408]{1,0:T(8,128)(2,1)} fusion(bf16[1536,1408]{1,0:T(8,128)(2,1)} %all-gather.11.cloned.1.call-done, f32[1536,1536]{1,0:T(8,128)} %fusion.96), kind=kOutput, calls=%fused_computation.21 | convolution fusion | flops 6667173888 | bytes 18087936 | tf_op jit(solution)/shard_map/dot_general | solution.py:35
  531.1 16.8 %collective-permute-done.40 = bf16[384,1408]{1,0:T(8,128)(2,1)} collective-permute-done((bf16[384,1408]{1,0:T(8,128)(2,1)}, bf16[384,1408]{1,0:T(8,128)(2,1)}, u32[]{:S(2)}, u32[]{:S(2)}) %collective-permute-start.40) | collective-permute-done | bytes 1081376 | tf_op jit(solution)/shard_map/ppermute | solution.py:452
  561.6 22.6 %collective-permute-done.43 = bf16[384,1408]{1,0:T(8,128)(2,1)} collective-permute-done((bf16[384,1408]{1,0:T(8,128)(2,1)}, bf16[384,1408]{1,0:T(8,128)(2,1)}, u32[]{:S(2)}, u32[]{:S(2)}) %collective-permute-start.43) | collective-permute-done | bytes 1081376 | tf_op jit(solution)/shard_map/ppermute | solution.py:452
  599.9 15.3 %shard_map.395 = (bf16[384,1408]{1,0:T(8,128)(2,1)}, bf16[1008,2816]{1,0:T(8,128)(2,1)}) custom-call(s32[2]{0:T(128)} %pad_add_fusion.1.span_ref, bf16[384,1408]{1,0:T(8,128)(2,1)} %convolution_convert_fusion.15.q_ref, bf16[1008,2816]{1,0:T(8,128)(2,1)} %convolution_convert_fusion.10.kv_ref, bf16[1008,1]{1,0:T(8,128)(2,1)} %copy.91.pen_ref, ...), custom_call_target="tpu_custom_call" | custom-call | flops 5284823040 | bytes 15679488 | tf_op jit(solution)/shard_map/pallas_call | solution.py:398
  615.2 9.9 convolution_convert_fusion.9
  705.6 37.9 %shard_map.397 = (bf16[1536,512]{1,0:T(8,128)(2,1)}, bf16[1536,512]{1,0:T(8,128)(2,1)}, bf16[1536,512]{1,0:T(8,128)(2,1)}) custom-call(bf16[1536,1536]{1,0:T(8,128)(2,1)} %shard_map.389.q_ref.k_ref.v_ref, bf16[1536,1536]{1,0:T(8,128)(2,1)} %shard_map.389.q_ref.k_ref.v_ref, bf16[1536,1536]{1,0:T(8,128)(2,1)} %shard_map.389.q_ref.k_ref.v_ref, ...), custom_call_target="tpu_custom_call" | custom-call | flops 12079595520 | bytes 11010048 | tf_op jit(solution)/shard_map/pallas_call | solution.py:197
  751.8 18.0 %shard_map.398 = (bf16[1536,1536]{1,0:T(8,128)(2,1)}, f32[2,128]{1,0:T(2,128)}, f32[2,128]{1,0:T(2,128)}) custom-call(f32[1536,1536]{1,0:T(8,128)} %fusion.95.pre_ref, bf16[1536,512]{1,0:T(8,128)(2,1)} %get-tuple-element.211.dq_ref, bf16[1536,512]{1,0:T(8,128)(2,1)} %get-tuple-element.212.dk_ref, bf16[1536,512]{1,0:T(8,128)(2,1)} %get-tuple-element.213.dv_ref, ...), custom_call_target="tpu_custom_call" | custom-call | flops 47185920 | bytes 23592960 | tf_op jit(solution)/shard_map/pallas_call | solution.py:256
  769.8 10.9 convolution_convert_fusion.1
  784.3 11.2 %convolution_convert_fusion = bf16[1408,1536]{1,0:T(8,128)(2,1)} fusion(bf16[1536,1408]{1,0:T(8,128)(2,1)} %constant_dynamic-update-slice_fusion, bf16[1536,1536]{1,0:T(8,128)(2,1)S(1)} %copy-done.134), kind=kOutput, calls=%fused_computation.18 | convolution fusion | flops 6645940224 | bytes 13369344 | tf_op jit(solution)/shard_map/dot_general | solution.py:35
  810.6 20.1 %collective-permute-done.55 = bf16[384,1408]{1,0:T(8,128)(2,1)} collective-permute-done((bf16[384,1408]{1,0:T(8,128)(2,1)S(1)}, bf16[384,1408]{1,0:T(8,128)(2,1)}, u32[]{:S(2)}, u32[]{:S(2)}) %collective-permute-start.55) | collective-permute-done | bytes 1081376 | tf_op jit(solution)/shard_map/ppermute | solution.py:452
  833.0 35.9 %collective-permute-done.57 = bf16[4,1,112,1408]{3,2,0,1:T(8,128)(2,1)} collective-permute-done((bf16[4,1,112,1408]{3,2,0,1:T(8,128)(2,1)}, bf16[4,1,112,1408]{3,2,0,1:T(8,128)(2,1)}, u32[]{:S(2)}, u32[]{:S(2)}) %collective-permute-start.57) | collective-permute-done | bytes 1261600 | tf_op jit(solution)/shard_map/ppermute | solution.py:452
  920.0 21.3 %collective-permute-done.82 = f32[3,1408]{1,0:T(4,128)S(1)} collective-permute-done((f32[3,1408]{1,0:T(4,128)S(1)}, f32[3,1408]{1,0:T(4,128)S(1)}, u32[]{:S(2)}, u32[]{:S(2)}) %collective-permute-start.82) | collective-permute-done | bytes 16928 | tf_op jit(solution)/shard_map/ppermute | solution.py:452
  1004.7 9.8 collective-permute-done.68
  1028.6 10.7 collective-permute-done.85
  1046.5 21.6 %collective-permute-done.70 = f32[11,1408]{1,0:T(8,128)S(1)} collective-permute-done((f32[11,1408]{1,0:T(8,128)S(1)}, f32[11,1408]{1,0:T(8,128)S(1)}, u32[]{:S(2)}, u32[]{:S(2)}) %collective-permute-start.70) | collective-permute-done | bytes 61984 | tf_op jit(solution)/shard_map/ppermute | solution.py:452
  (733 shorter events, 559.2 us)
Async XLA Ops:
  7.2 98.5 %all-gather.5.cloned.1.call-start = ((), (), s32[]{:S(2)}) async-start(), calls=%async_computation.3 | async-start | bytes 2433024 | tf_op jit(solution)/shard_map/all_gather | solution.py:953
  9.3 236.1 %all-gather.7.cloned.1.call-start = ((), (), s32[]{:S(2)}) async-start(), calls=%async_computation.4 | async-start | bytes 4866048 | tf_op jit(solution)/shard_map/all_gather | solution.py:955
  21.7 54.3 %collective-permute-start = (bf16[384,2816]{1,0:T(8,128)(2,1)}, bf16[384,2816]{1,0:T(8,128)(2,1)}, u32[]{:S(2)}, u32[]{:S(2)}) collective-permute-start(bf16[384,2816]{1,0:T(8,128)(2,1)} %fusion.16), channel_id=1, source_target_pairs={{0,1},{1,0},{2,3},{3,2},{4,5},{5,4},{6,7},{7,6},{8,9},{9,8},{10,11... | collective-permute-start | bytes 6488072 | tf_op jit(solution)/shard_map/ppermute | solution.py:452
  21.7 54.3 %collective-permute-start.1 = (bf16[384,2816]{1,0:T(8,128)(2,1)}, bf16[384,2816]{1,0:T(8,128)(2,1)}, u32[]{:S(2)}, u32[]{:S(2)}) collective-permute-start(bf16[384,2816]{1,0:T(8,128)(2,1)} %fusion.16), channel_id=1, source_target_pairs={{0,2},{1,3},{2,0},{3,1},{4,6},{5,7},{6,4},{7,5},{8,10},{9,11},{10,... | collective-permute-start | bytes 6488072 | tf_op jit(solution)/shard_map/ppermute | solution.py:452
  24.4 51.5 %collective-permute-start.2 = (bf16[1,144,1408]{2,1,0:T(8,128)(2,1)}, bf16[1,144,1408]{2,1,0:T(8,128)(2,1)S(1)}, u32[]{:S(2)}, u32[]{:S(2)}) collective-permute-start(bf16[1,144,1408]{2,1,0:T(8,128)(2,1)} %bitcast.2), channel_id=1, source_target_pairs={{0,16},{4,20},{8,24},{12,28},{16,0},{20,4},{24,8},{28,12},{1,17},{... | collective-permute-start | bytes 1216520 | tf_op jit(solution)/shard_map/ppermute | solution.py:452
  26.8 49.2 %collective-permute-start.3 = (bf16[1,32,2816]{2,1,0:T(8,128)(2,1)S(1)}, bf16[1,32,2816]{2,1,0:T(8,128)(2,1)}, u32[]{:S(2)}, u32[]{:S(2)}) collective-permute-start(bf16[1,32,2816]{2,1,0:T(8,128)(2,1)S(1)} %bitcast.181), channel_id=1, source_target_pairs={{0,2},{1,3},{2,0},{3,1},{4,6},{5,7},{6,4},{7,5},{8,10},{9,11},{10,... | collective-permute-start | bytes 540680 | tf_op jit(solution)/shard_map/ppermute | solution.py:452
  28.2 293.2 %all-gather.9.cloned.1.call-start = ((), (), s32[]{:S(2)}) async-start(), calls=%async_computation.5 | async-start | bytes 4866048 | tf_op jit(solution)/shard_map/all_gather | solution.py:1015
  99.6 58.6 %collective-permute-start.14 = (bf16[2,144,1408]{2,1,0:T(8,128)(2,1)}, bf16[2,144,1408]{2,1,0:T(8,128)(2,1)}, u32[]{:S(2)}, u32[]{:S(2)}) collective-permute-start(bf16[2,144,1408]{2,1,0:T(8,128)(2,1)} %pad_maximum_fusion.11), channel_id=1, source_target_pairs={{0,8},{4,12},{8,0},{12,4},{16,24},{20,28},{24,16},{28,20},{1,9},{5... | collective-permute-start | bytes 2433032 | tf_op jit(solution)/shard_map/ppermute | solution.py:452
  168.1 51.1 %collective-permute-start.19 = (bf16[4,144,1408]{2,1,0:T(8,128)(2,1)}, bf16[4,144,1408]{2,1,0:T(8,128)(2,1)}, u32[]{:S(2)}, u32[]{:S(2)}) collective-permute-start(bf16[4,144,1408]{2,1,0:T(8,128)(2,1)} %pad_maximum_fusion.6), channel_id=1, source_target_pairs={{0,4},{4,0},{8,12},{12,8},{16,20},{20,16},{24,28},{28,24},{1,5},{5... | collective-permute-start | bytes 4866056 | tf_op jit(solution)/shard_map/ppermute | solution.py:452
  172.4 46.8 %collective-permute-start.16 = (bf16[384,1408]{1,0:T(8,128)(2,1)}, bf16[384,1408]{1,0:T(8,128)(2,1)}, u32[]{:S(2)}, u32[]{:S(2)}) collective-permute-start(bf16[384,1408]{1,0:T(8,128)(2,1)} %add_convert_fusion.8), channel_id=1, source_target_pairs={{0,1},{1,0},{2,3},{3,2},{4,5},{5,4},{6,7},{7,6},{8,9},{9,8},{10,11... | collective-permute-start | bytes 3244040 | tf_op jit(solution)/shard_map/ppermute | solution.py:452
  194.2 243.5 %all-gather.11.cloned.1.call-start = ((), (), s32[]{:S(2)}) async-start(), calls=%async_computation.6 | async-start | bytes 4866048 | tf_op jit(solution)/shard_map/all_gather | solution.py:1017
  222.8 69.6 %collective-permute-start.21 = (bf16[8,144,1408]{2,1,0:T(8,128)(2,1)}, bf16[8,144,1408]{2,1,0:T(8,128)(2,1)}, u32[]{:S(2)}, u32[]{:S(2)}) collective-permute-start(bf16[8,144,1408]{2,1,0:T(8,128)(2,1)} %pad_maximum_fusion.2.refs_0_), channel_id=1, source_target_pairs={{0,1},{1,0},{2,3},{3,2},{4,5},{5,4},{6,7},{7,6},{8,9},{9,8},{10,11... | collective-permute-start | bytes 9732104 | tf_op jit(solution)/shard_map/ppermute | solution.py:452
  225.7 72.2 %collective-permute-start.22 = (bf16[8,144,1408]{2,1,0:T(8,128)(2,1)}, bf16[8,144,1408]{2,1,0:T(8,128)(2,1)}, u32[]{:S(2)}, u32[]{:S(2)}) collective-permute-start(bf16[8,144,1408]{2,1,0:T(8,128)(2,1)} %pad_maximum_fusion.2.refs_0_), channel_id=1, source_target_pairs={{0,2},{1,3},{2,0},{3,1},{4,6},{5,7},{6,4},{7,5},{8,10},{9,11},{10,... | collective-permute-start | bytes 9732104 | tf_op jit(solution)/shard_map/ppermute | solution.py:452
  226.9 65.4 %collective-permute-start.23 = (bf16[4,2,32,2816]{3,2,1,0:T(8,128)(2,1)}, bf16[4,2,32,2816]{3,2,1,0:T(8,128)(2,1)}, u32[]{:S(2)}, u32[]{:S(2)}) collective-permute-start(bf16[4,2,32,2816]{3,2,1,0:T(8,128)(2,1)} %pad_maximum_fusion.9), channel_id=1, source_target_pairs={{0,4},{4,0},{8,12},{12,8},{16,20},{20,16},{24,28},{28,24},{1,5},{5... | collective-permute-start | bytes 4325384 | tf_op jit(solution)/shard_map/ppermute | solution.py:452
  305.5 597.5 %reduce-scatter.6.cloned.1.call-start = ((), (), s32[]{:S(2)}) async-start(), calls=%async_computation.8 | async-start | bytes 4866048 | tf_op jit(solution)/shard_map/reduce_scatter | solution.py:1079
  347.2 44.0 %collective-permute-start.29 = (bf16[384,1408]{1,0:T(8,128)(2,1)S(1)}, bf16[384,1408]{1,0:T(8,128)(2,1)}, u32[]{:S(2)}, u32[]{:S(2)}) collective-permute-start(bf16[384,1408]{1,0:T(8,128)(2,1)S(1)} %copy-done.22), channel_id=1, source_target_pairs={{0,1},{1,0},{2,3},{3,2},{4,5},{5,4},{6,7},{7,6},{8,9},{9,8},{10,11... | collective-permute-start | bytes 3244040 | tf_op jit(solution)/shard_map/ppermute | solution.py:452
  442.0 47.2 %collective-permute-start.36 = (bf16[2816,352]{0,1:T(8,128)(2,1)}, bf16[2816,352]{0,1:T(8,128)(2,1)}, u32[]{:S(2)}, u32[]{:S(2)}) collective-permute-start(bf16[2816,352]{0,1:T(8,128)(2,1)} %copy.92), channel_id=1, source_target_pairs={{0,2},{1,3},{2,0},{3,1},{4,6},{5,7},{6,4},{7,5},{8,10},{9,11},{10,... | collective-permute-start | bytes 5947400 | tf_op jit(solution)/shard_map/ppermute | solution.py:452
  443.4 59.9 %collective-permute-start.35 = (bf16[2816,352]{0,1:T(8,128)(2,1)}, bf16[2816,352]{0,1:T(8,128)(2,1)}, u32[]{:S(2)}, u32[]{:S(2)}) collective-permute-start(bf16[2816,352]{0,1:T(8,128)(2,1)} %copy.92), channel_id=1, source_target_pairs={{0,1},{1,0},{2,3},{3,2},{4,5},{5,4},{6,7},{7,6},{8,9},{9,8},{10,11... | collective-permute-start | bytes 5947400 | tf_op jit(solution)/shard_map/ppermute | solution.py:452
  558.9 344.1 %reduce-scatter.4.cloned.1.call-start = ((), (), s32[]{:S(2)}) async-start(), calls=%async_computation.7 | async-start | bytes 4866048 | tf_op jit(solution)/shard_map/reduce_scatter | solution.py:1074
  635.5 51.4 %collective-permute-start.49 = (bf16[8,2,112,1408]{3,2,1,0:T(8,128)(2,1)}, bf16[8,2,112,1408]{3,2,1,0:T(8,128)(2,1)}, u32[]{:S(2)}, u32[]{:S(2)}) collective-permute-start(bf16[8,2,112,1408]{3,2,1,0:T(8,128)(2,1)} %dynamic-slice_bitcast_fusion), channel_id=1, source_target_pairs={{0,1},{1,0},{2,3},{3,2},{4,5},{5,4},{6,7},{7,6},{8,9},{9,8},{10,11... | collective-permute-start | bytes 15138824 | tf_op jit(solution)/shard_map/ppermute | solution.py:452
  695.1 56.6 %collective-permute-start.51 = (bf16[8,1,112,1408]{3,2,1,0:T(8,128)(2,1)}, bf16[8,1,112,1408]{3,2,1,0:T(8,128)(2,1)}, u32[]{:S(2)}, u32[]{:S(2)}) collective-permute-start(bf16[8,1,112,1408]{3,2,1,0:T(8,128)(2,1)} %constant_dynamic-slice_fusion.5), channel_id=1, source_target_pairs={{0,2},{1,3},{2,0},{3,1},{4,6},{5,7},{6,4},{7,5},{8,10},{9,11},{10,... | collective-permute-start | bytes 7569416 | tf_op jit(solution)/shard_map/ppermute | solution.py:452
  701.8 41.8 %collective-permute-start.52 = (bf16[8,2,48,1408]{3,2,1,0:T(8,128)(2,1)}, bf16[8,2,48,1408]{3,2,1,0:T(8,128)(2,1)}, u32[]{:S(2)}, u32[]{:S(2)}) collective-permute-start(bf16[8,2,48,1408]{3,2,1,0:T(8,128)(2,1)} %dynamic-slice_bitcast_fusion.1), channel_id=1, source_target_pairs={{0,1},{1,0},{2,3},{3,2},{4,5},{5,4},{6,7},{7,6},{8,9},{9,8},{10,11... | collective-permute-start | bytes 6488072 | tf_op jit(solution)/shard_map/ppermute | solution.py:452
  702.4 339.5 %reduce-scatter.8.cloned.1.call-start = ((), (), s32[]{:S(2)}) async-start(), calls=%async_computation.9 | async-start | bytes 4866048 | tf_op jit(solution)/shard_map/reduce_scatter | solution.py:1118
  808.0 60.9 %collective-permute-start.57 = (bf16[4,1,112,1408]{3,2,0,1:T(8,128)(2,1)}, bf16[4,1,112,1408]{3,2,0,1:T(8,128)(2,1)}, u32[]{:S(2)}, u32[]{:S(2)}) collective-permute-start(bf16[4,1,112,1408]{3,2,0,1:T(8,128)(2,1)} %dynamic-slice_bitcast_fusion.3), channel_id=1, source_target_pairs={{0,4},{4,0},{8,12},{12,8},{16,20},{20,16},{24,28},{28,24},{1,5},{5... | collective-permute-start | bytes 3784712 | tf_op jit(solution)/shard_map/ppermute | solution.py:452
  872.3 84.9 %collective-permute-start.65 = (bf16[2,2,48,1408]{3,2,1,0:T(8,128)(2,1)}, bf16[2,2,48,1408]{3,2,1,0:T(8,128)(2,1)}, u32[]{:S(2)}, u32[]{:S(2)}) collective-permute-start(bf16[2,2,48,1408]{3,2,1,0:T(8,128)(2,1)} %dynamic-slice_bitcast_fusion.7), channel_id=1, source_target_pairs={{0,8},{4,12},{8,0},{12,4},{16,24},{20,28},{24,16},{28,20},{1,9},{5... | collective-permute-start | bytes 1622024 | tf_op jit(solution)/shard_map/ppermute | solution.py:452
  884.5 76.0 %collective-permute-start.64 = (bf16[2,1,112,1408]{3,2,1,0:T(8,128)(2,1)}, bf16[2,1,112,1408]{3,2,1,0:T(8,128)(2,1)}, u32[]{:S(2)}, u32[]{:S(2)}) collective-permute-start(bf16[2,1,112,1408]{3,2,1,0:T(8,128)(2,1)} %dynamic-slice_bitcast_fusion.6), channel_id=1, source_target_pairs={{0,8},{4,12},{8,0},{12,4},{16,24},{20,28},{24,16},{28,20},{1,9},{5... | collective-permute-start | bytes 1892360 | tf_op jit(solution)/shard_map/ppermute | solution.py:452
  906.6 42.4 %collective-permute-start.63 = (bf16[1,1,48,1408]{3,2,1,0:T(8,128)(2,1)}, bf16[1,1,48,1408]{3,2,1,0:T(8,128)(2,1)}, u32[]{:S(2)}, u32[]{:S(2)}) collective-permute-start(bf16[1,1,48,1408]{3,2,1,0:T(8,128)(2,1)} %constant_dynamic-slice_fusion.3), channel_id=1, source_target_pairs={{0,2},{1,3},{2,0},{3,1},{4,6},{5,7},{6,4},{7,5},{8,10},{9,11},{10,... | collective-permute-start | bytes 405512 | tf_op jit(solution)/shard_map/ppermute | solution.py:452
  915.5 60.1 %collective-permute-start.62 = (bf16[4,352,352]{2,1,0:T(8,128)(2,1)}, bf16[4,352,352]{2,1,0:T(8,128)(2,1)S(1)}, u32[]{:S(2)}, u32[]{:S(2)}) collective-permute-start(bf16[4,352,352]{2,1,0:T(8,128)(2,1)} %get-tuple-element.232), channel_id=1, source_target_pairs={{0,4},{4,0},{8,12},{12,8},{16,20},{20,16},{24,28},{28,24},{1,5},{5... | collective-permute-start | bytes 2973704 | tf_op jit(solution)/shard_map/ppermute | solution.py:452
  979.9 41.4 %collective-permute-start.66 = (bf16[2,352,352]{2,1,0:T(8,128)(2,1)}, bf16[2,352,352]{2,1,0:T(8,128)(2,1)}, u32[]{:S(2)}, u32[]{:S(2)}) collective-permute-start(bf16[2,352,352]{2,1,0:T(8,128)(2,1)} %get-tuple-element.239), channel_id=1, source_target_pairs={{0,8},{4,12},{8,0},{12,4},{16,24},{20,28},{24,16},{28,20},{1,9},{5... | collective-permute-start | bytes 1486856 | tf_op jit(solution)/shard_map/ppermute | solution.py:452
  1040.1 46.0 %collective-permute-start.94 = (bf16[208,1408]{1,0:T(8,128)(2,1)S(1)}, bf16[208,1408]{1,0:T(8,128)(2,1)}, u32[]{:S(2)}, u32[]{:S(2)}) collective-permute-start(bf16[208,1408]{1,0:T(8,128)(2,1)S(1)} %pad_maximum_fusion.13.refs_0_), channel_id=1, source_target_pairs={{0,2},{1,3},{2,0},{3,1},{4,6},{5,7},{6,4},{7,5},{8,10},{9,11},{10,... | collective-permute-start | bytes 1757192 | tf_op jit(solution)/shard_map/ppermute | solution.py:452
  1042.0 45.4 %collective-permute-start.91 = (bf16[176,1536]{1,0:T(8,128)(2,1)}, bf16[176,1536]{1,0:T(8,128)(2,1)}, u32[]{:S(2)}, u32[]{:S(2)}) collective-permute-start(bf16[176,1536]{1,0:T(8,128)(2,1)} %reduce-scatter.8.cloned.1.call-done.refs_0_), channel_id=1, source_target_pairs={{0,2},{1,3},{2,0},{3,1},{4,6},{5,7},{6,4},{7,5},{8,10},{9,11},{10,... | collective-permute-start | bytes 1622024 | tf_op jit(solution)/shard_map/ppermute | solution.py:452
  1044.7 41.3 %collective-permute-start.88 = (bf16[352,352]{1,0:T(8,128)(2,1)S(1)}, bf16[352,352]{1,0:T(8,128)(2,1)S(1)}, u32[]{:S(2)}, u32[]{:S(2)}) collective-permute-start(bf16[352,352]{1,0:T(8,128)(2,1)S(1)} %fusion.43.refs_0_), channel_id=1, source_target_pairs={{0,2},{1,3},{2,0},{3,1},{4,6},{5,7},{6,4},{7,5},{8,10},{9,11},{10,... | collective-permute-start | bytes 743432 | tf_op jit(solution)/shard_map/ppermute | solution.py:452
  (222 other events, 4034.1 us)
Sparse Core Ops, SparseCore 0:
  10.8 61.5 all-gather.4
  74.6 89.6 all-gather.6
  194.3 104.4 all-gather.8
  305.7 78.8 all-gather.10
  559.0 96.2 reduce-scatter.5
  702.5 95.0 reduce-scatter.3
  810.2 108.8 reduce-scatter.7

commit v4 on v3

--- a/solution.py
+++ b/solution.py
@@ -875,6 +875,35 @@
         else:
             total = self.held.astype(jnp.float32) + self.came.astype(jnp.float32)
             self.held, self.came = total.astype(self.held.dtype), None
+
+    def total(self):
+        while self.came is not None:
+            self.step()
+        return self.held[0]
+
+
+class SumWay:
+    def __init__(self, parts, axis):
+        self.held, self.axis, self.bit = dict(enumerate(parts)), axis, 1
+        self.came = None
+        self.send()
+
+    def send(self):
+        if self.bit < lax.axis_size(self.axis):
+            self.came = {
+                mask ^ self.bit: swap(self.held.pop(mask).astype(jnp.bfloat16), self.axis, self.bit)
+                for mask in sorted(self.held)
+                if mask & self.bit
+            }
+            self.bit *= 2
+
+    def step(self):
+        if self.came is None:
+            return
+        for mask, arrived in self.came.items():
+            self.held[mask] = self.held[mask].astype(jnp.float32) + arrived.astype(jnp.float32)
+        self.came = None
+        self.send()
 
     def total(self):
         while self.came is not None:
@@ -997,6 +1026,10 @@
 
     cond = silu_gate(timestep[0].astype(jnp.float32)).astype(jnp.bfloat16)
     cond_all = gather_small(cond, "dp")
+    xor_order = dp_rank ^ jnp.arange(dp_count, dtype=jnp.int32)
+    cond_ranked = jnp.take(cond_all.reshape(dp_count, IMGS, model_width), xor_order, axis=0).reshape(
+        dp_count * IMGS, model_width
+    )
     cond_rows = lax.dynamic_slice_in_dim(cond_all, dp_rank * row_count, row_count, axis=1)
     shifts = scatter_small(matmul(cond_rows, w_mod), "dp")
     time_shift = jnp.sum(jnp.where(member[:, :, None], shifts[None], 0.0), axis=1)
@@ -1012,17 +1045,17 @@
     n_float, pull_one = jax.vjp(layer_norm, x_one, ln_gains[2], ln_biases[2])
     n_one = (n_float + time_shift).astype(jnp.bfloat16)
     n_one_blocks, w_down = advance((blocks_of(n_one, "seq"), w_down), ways)
-    part_up = lax.all_gather(own_up, "dp", axis=0, tiled=True)
     own_down = lax.dynamic_slice_in_dim(w_down, seq_rank * part, part)
     part_down = lax.all_gather(own_down, "dp", axis=0, tiled=True)
     n_one_all = jnp.concatenate(n_one_blocks, axis=0)
     qkv_pre = matmul(n_one_all, part_qkv)
     packed = prep_heads(qkv_pre, tables, seg_column, head_gains, head_biases, local_heads, 256)
     head_out, inverse = self_forward(packed, local_heads, 256)
-    head_out = advance(head_out, ways)
+    head_out, own_up = advance((head_out, own_up), ways)
+    part_up = lax.all_gather(own_up, "dp", axis=0, tiled=True)
     out_blocks = head_out.reshape(seq_count, local_tok, head_cols)
     attn_o = join_columns(exchange([out_blocks[k] for k in seq_range], "seq"), ranks, jnp.bfloat16)
-    attn_o, part_up = advance((attn_o, part_up), ways)
+    attn_o = advance(attn_o, ways)
     if aligned(w_ckv.shape[0]):
         ckv_rows = w_ckv.shape[0]
         quarters = [q.reshape(dp_count, -1, w_ckv.shape[1]) for q in ckv_way.finish()]
@@ -1052,15 +1085,17 @@
     seg_row = seg_local[None]
     span = jnp.stack([seg_local[0], seg_local[-1]])
     cross_o, cross_top, cross_inv = cross_forward(cross_q, text_kv, penalty, seg_row, span)
-    cross_o, cot_blocks = lax.optimization_barrier((cross_o, blocks_of(cotangent, "seq")))
+    cross_o, cot_blocks, part_up = lax.optimization_barrier(
+        (cross_o, blocks_of(cotangent, "seq"), part_up)
+    )
+    cot_all = jnp.concatenate(cot_blocks, axis=0)
     x_three = x_two + matmul(cross_o, full_co)
     n2_float, pull_two = jax.vjp(layer_norm, x_three, ln_gains[4], ln_biases[4])
     n_two = n2_float.astype(jnp.bfloat16)
-    n_two_blocks, part_skip, part_down = lax.optimization_barrier(
-        (blocks_of(n_two, "seq"), part_skip, part_down)
+    n_two_blocks, part_skip, part_down, cot_all = lax.optimization_barrier(
+        (blocks_of(n_two, "seq"), part_skip, part_down, cot_all)
     )
     n_two_all = jnp.concatenate(n_two_blocks, axis=0)
-    cot_all = jnp.concatenate(cot_blocks, axis=0)
     skip_blocks = blocks_of(part_skip, "seq")
     up_proj = matmul(n_two_all, part_up)
     act_float, pull_gelu = jax.vjp(gelu_tanh, up_proj)
@@ -1072,16 +1107,12 @@
     d_up = pull_gelu(d_act)[0].astype(jnp.bfloat16)
     d_two_part = matmul(d_up, part_up.T).astype(jnp.bfloat16)
     total_down = lax.psum_scatter(grad_down, "dp", scatter_dimension=0, tiled=True)
-    d_two_part, skip_blocks, _ = lax.optimization_barrier((d_two_part, skip_blocks, grad_down))
+    d_two_part, skip_blocks = lax.optimization_barrier((d_two_part, skip_blocks))
     d_two_part = d_two_part.reshape(seq_count, local_tok, model_width)
     grad_up = matmul(n_two_all.T, d_up).astype(jnp.bfloat16)
     d_n_two = sum_parts([d_two_part[k] for k in seq_range], "seq", jnp.bfloat16)
     total_up = lax.psum_scatter(grad_up, "dp", scatter_dimension=0, tiled=True)
-    d_n_two, down_part, _ = lax.optimization_barrier((d_n_two, down_part, grad_up))
-    down_part = down_part.reshape(seq_count, local_tok, model_width)
-    block_out = (
-        x_three + sum_parts([down_part[k] for k in seq_range], "seq", jnp.bfloat16)
-    ).astype(jnp.bfloat16)
+    d_n_two, _, _ = lax.optimization_barrier((d_n_two, grad_up, grad_down))
     back_three_x, gain_four, bias_four = pull_two(d_n_two)
     d_x_three = cotangent.astype(jnp.float32) + back_three_x
     d_co = d_x_three.astype(jnp.bfloat16)
@@ -1106,10 +1137,13 @@
         axis=2,
     )
     scatters.append(Scatter(grad_cross, ranks))
-    d_heads = advance(d_heads, scatters)
+    d_heads, down_part = advance((d_heads, down_part), scatters)
+    down_part = down_part.reshape(seq_count, local_tok, model_width)
+    block_way = SumWay([down_part[k] for k in seq_range], "seq")
     scatters.append(Scatter(shared_rows(matmul(attn_o.T, d_attn)), ranks, 1))
     d_query, d_key, d_value = self_backward(packed, d_heads, inverse, local_heads, 256)
-    d_query = advance(d_query, scatters)
+    d_query, total_up = advance((d_query, total_up), scatters + [block_way])
+    up_way = Gather(total_up, [("seq", seq_bits, False)])
     d_qkv, gain_qk, bias_qk = prep_back(
         qkv_pre, d_query, d_key, d_value, tables, head_gains, local_heads, 256
     )
@@ -1117,41 +1151,38 @@
     grad_qkv = matmul(n_one_all.T, d_qkv).astype(jnp.bfloat16)
     total_qkv = lax.psum_scatter(grad_qkv, "dp", scatter_dimension=0, tiled=True)
     d_n_one = sum_parts([d_one_part[k] for k in seq_range], "seq", jnp.bfloat16)
-    d_n_one = advance(d_n_one, scatters)
+    d_n_one, total_down = advance(
+        (d_n_one, total_down), [scatters[0], scatters[2], block_way, up_way]
+    )
+    block_out = (x_three + block_way.total()).astype(jnp.bfloat16)
+    down_way = Gather(total_down, [("seq", seq_bits, False)])
     back_one_x, gain_one, bias_one = pull_one(d_n_one)
     d_x_one = d_x_two + back_one_x
     d_y = d_x_one.astype(jnp.bfloat16)
     y_blocks = split_columns(d_y, ranks)
     y_cols = jnp.concatenate(exchange(y_blocks, "seq"), axis=0)
     grad_skip_w = matmul(h_all.T, y_cols).astype(jnp.bfloat16)
-    grad_skip_w, d_n_one, y_blocks, total_down, total_up = lax.optimization_barrier(
-        (grad_skip_w, d_n_one, y_blocks, total_down, total_up)
-    )
-    moving = scatters
+    grad_skip_w, d_n_one, y_blocks = lax.optimization_barrier((grad_skip_w, d_n_one, y_blocks))
+    moving = scatters + [up_way, down_way]
     if aligned(skip_rows):
         skip_scatter = PartScatter(grad_skip_w, ranks)
-        moving = [skip_scatter] + scatters
+        moving = [skip_scatter] + moving
     else:
         total_skip = lax.psum_scatter(grad_skip_w, "dp", scatter_dimension=0, tiled=True)
-    down_blocks, up_blocks = blocks_of(total_down, "seq"), blocks_of(total_up, "seq")
 
     d_shift = d_n_one.astype(jnp.bfloat16)
     d_image = matmul(member.astype(jnp.bfloat16).T, d_shift)
-    d_image_all = gather_small(sum_all(d_image, "seq"), "dp")
-    grad_mod = jnp.dot(
-        cond_rows.astype(jnp.float32).T,
-        d_image_all,
-        precision=lax.Precision.HIGHEST,
-        preferred_element_type=jnp.float32,
-    )
     d_h_zero = sum(dot_nt(y, w) for y, w in zip(y_blocks, skip_blocks))
     d_h_zero = advance(d_h_zero, moving)
     d_joined, gain_skip, bias_skip = advance(pull_skip(d_h_zero), moving)
     grad_tokens = d_joined[:, :model_width].astype(jnp.bfloat16)
     grad_skip = d_joined[:, model_width:].astype(jnp.bfloat16)
     qk_cols = 4 * HEAD
+    mine = lax.broadcasted_iota(jnp.int32, (dp_count, 1, 1), 0) == dp_rank
+    d_images = jnp.where(mine, d_image[None], 0.0).reshape(dp_count * IMGS, model_width)
     small = jnp.concatenate(
         [
+            d_images,
             jnp.stack([gain_skip[:model_width], gain_skip[model_width:]]),
             jnp.stack([gain_one, gain_three, gain_four]),
             jnp.stack([bias_skip[:model_width], bias_skip[model_width:]]),
@@ -1162,18 +1193,28 @@
             ),
         ]
     )
-    small = sum_all(sum_all(small, "seq"), "dp")
+    small = sum_all(sum_all(small, "dp"), "seq")
+    cond_abs = lax.dynamic_slice_in_dim(
+        cond_ranked, dp_rank * row_count, row_count, axis=1
+    ).astype(jnp.float32)
+    grad_mod = jnp.dot(
+        cond_abs.T,
+        small[: dp_count * IMGS],
+        precision=lax.Precision.HIGHEST,
+        preferred_element_type=jnp.float32,
+    )
+    d_image_all, small = small[: dp_count * IMGS], small[dp_count * IMGS :]
     qk_total = small[10, :qk_cols].reshape(4, HEAD)
 
-    (grad_down,) = put_rows(down_blocks, ranks, [(seq_count * part, model_width)], [part])
+    (grad_down,) = put_rows(down_way.finish(), ranks, [(seq_count * part, model_width)], [part])
     grad_up = put_columns(
-        up_blocks,
+        up_way.finish(),
         ranks,
         [[(at, first, size) for first, at, size in m] for m in up_moves],
         wide,
         jnp.float32,
     )
-    grad_down, grad_up, grad_mod = advance((grad_down, grad_up, grad_mod), moving)
+    grad_down, grad_up = advance((grad_down, grad_up), moving)
     if aligned(skip_rows):
         total_skip = skip_scatter.total()
     share, ckv_share = share_of(row_count, seq_count), share_of(w_ckv.shape[0], seq_count)

time: 1120 us -> 1030 us (0.920)
  waiting for transfers between devices: 381 us -> 305 us
  starting transfers between devices: 131 us -> 108 us
  other arithmetic: 103 us -> 120 us
    ppermute x96 -> x91, waiting for transfers between devices: 380 us -> 294 us  [swap(): lax.ppermute(value, axis, [(rank, rank ^ mask) for rank in range(count)])]
    ppermute x96 -> x91, starting transfers between devices: 130 us -> 107 us  [swap(): lax.ppermute(value, axis, [(rank, rank ^ mask) for rank in range(count)])]
    unnamed x312 -> x319, local copies, waits for them, and re-layouts: 42.1 us -> 32.6 us
  transfers between devices with their start and end apart: 103 -> 98, of which waited for: 38 -> 31; matrix products, arithmetic and copies ran while one was open for 32% -> 37% of each run, Pallas kernels for 16% -> 18%
where the time goes in v4:
time: 1030 us
  waiting for transfers between devices  305 us (30%)
  Pallas kernels  186 us (18%)
  matrix products  185 us (18%)
  other arithmetic  120 us (12%)
  starting transfers between devices  108 us (10%)
  local copies, waits for them, and re-layouts  105 us (10%)
  between operations  16.4 us (2%)
    ppermute x91, waiting for transfers between devices, swap(): lax.ppermute(value, axis, [(rank, rank ^ mask) for rank in range(count)])  294 us
    dot_general x24, matrix products, matmul(): return jnp.dot(left, right, preferred_element_type=jnp.float32)  174 us
    ppermute x91, starting transfers between devices, swap(): lax.ppermute(value, axis, [(rank, rank ^ mask) for rank in range(count)])  107 us
    pallas_call x1, Pallas kernels, self_backward(): pl.pallas_call(functools.partial(self_backward_kernel, heads, blocks), gr...  37.8 us
    unnamed x319, local copies, waits for them, and re-layouts  32.6 us
    convert_element_type x12, other arithmetic, step(): self.held, self.came = (total.astype(jnp.bfloat16), None)  24.3 us
    pallas_call x2, Pallas kernels, place_quarters(): pl.pallas_call(functools.partial(quarter_kernel, row_counts, shares), gri...  21.1 us
  transfers between devices with their start and end apart: 98, of which 31 were waited for; matrix products, arithmetic and copies ran while one was open for 37% of the time, Pallas kernels for 18%

profile of v4, /device:TPU:1, one launch (start us, length us, event | category | flops | bytes accessed | tf_op | source)
XLA Modules:
  0.0 1025.0 jit_solution(1697309002962652128)
XLA Ops:
  48.0 28.1 %collective-permute-done.3 = bf16[1,32,2816]{2,1,0:T(8,128)(2,1)S(1)} collective-permute-done((bf16[1,32,2816]{2,1,0:T(8,128)(2,1)S(1)}, bf16[1,32,2816]{2,1,0:T(8,128)(2,1)S(1)}, u32[]{:S(2)}, u32[]{:S(2)}) %collective-permute-start.3) | collective-permute-done | bytes 180256 | tf_op jit(solution)/shard_map/ppermute | solution.py:452
  104.1 9.6 convolution_convert_fusion.12
  156.7 14.2 %collective-permute-done.17 = bf16[384,1408]{1,0:T(8,128)(2,1)} collective-permute-done((bf16[384,1408]{1,0:T(8,128)(2,1)}, bf16[384,1408]{1,0:T(8,128)(2,1)}, u32[]{:S(2)}, u32[]{:S(2)}) %collective-permute-start.17) | collective-permute-done | bytes 1081376 | tf_op jit(solution)/shard_map/ppermute | solution.py:452
  178.1 15.7 %collective-permute-done.20 = bf16[2,2,32,2816]{3,2,1,0:T(8,128)(2,1)S(1)} collective-permute-done((bf16[2,2,32,2816]{3,2,1,0:T(8,128)(2,1)}, bf16[2,2,32,2816]{3,2,1,0:T(8,128)(2,1)S(1)}, u32[]{:S(2)}, u32[]{:S(2)}) %collective-permute-start.20) | collective-permute-done | bytes 720928 | tf_op jit(solution)/shard_map/ppermute | solution.py:452
  210.6 12.9 %fusion.90.pre_ref = f32[1536,1536]{1,0:T(8,128)} fusion(bf16[1536,1408]{1,0:T(8,128)(2,1)} %constant_dynamic-update-slice_fusion, bf16[1408,1536]{1,0:T(8,128)(2,1)} %all-gather.7.cloned.1.call-done), kind=kOutput, calls=%fused_computation.282 | convolution fusion | flops 6643777536 | bytes 18087936 | tf_op jit(solution)/shard_map/dot_general | solution.py:35
  223.5 15.3 %shard_map.389.q_ref.k_ref.v_ref = bf16[1536,1536]{1,0:T(8,128)(2,1)} custom-call(f32[1536,1536]{1,0:T(8,128)} %fusion.90.pre_ref, f32[1536,128]{1,0:T(8,128)} %get-tuple-element.167.cos_ref, f32[1536,128]{1,0:T(8,128)} %get-tuple-element.168.sa_ref, f32[1536,128]{1,0:T(8,128)} %get-tuple-element.169.sb_ref, s32[1536,1]{1,0:T(8,128)} %copy.90.seg_ref, ...), custom_call_target="tpu_custom_call" | custom-call | flops 47185920 | bytes 18874368 | tf_op jit(solution)/shard_map/pallas_call | solution.py:94
  238.9 18.7 %shard_map.390 = (bf16[1536,352]{1,0:T(8,128)(2,1)}, f32[4,1536]{1,0:T(4,128)}) custom-call(bf16[1536,1536]{1,0:T(8,128)(2,1)} %shard_map.389.q_ref.k_ref.v_ref, bf16[1536,1536]{1,0:T(8,128)(2,1)} %shard_map.389.q_ref.k_ref.v_ref, bf16[1536,1536]{1,0:T(8,128)(2,1)} %shard_map.389.q_ref.k_ref.v_ref), custom_call_target="tpu_custom_call" | custom-call | flops 4831838208 | bytes 6291456 | tf_op jit(solution)/shard_map/pallas_call | solution.py:140
  257.5 12.7 %collective-permute-done.22.refs_2_ = bf16[8,144,1408]{2,1,0:T(8,128)(2,1)} collective-permute-done((bf16[8,144,1408]{2,1,0:T(8,128)(2,1)}, bf16[8,144,1408]{2,1,0:T(8,128)(2,1)}, u32[]{:S(2)}, u32[]{:S(2)}) %collective-permute-start.22) | collective-permute-done | bytes 3244064 | tf_op jit(solution)/shard_map/ppermute | solution.py:452
  294.3 12.4 %shard_map.392 = (bf16[1408,1408]{1,0:T(8,128)(2,1)}, bf16[1408,1408]{1,0:T(8,128)(2,1)}, bf16[1408,1408]{1,0:T(8,128)(2,1)}) custom-call(s32[2]{0:T(128)} %pad_add_fusion.ranks_ref, bf16[8,144,1408]{2,1,0:T(8,128)(2,1)} %pad_maximum_fusion.3.refs_0_, bf16[8,144,1408]{2,1,0:T(8,128)(2,1)} %collective-permute-done.21.refs_1_, ...), custom_call_target="tpu_custom_call" | custom-call | bytes 23789568 | tf_op jit(solution)/shard_map/pallas_call | solution.py:617
  339.7 10.5 %convolution_convert_fusion.10.kv_ref = bf16[1008,2816]{1,0:T(8,128)(2,1)} fusion(bf16[1008,1024]{1,0:T(8,128)(2,1)S(1)} %bitcast.187, bf16[1024,2816]{1,0:T(8,128)(2,1)} %shard_map.393), kind=kOutput, calls=%fused_computation.31 | convolution fusion | flops 5816143872 | bytes 13508608 | tf_op jit(solution)/shard_map/dot_general | solution.py:35
  353.1 11.1 %shard_map.394 = (bf16[384,1408]{1,0:T(8,128)(2,1)}, f32[16,384]{1,0:T(8,128)}, f32[16,384]{1,0:T(8,128)}) custom-call(s32[2]{0:T(128)} %pad_add_fusion.1.span_ref, bf16[384,1408]{1,0:T(8,128)(2,1)} %convolution_convert_fusion.15.q_ref, bf16[1008,2816]{1,0:T(8,128)(2,1)} %convolution_convert_fusion.10.kv_ref, bf16[1008,1]{1,0:T(8,128)(2,1)} %copy.91.pen_ref, ...), custom_call_target="tpu_custom_call" | custom-call | flops 2113929216 | bytes 10002432 | tf_op jit(solution)/shard_map/pallas_call | solution.py:336
  378.1 23.6 %collective-permute-done.33 = bf16[384,1408]{1,0:T(8,128)(2,1)} collective-permute-done((bf16[384,1408]{1,0:T(8,128)(2,1)}, bf16[384,1408]{1,0:T(8,128)(2,1)}, u32[]{:S(2)}, u32[]{:S(2)}) %collective-permute-start.33) | collective-permute-done | bytes 1081376 | tf_op jit(solution)/shard_map/ppermute | solution.py:452
  414.0 10.5 %all-gather.11.cloned.1.call-done = bf16[1536,1408]{1,0:T(8,128)(2,1)} async-done(((bf16[192,1408]{1,0:T(8,128)(2,1)}), bf16[1536,1408]{1,0:T(8,128)(2,1)}) %all-gather.11.cloned.1.call-update) | async-done | bytes 4325392 | tf_op jit(solution)/shard_map/all_gather | solution.py:1049
  437.7 14.0 %fusion.91 = f32[1536,1536]{1,0:T(8,128)} fusion(bf16[1536,1408]{1,0:T(8,128)(2,1)S(1)} %constant_dynamic-update-slice_fusion.4, bf16[1408,1536]{1,0:T(8,128)(2,1)} %all-gather.9.cloned.1.call-done), kind=kOutput, calls=%fused_computation.283 | convolution fusion | flops 6643777536 | bytes 18087936 | tf_op jit(solution)/shard_map/dot_general | solution.py:35
  451.8 16.6 %fusion.4 = bf16[1536,1536]{1,0:T(8,128)(2,1)} fusion(f32[1536,1536]{1,0:T(8,128)} %fusion.91, bf16[1536,1408]{1,0:T(8,128)(2,1)S(1)} %bitcast.178, bf16[1536,1408]{1,0:T(8,128)(2,1)S(1)} %bitcast.198), kind=kOutput, calls=%fused_computation.14 | convolution fusion | flops 6700400640 | bytes 22806528 | tf_op jit(solution)/shard_map/dot_general | solution.py:35
  474.4 11.0 %convolution_convert_fusion.5 = bf16[1536,1408]{1,0:T(8,128)(2,1)S(1)} fusion(bf16[1536,1536]{1,0:T(8,128)(2,1)} %fusion.4, bf16[1408,1536]{1,0:T(8,128)(2,1)} %all-gather.9.cloned.1.call-done), kind=kOutput, calls=%fused_computation.24 | convolution fusion | flops 6645940224 | bytes 13369344 | tf_op jit(solution)/shard_map/dot_general | solution.py:35
  489.5 9.6 convolution_convert_fusion.3
  503.7 11.6 %convolution_convert_fusion.4 = bf16[1408,1536]{1,0:T(8,128)(2,1)} fusion(bf16[1536,1408]{1,0:T(8,128)(2,1)} %copy-done.86, bf16[1536,1536]{1,0:T(8,128)(2,1)} %fusion.4), kind=kOutput, calls=%fused_computation.23 | convolution fusion | flops 6645940224 | bytes 13369344 | tf_op jit(solution)/shard_map/dot_general | solution.py:35
  515.8 12.5 %collective-permute-done.40 = bf16[384,1408]{1,0:T(8,128)(2,1)} collective-permute-done((bf16[384,1408]{1,0:T(8,128)(2,1)}, bf16[384,1408]{1,0:T(8,128)(2,1)}, u32[]{:S(2)}, u32[]{:S(2)}) %collective-permute-start.40) | collective-permute-done | bytes 1081376 | tf_op jit(solution)/shard_map/ppermute | solution.py:452
  544.8 15.5 %shard_map.395 = (bf16[384,1408]{1,0:T(8,128)(2,1)}, bf16[1008,2816]{1,0:T(8,128)(2,1)}) custom-call(s32[2]{0:T(128)} %pad_add_fusion.1.span_ref, bf16[384,1408]{1,0:T(8,128)(2,1)} %convolution_convert_fusion.15.q_ref, bf16[1008,2816]{1,0:T(8,128)(2,1)} %convolution_convert_fusion.10.kv_ref, bf16[1008,1]{1,0:T(8,128)(2,1)} %copy.91.pen_ref, ...), custom_call_target="tpu_custom_call" | custom-call | flops 5284823040 | bytes 15679488 | tf_op jit(solution)/shard_map/pallas_call | solution.py:398
  560.3 9.4 convolution_convert_fusion.9
  580.2 9.3 collective-permute-start.46
  589.5 11.9 %convolution_convert_fusion.2 = bf16[1536,1408]{1,0:T(8,128)(2,1)} fusion(bf16[1536,1408]{1,0:T(8,128)(2,1)S(1)} %bitcast.200, f32[1536,1536]{1,0:T(8,128)} %fusion.91), kind=kOutput, calls=%fused_computation.21 | convolution fusion | flops 6667173888 | bytes 18087936 | tf_op jit(solution)/shard_map/dot_general | solution.py:35
  662.1 37.8 %shard_map.397 = (bf16[1536,512]{1,0:T(8,128)(2,1)}, bf16[1536,512]{1,0:T(8,128)(2,1)}, bf16[1536,512]{1,0:T(8,128)(2,1)}) custom-call(bf16[1536,1536]{1,0:T(8,128)(2,1)} %shard_map.389.q_ref.k_ref.v_ref, bf16[1536,1536]{1,0:T(8,128)(2,1)} %shard_map.389.q_ref.k_ref.v_ref, bf16[1536,1536]{1,0:T(8,128)(2,1)} %shard_map.389.q_ref.k_ref.v_ref, ...), custom_call_target="tpu_custom_call" | custom-call | flops 12079595520 | bytes 11010048 | tf_op jit(solution)/shard_map/pallas_call | solution.py:197
  708.1 17.9 %shard_map.398 = (bf16[1536,1536]{1,0:T(8,128)(2,1)}, f32[2,128]{1,0:T(2,128)}, f32[2,128]{1,0:T(2,128)}) custom-call(f32[1536,1536]{1,0:T(8,128)} %fusion.90.pre_ref, bf16[1536,512]{1,0:T(8,128)(2,1)} %get-tuple-element.224.dq_ref, bf16[1536,512]{1,0:T(8,128)(2,1)} %get-tuple-element.225.dk_ref, bf16[1536,512]{1,0:T(8,128)(2,1)} %get-tuple-element.226.dv_ref, ...), custom_call_target="tpu_custom_call" | custom-call | flops 47185920 | bytes 23592960 | tf_op jit(solution)/shard_map/pallas_call | solution.py:256
  726.0 10.8 %convolution_convert_fusion.1 = bf16[1536,1408]{1,0:T(8,128)(2,1)S(1)} fusion(bf16[1536,1536]{1,0:T(8,128)(2,1)} %get-tuple-element.227, bf16[1408,1536]{1,0:T(8,128)(2,1)} %all-gather.7.cloned.1.call-done), kind=kOutput, calls=%fused_computation.20 | convolution fusion | flops 6645940224 | bytes 13369344 | tf_op jit(solution)/shard_map/dot_general | solution.py:35
  742.3 11.0 %convolution_convert_fusion = bf16[1408,1536]{1,0:T(8,128)(2,1)} fusion(bf16[1536,1408]{1,0:T(8,128)(2,1)} %constant_dynamic-update-slice_fusion, bf16[1536,1536]{1,0:T(8,128)(2,1)S(1)} %copy-done.136), kind=kOutput, calls=%fused_computation.19 | convolution fusion | flops 6645940224 | bytes 13369344 | tf_op jit(solution)/shard_map/dot_general | solution.py:35
  767.8 19.7 %collective-permute-done.54 = bf16[384,1408]{1,0:T(8,128)(2,1)S(1)} collective-permute-done((bf16[384,1408]{1,0:T(8,128)(2,1)S(1)}, bf16[384,1408]{1,0:T(8,128)(2,1)S(1)}, u32[]{:S(2)}, u32[]{:S(2)}) %collective-permute-start.54) | collective-permute-done | bytes 1081376 | tf_op jit(solution)/shard_map/ppermute | solution.py:452
  793.8 23.9 %collective-permute-done.55 = bf16[1,2,48,1408]{3,2,1,0:T(8,128)(2,1)S(1)} collective-permute-done((bf16[1,2,48,1408]{3,2,1,0:T(8,128)(2,1)S(1)}, bf16[1,2,48,1408]{3,2,1,0:T(8,128)(2,1)S(1)}, u32[]{:S(2)}, u32[]{:S(2)}) %collective-permute-start.55) | collective-permute-done | bytes 270368 | tf_op jit(solution)/shard_map/ppermute | solution.py:452
  872.9 20.5 %collective-permute-done.66 = bf16[2,2,48,1408]{3,2,1,0:T(8,128)(2,1)} collective-permute-done((bf16[2,2,48,1408]{3,2,1,0:T(8,128)(2,1)}, bf16[2,2,48,1408]{3,2,1,0:T(8,128)(2,1)}, u32[]{:S(2)}, u32[]{:S(2)}) %collective-permute-start.66) | collective-permute-done | bytes 540704 | tf_op jit(solution)/shard_map/ppermute | solution.py:452
  915.7 15.4 %collective-permute-done.70.refs_1_.refs_3_ = bf16[2,352,352]{2,1,0:T(8,128)(2,1)S(1)} collective-permute-done((bf16[2,352,352]{2,1,0:T(8,128)(2,1)}, bf16[2,352,352]{2,1,0:T(8,128)(2,1)S(1)}, u32[]{:S(2)}, u32[]{:S(2)}) %collective-permute-start.70) | collective-permute-done | bytes 495648 | tf_op jit(solution)/shard_map/ppermute | solution.py:452
  951.1 13.1 %collective-permute-done.79 = bf16[1,352,352]{2,1,0:T(8,128)(2,1)S(1)} collective-permute-done((bf16[1,352,352]{2,1,0:T(8,128)(2,1)}, bf16[1,352,352]{2,1,0:T(8,128)(2,1)S(1)}, u32[]{:S(2)}, u32[]{:S(2)}) %collective-permute-start.79) | collective-permute-done | bytes 247840 | tf_op jit(solution)/shard_map/ppermute | solution.py:452
  (742 shorter events, 521.9 us)
Async XLA Ops:
  7.2 96.8 %all-gather.5.cloned.1.call-start = ((), (), s32[]{:S(2)}) async-start(), calls=%async_computation.3 | async-start | bytes 2433024 | tf_op jit(solution)/shard_map/all_gather | solution.py:982
  9.3 201.3 %all-gather.7.cloned.1.call-start = ((), (), s32[]{:S(2)}) async-start(), calls=%async_computation.4 | async-start | bytes 4866048 | tf_op jit(solution)/shard_map/all_gather | solution.py:984
  21.8 54.2 %collective-permute-start = (bf16[384,2816]{1,0:T(8,128)(2,1)}, bf16[384,2816]{1,0:T(8,128)(2,1)}, u32[]{:S(2)}, u32[]{:S(2)}) collective-permute-start(bf16[384,2816]{1,0:T(8,128)(2,1)} %fusion.16), channel_id=1, source_target_pairs={{0,1},{1,0},{2,3},{3,2},{4,5},{5,4},{6,7},{7,6},{8,9},{9,8},{10,11... | collective-permute-start | bytes 6488072 | tf_op jit(solution)/shard_map/ppermute | solution.py:452
  21.8 54.2 %collective-permute-start.1 = (bf16[384,2816]{1,0:T(8,128)(2,1)}, bf16[384,2816]{1,0:T(8,128)(2,1)}, u32[]{:S(2)}, u32[]{:S(2)}) collective-permute-start(bf16[384,2816]{1,0:T(8,128)(2,1)} %fusion.16), channel_id=1, source_target_pairs={{0,2},{1,3},{2,0},{3,1},{4,6},{5,7},{6,4},{7,5},{8,10},{9,11},{10,... | collective-permute-start | bytes 6488072 | tf_op jit(solution)/shard_map/ppermute | solution.py:452
  24.5 51.5 %collective-permute-start.2 = (bf16[1,144,1408]{2,1,0:T(8,128)(2,1)}, bf16[1,144,1408]{2,1,0:T(8,128)(2,1)S(1)}, u32[]{:S(2)}, u32[]{:S(2)}) collective-permute-start(bf16[1,144,1408]{2,1,0:T(8,128)(2,1)} %bitcast.2), channel_id=1, source_target_pairs={{0,16},{4,20},{8,24},{12,28},{16,0},{20,4},{24,8},{28,12},{1,17},{... | collective-permute-start | bytes 1216520 | tf_op jit(solution)/shard_map/ppermute | solution.py:452
  26.9 49.2 %collective-permute-start.3 = (bf16[1,32,2816]{2,1,0:T(8,128)(2,1)S(1)}, bf16[1,32,2816]{2,1,0:T(8,128)(2,1)S(1)}, u32[]{:S(2)}, u32[]{:S(2)}) collective-permute-start(bf16[1,32,2816]{2,1,0:T(8,128)(2,1)S(1)} %bitcast.189), channel_id=1, source_target_pairs={{0,2},{1,3},{2,0},{3,1},{4,6},{5,7},{6,4},{7,5},{8,10},{9,11},{10,... | collective-permute-start | bytes 540680 | tf_op jit(solution)/shard_map/ppermute | solution.py:452
  28.3 335.9 %all-gather.9.cloned.1.call-start = ((), (), s32[]{:S(2)}) async-start(), calls=%async_computation.5 | async-start | bytes 4866048 | tf_op jit(solution)/shard_map/all_gather | solution.py:1055
  98.8 42.1 %collective-permute-start.14 = (bf16[2,144,1408]{2,1,0:T(8,128)(2,1)}, bf16[2,144,1408]{2,1,0:T(8,128)(2,1)}, u32[]{:S(2)}, u32[]{:S(2)}) collective-permute-start(bf16[2,144,1408]{2,1,0:T(8,128)(2,1)} %pad_maximum_fusion.12), channel_id=1, source_target_pairs={{0,8},{4,12},{8,0},{12,4},{16,24},{20,28},{24,16},{28,20},{1,9},{5... | collective-permute-start | bytes 2433032 | tf_op jit(solution)/shard_map/ppermute | solution.py:452
  151.7 42.0 %collective-permute-start.19 = (bf16[4,144,1408]{2,1,0:T(8,128)(2,1)}, bf16[4,144,1408]{2,1,0:T(8,128)(2,1)}, u32[]{:S(2)}, u32[]{:S(2)}) collective-permute-start(bf16[4,144,1408]{2,1,0:T(8,128)(2,1)} %pad_maximum_fusion.7), channel_id=1, source_target_pairs={{0,4},{4,0},{8,12},{12,8},{16,20},{20,16},{24,28},{28,24},{1,5},{5... | collective-permute-start | bytes 4866056 | tf_op jit(solution)/shard_map/ppermute | solution.py:452
  153.0 40.8 %collective-permute-start.16 = (bf16[384,1408]{1,0:T(8,128)(2,1)}, bf16[384,1408]{1,0:T(8,128)(2,1)}, u32[]{:S(2)}, u32[]{:S(2)}) collective-permute-start(bf16[384,1408]{1,0:T(8,128)(2,1)} %add_convert_fusion.8), channel_id=1, source_target_pairs={{0,1},{1,0},{2,3},{3,2},{4,5},{5,4},{6,7},{7,6},{8,9},{9,8},{10,11... | collective-permute-start | bytes 3244040 | tf_op jit(solution)/shard_map/ppermute | solution.py:452
  197.3 60.2 %collective-permute-start.21 = (bf16[8,144,1408]{2,1,0:T(8,128)(2,1)}, bf16[8,144,1408]{2,1,0:T(8,128)(2,1)}, u32[]{:S(2)}, u32[]{:S(2)}) collective-permute-start(bf16[8,144,1408]{2,1,0:T(8,128)(2,1)} %pad_maximum_fusion.3.refs_0_), channel_id=1, source_target_pairs={{0,1},{1,0},{2,3},{3,2},{4,5},{5,4},{6,7},{7,6},{8,9},{9,8},{10,11... | collective-permute-start | bytes 9732104 | tf_op jit(solution)/shard_map/ppermute | solution.py:452
  198.1 72.2 %collective-permute-start.22 = (bf16[8,144,1408]{2,1,0:T(8,128)(2,1)}, bf16[8,144,1408]{2,1,0:T(8,128)(2,1)}, u32[]{:S(2)}, u32[]{:S(2)}) collective-permute-start(bf16[8,144,1408]{2,1,0:T(8,128)(2,1)} %pad_maximum_fusion.3.refs_0_), channel_id=1, source_target_pairs={{0,2},{1,3},{2,0},{3,1},{4,6},{5,7},{6,4},{7,5},{8,10},{9,11},{10,... | collective-permute-start | bytes 9732104 | tf_op jit(solution)/shard_map/ppermute | solution.py:452
  200.2 57.3 %collective-permute-start.23 = (bf16[4,2,32,2816]{3,2,1,0:T(8,128)(2,1)}, bf16[4,2,32,2816]{3,2,1,0:T(8,128)(2,1)}, u32[]{:S(2)}, u32[]{:S(2)}) collective-permute-start(bf16[4,2,32,2816]{3,2,1,0:T(8,128)(2,1)} %pad_maximum_fusion.10), channel_id=1, source_target_pairs={{0,4},{4,0},{8,12},{12,8},{16,20},{20,16},{24,28},{28,24},{1,5},{5... | collective-permute-start | bytes 4325384 | tf_op jit(solution)/shard_map/ppermute | solution.py:452
  270.3 154.3 %all-gather.11.cloned.1.call-start = ((), (), s32[]{:S(2)}) async-start(), calls=%async_computation.6 | async-start | bytes 4866048 | tf_op jit(solution)/shard_map/all_gather | solution.py:1049
  278.1 421.8 %reduce-scatter.4.cloned.1.call-start = ((), (), s32[]{:S(2)}) async-start(), calls=%async_computation.7 | async-start | bytes 4866048 | tf_op jit(solution)/shard_map/reduce_scatter | solution.py:1114
  321.0 43.1 %collective-permute-start.29 = (bf16[384,1408]{1,0:T(8,128)(2,1)S(1)}, bf16[384,1408]{1,0:T(8,128)(2,1)}, u32[]{:S(2)}, u32[]{:S(2)}) collective-permute-start(bf16[384,1408]{1,0:T(8,128)(2,1)S(1)} %copy-done.21), channel_id=1, source_target_pairs={{0,1},{1,0},{2,3},{3,2},{4,5},{5,4},{6,7},{7,6},{8,9},{9,8},{10,11... | collective-permute-start | bytes 3244040 | tf_op jit(solution)/shard_map/ppermute | solution.py:452
  378.1 46.4 %collective-permute-start.32 = (bf16[384,1408]{1,0:T(8,128)(2,1)}, bf16[384,1408]{1,0:T(8,128)(2,1)}, u32[]{:S(2)}, u32[]{:S(2)}) collective-permute-start(bf16[384,1408]{1,0:T(8,128)(2,1)} %add_convert_fusion.6), channel_id=1, source_target_pairs={{0,1},{1,0},{2,3},{3,2},{4,5},{5,4},{6,7},{7,6},{8,9},{9,8},{10,11... | collective-permute-start | bytes 3244040 | tf_op jit(solution)/shard_map/ppermute | solution.py:452
  428.6 43.0 %collective-permute-start.36 = (bf16[2816,352]{0,1:T(8,128)(2,1)}, bf16[2816,352]{0,1:T(8,128)(2,1)S(1)}, u32[]{:S(2)}, u32[]{:S(2)}) collective-permute-start(bf16[2816,352]{0,1:T(8,128)(2,1)} %copy.92), channel_id=1, source_target_pairs={{0,2},{1,3},{2,0},{3,1},{4,6},{5,7},{6,4},{7,5},{8,10},{9,11},{10,... | collective-permute-start | bytes 5947400 | tf_op jit(solution)/shard_map/ppermute | solution.py:452
  429.8 55.7 %collective-permute-start.35 = (bf16[2816,352]{0,1:T(8,128)(2,1)}, bf16[2816,352]{0,1:T(8,128)(2,1)S(1)}, u32[]{:S(2)}, u32[]{:S(2)}) collective-permute-start(bf16[2816,352]{0,1:T(8,128)(2,1)} %copy.92), channel_id=1, source_target_pairs={{0,1},{1,0},{2,3},{3,2},{4,5},{5,4},{6,7},{7,6},{8,9},{9,8},{10,11... | collective-permute-start | bytes 5947400 | tf_op jit(solution)/shard_map/ppermute | solution.py:452
  515.3 304.2 %reduce-scatter.6.cloned.1.call-start = ((), (), s32[]{:S(2)}) async-start(), calls=%async_computation.8 | async-start | bytes 4866048 | tf_op jit(solution)/shard_map/reduce_scatter | solution.py:1109
  580.2 61.0 %collective-permute-start.46 = (bf16[8,2,112,1408]{3,2,1,0:T(8,128)(2,1)}, bf16[8,2,112,1408]{3,2,1,0:T(8,128)(2,1)}, u32[]{:S(2)}, u32[]{:S(2)}) collective-permute-start(bf16[8,2,112,1408]{3,2,1,0:T(8,128)(2,1)} %dynamic-slice_bitcast_fusion), channel_id=1, source_target_pairs={{0,1},{1,0},{2,3},{3,2},{4,5},{5,4},{6,7},{7,6},{8,9},{9,8},{10,11... | collective-permute-start | bytes 15138824 | tf_op jit(solution)/shard_map/ppermute | solution.py:452
  601.4 380.5 %reduce-scatter.8.cloned.1.call-start = ((), (), s32[]{:S(2)}) async-start(), calls=%async_computation.9 | async-start | bytes 4866048 | tf_op jit(solution)/shard_map/reduce_scatter | solution.py:1152
  650.6 54.7 %collective-permute-start.48 = (bf16[8,1,112,1408]{3,2,1,0:T(8,128)(2,1)}, bf16[8,1,112,1408]{3,2,1,0:T(8,128)(2,1)}, u32[]{:S(2)}, u32[]{:S(2)}) collective-permute-start(bf16[8,1,112,1408]{3,2,1,0:T(8,128)(2,1)} %constant_dynamic-slice_fusion.6), channel_id=1, source_target_pairs={{0,2},{1,3},{2,0},{3,1},{4,6},{5,7},{6,4},{7,5},{8,10},{9,11},{10,... | collective-permute-start | bytes 7569416 | tf_op jit(solution)/shard_map/ppermute | solution.py:452
  652.1 47.8 %collective-permute-start.49 = (bf16[8,2,48,1408]{3,2,1,0:T(8,128)(2,1)}, bf16[8,2,48,1408]{3,2,1,0:T(8,128)(2,1)}, u32[]{:S(2)}, u32[]{:S(2)}) collective-permute-start(bf16[8,2,48,1408]{3,2,1,0:T(8,128)(2,1)} %dynamic-slice_bitcast_fusion.1), channel_id=1, source_target_pairs={{0,1},{1,0},{2,3},{3,2},{4,5},{5,4},{6,7},{7,6},{8,9},{9,8},{10,11... | collective-permute-start | bytes 6488072 | tf_op jit(solution)/shard_map/ppermute | solution.py:452
  657.5 42.4 %collective-permute-start.47 = (bf16[2,2,48,1408]{3,2,1,0:T(8,128)(2,1)}, bf16[2,2,48,1408]{3,2,1,0:T(8,128)(2,1)}, u32[]{:S(2)}, u32[]{:S(2)}) collective-permute-start(bf16[2,2,48,1408]{3,2,1,0:T(8,128)(2,1)} %dynamic-slice_bitcast_fusion.8), channel_id=1, source_target_pairs={{0,8},{4,12},{8,0},{12,4},{16,24},{20,28},{24,16},{28,20},{1,9},{5... | collective-permute-start | bytes 1622024 | tf_op jit(solution)/shard_map/ppermute | solution.py:452
  707.8 111.7 %collective-permute-start.57 = (bf16[384,1408]{1,0:T(8,128)(2,1)}, bf16[384,1408]{1,0:T(8,128)(2,1)}, u32[]{:S(2)}, u32[]{:S(2)}) collective-permute-start(bf16[384,1408]{1,0:T(8,128)(2,1)} %add_convert_fusion.3), channel_id=1, source_target_pairs={{0,2},{1,3},{2,0},{3,1},{4,6},{5,7},{6,4},{7,5},{8,10},{9,11},{10,... | collective-permute-start | bytes 3244040 | tf_op jit(solution)/shard_map/ppermute | solution.py:452
  757.3 62.1 %collective-permute-start.56 = (bf16[4,2,48,1408]{3,2,1,0:T(8,128)(2,1)}, bf16[4,2,48,1408]{3,2,1,0:T(8,128)(2,1)}, u32[]{:S(2)}, u32[]{:S(2)}) collective-permute-start(bf16[4,2,48,1408]{3,2,1,0:T(8,128)(2,1)} %dynamic-slice_bitcast_fusion.4), channel_id=1, source_target_pairs={{0,4},{4,0},{8,12},{12,8},{16,20},{20,16},{24,28},{28,24},{1,5},{5... | collective-permute-start | bytes 3244040 | tf_op jit(solution)/shard_map/ppermute | solution.py:452
  757.3 62.1 %collective-permute-start.58 = (bf16[176,1536]{1,0:T(8,128)(2,1)}, bf16[176,1536]{1,0:T(8,128)(2,1)}, u32[]{:S(2)}, u32[]{:S(2)}) collective-permute-start(bf16[176,1536]{1,0:T(8,128)(2,1)} %reduce-scatter.4.cloned.1.call-done.refs_0_), channel_id=1, source_target_pairs={{0,1},{1,0},{2,3},{3,2},{4,5},{5,4},{6,7},{7,6},{8,9},{9,8},{10,11... | collective-permute-start | bytes 1622024 | tf_op jit(solution)/shard_map/ppermute | solution.py:452
  767.7 51.7 %collective-permute-start.59 = (bf16[176,1536]{1,0:T(8,128)(2,1)}, bf16[176,1536]{1,0:T(8,128)(2,1)}, u32[]{:S(2)}, u32[]{:S(2)}) collective-permute-start(bf16[176,1536]{1,0:T(8,128)(2,1)} %reduce-scatter.4.cloned.1.call-done.refs_0_), channel_id=1, source_target_pairs={{0,2},{1,3},{2,0},{3,1},{4,6},{5,7},{6,4},{7,5},{8,10},{9,11},{10,... | collective-permute-start | bytes 1622024 | tf_op jit(solution)/shard_map/ppermute | solution.py:452
  818.5 53.1 %collective-permute-start.65 = (bf16[4,1,112,1408]{3,2,0,1:T(8,128)(2,1)}, bf16[4,1,112,1408]{3,2,0,1:T(8,128)(2,1)}, u32[]{:S(2)}, u32[]{:S(2)}) collective-permute-start(bf16[4,1,112,1408]{3,2,0,1:T(8,128)(2,1)} %dynamic-slice_bitcast_fusion.3), channel_id=1, source_target_pairs={{0,4},{4,0},{8,12},{12,8},{16,20},{20,16},{24,28},{28,24},{1,5},{5... | collective-permute-start | bytes 3784712 | tf_op jit(solution)/shard_map/ppermute | solution.py:452
  834.0 59.4 %collective-permute-start.68 = (bf16[192,1408]{1,0:T(8,128)(2,1)}, bf16[192,1408]{1,0:T(8,128)(2,1)}, u32[]{:S(2)}, u32[]{:S(2)}) collective-permute-start(bf16[192,1408]{1,0:T(8,128)(2,1)} %reduce-scatter.6.cloned.1.call-done.refs_0_), channel_id=1, source_target_pairs={{0,1},{1,0},{2,3},{3,2},{4,5},{5,4},{6,7},{7,6},{8,9},{9,8},{10,11... | collective-permute-start | bytes 1622024 | tf_op jit(solution)/shard_map/ppermute | solution.py:452
  836.2 57.2 %collective-permute-start.69 = (bf16[192,1408]{1,0:T(8,128)(2,1)}, bf16[192,1408]{1,0:T(8,128)(2,1)}, u32[]{:S(2)}, u32[]{:S(2)}) collective-permute-start(bf16[192,1408]{1,0:T(8,128)(2,1)} %reduce-scatter.6.cloned.1.call-done.refs_0_), channel_id=1, source_target_pairs={{0,2},{1,3},{2,0},{3,1},{4,6},{5,7},{6,4},{7,5},{8,10},{9,11},{10,... | collective-permute-start | bytes 1622024 | tf_op jit(solution)/shard_map/ppermute | solution.py:452
  (222 other events, 3648.6 us)
Sparse Core Ops, SparseCore 0:
  10.8 61.6 all-gather.4
  74.7 90.7 all-gather.6
  270.4 78.2 all-gather.8
  351.3 73.2 all-gather.10
  515.4 88.3 reduce-scatter.3
  607.6 93.0 reduce-scatter.5
  758.7 127.6 reduce-scatter.7

commit v5 on v4

--- a/solution.py
+++ b/solution.py
@@ -1005,11 +1005,6 @@
             [("seq", seq_bits[:-1], True), ("dp", dp_bits, True), ("seq", seq_bits[-1:], False)],
         )
         ways.append(ckv_way)
-    own_up = advance(own_up, [h_way] + ways)
-    h_all = jnp.concatenate(h_way.finish(), axis=0)
-    x_cols = matmul(h_all, part_skip).astype(jnp.bfloat16).reshape(seq_count, local_tok, head_cols)
-    x_one = join_columns(exchange([x_cols[k] for k in seq_range], "seq"), ranks, jnp.float32)
-
     seg_all = segment_ids[0]
     seg_local, member, _, _ = grid_positions(
         seg_all, grid_widths[0], seq_rank * local_tok, local_tok
@@ -1023,6 +1018,18 @@
     seg_column = reorder(seg_all)[:, None]
     lane_pad = ((0, 0), (0, LANES - HEAD))
     head_gains, head_biases = jnp.pad(qk_gains, lane_pad), jnp.pad(qk_biases, lane_pad)
+
+    keys = -(-CAP // 16) * 16
+    caption_rows = jnp.pad(
+        captions[0].reshape(IMGS, CAP, -1), ((0, 0), (0, keys - CAP), (0, 0))
+    ).reshape(IMGS * keys, -1)
+    penalty = caption_penalty(clip_lengths[0], t5_lengths[0], keys)
+    own_up, tables, seg_column, caption_rows, penalty = advance(
+        (own_up, tables, seg_column, caption_rows, penalty), [h_way] + ways
+    )
+    h_all = jnp.concatenate(h_way.finish(), axis=0)
+    x_cols = matmul(h_all, part_skip).astype(jnp.bfloat16).reshape(seq_count, local_tok, head_cols)
+    x_one = join_columns(exchange([x_cols[k] for k in seq_range], "seq"), ranks, jnp.float32)
 
     cond = silu_gate(timestep[0].astype(jnp.float32)).astype(jnp.bfloat16)
     cond_all = gather_small(cond, "dp")
@@ -1034,14 +1041,7 @@
     shifts = scatter_small(matmul(cond_rows, w_mod), "dp")
     time_shift = jnp.sum(jnp.where(member[:, :, None], shifts[None], 0.0), axis=1)
 
-    keys = -(-CAP // 16) * 16
-    caption_rows = jnp.pad(
-        captions[0].reshape(IMGS, CAP, -1), ((0, 0), (0, keys - CAP), (0, 0))
-    ).reshape(IMGS * keys, -1)
-    penalty = caption_penalty(clip_lengths[0], t5_lengths[0], keys)
-    x_one, tables, seg_column, caption_rows, penalty, time_shift = advance(
-        (x_one, tables, seg_column, caption_rows, penalty, time_shift), ways
-    )
+    x_one, time_shift = advance((x_one, time_shift), ways[:1])
     n_float, pull_one = jax.vjp(layer_norm, x_one, ln_gains[2], ln_biases[2])
     n_one = (n_float + time_shift).astype(jnp.bfloat16)
     n_one_blocks, w_down = advance((blocks_of(n_one, "seq"), w_down), ways)
@@ -1056,14 +1056,6 @@
     out_blocks = head_out.reshape(seq_count, local_tok, head_cols)
     attn_o = join_columns(exchange([out_blocks[k] for k in seq_range], "seq"), ranks, jnp.bfloat16)
     attn_o = advance(attn_o, ways)
-    if aligned(w_ckv.shape[0]):
-        ckv_rows = w_ckv.shape[0]
-        quarters = [q.reshape(dp_count, -1, w_ckv.shape[1]) for q in ckv_way.finish()]
-        (full_ckv,) = place_quarters(
-            quarters, ranks, [ckv_rows], [share_of(ckv_rows, seq_count)], dp_bits
-        )
-    else:
-        full_ckv = lax.all_gather(w_ckv, "dp", axis=0, tiled=True)
     if aligned(row_count):
         full_out, full_cq, full_co = place_quarters(
             square_way.finish(),
@@ -1079,8 +1071,16 @@
     x_two = x_one + matmul(attn_o, full_out)
     n3_float, pull_three = jax.vjp(layer_norm, x_two, ln_gains[3], ln_biases[3])
     n_three = n3_float.astype(jnp.bfloat16)
-    n_three, cotangent = lax.optimization_barrier((n_three, cotangent))
+    n_three, cotangent = advance((n_three, cotangent), ways)
     cross_q = matmul(n_three, full_cq).astype(jnp.bfloat16)
+    if aligned(w_ckv.shape[0]):
+        ckv_rows = w_ckv.shape[0]
+        quarters = [q.reshape(dp_count, -1, w_ckv.shape[1]) for q in ckv_way.finish()]
+        (full_ckv,) = place_quarters(
+            quarters, ranks, [ckv_rows], [share_of(ckv_rows, seq_count)], dp_bits
+        )
+    else:
+        full_ckv = lax.all_gather(w_ckv, "dp", axis=0, tiled=True)
     text_kv = matmul(caption_rows, full_ckv).astype(jnp.bfloat16)
     seg_row = seg_local[None]
     span = jnp.stack([seg_local[0], seg_local[-1]])
@@ -1152,7 +1152,7 @@
     total_qkv = lax.psum_scatter(grad_qkv, "dp", scatter_dimension=0, tiled=True)
     d_n_one = sum_parts([d_one_part[k] for k in seq_range], "seq", jnp.bfloat16)
     d_n_one, total_down = advance(
-        (d_n_one, total_down), [scatters[0], scatters[2], block_way, up_way]
+        (d_n_one, total_down), [block_way, up_way]
     )
     block_out = (x_three + block_way.total()).astype(jnp.bfloat16)
     down_way = Gather(total_down, [("seq", seq_bits, False)])
@@ -1164,16 +1164,18 @@
     grad_skip_w = matmul(h_all.T, y_cols).astype(jnp.bfloat16)
     grad_skip_w, d_n_one, y_blocks = lax.optimization_barrier((grad_skip_w, d_n_one, y_blocks))
     moving = scatters + [up_way, down_way]
+    first_moving = moving
     if aligned(skip_rows):
         skip_scatter = PartScatter(grad_skip_w, ranks)
-        moving = [skip_scatter] + moving
+        y_blocks = advance(y_blocks, moving)
+        first_moving, moving = [skip_scatter], [skip_scatter] + moving
     else:
         total_skip = lax.psum_scatter(grad_skip_w, "dp", scatter_dimension=0, tiled=True)
 
     d_shift = d_n_one.astype(jnp.bfloat16)
     d_image = matmul(member.astype(jnp.bfloat16).T, d_shift)
     d_h_zero = sum(dot_nt(y, w) for y, w in zip(y_blocks, skip_blocks))
-    d_h_zero = advance(d_h_zero, moving)
+    d_h_zero = advance(d_h_zero, first_moving)
     d_joined, gain_skip, bias_skip = advance(pull_skip(d_h_zero), moving)
     grad_tokens = d_joined[:, :model_width].astype(jnp.bfloat16)
     grad_skip = d_joined[:, model_width:].astype(jnp.bfloat16)

time: 1030 us -> 1060 us (1.029)
  starting transfers between devices: 108 us -> 138 us
  waiting for transfers between devices: 305 us -> 293 us
    ppermute x91, starting transfers between devices: 107 us -> 137 us  [swap(): lax.ppermute(value, axis, [(rank, rank ^ mask) for rank in range(count)])]
    unnamed x319 -> x331, local copies, waits for them, and re-layouts: 32.6 us -> 32.9 us
  transfers between devices with their start and end apart: 98 -> 98, of which waited for: 31 -> 33; matrix products, arithmetic and copies ran while one was open for 37% -> 37% of each run, Pallas kernels for 18% -> 17%
where the time goes in v5:
time: 1060 us; the launch traced here: 1050 us
  waiting for transfers between devices  293 us (28%)
  matrix products  187 us (18%)
  Pallas kernels  186 us (18%)
  starting transfers between devices  138 us (13%)
  other arithmetic  121 us (11%)
  local copies, waits for them, and re-layouts  107 us (10%)
  between operations  16.4 us (2%)
    ppermute x91, waiting for transfers between devices, swap(): lax.ppermute(value, axis, [(rank, rank ^ mask) for rank in range(count)])  293 us
    dot_general x24, matrix products, matmul(): return jnp.dot(left, right, preferred_element_type=jnp.float32)  175 us
    ppermute x91, starting transfers between devices, swap(): lax.ppermute(value, axis, [(rank, rank ^ mask) for rank in range(count)])  137 us
    pallas_call x1, Pallas kernels, self_backward(): pl.pallas_call(functools.partial(self_backward_kernel, heads, blocks), gr...  37.8 us
    unnamed x331, local copies, waits for them, and re-layouts  32.9 us
    convert_element_type x12, other arithmetic, step(): self.held, self.came = (total.astype(jnp.bfloat16), None)  26.9 us
  transfers between devices with their start and end apart: 98, of which 33 were waited for; matrix products, arithmetic and copies ran while one was open for 37% of the time, Pallas kernels for 17%

profile of v5, /device:TPU:1, one launch (start us, length us, event | category | flops | bytes accessed | tf_op | source)
XLA Modules:
  0.0 1047.2 jit_solution(15869145967289740990)
XLA Ops:
  46.3 29.6 %collective-permute-done.3 = bf16[1,32,2816]{2,1,0:T(8,128)(2,1)S(1)} collective-permute-done((bf16[1,32,2816]{2,1,0:T(8,128)(2,1)S(1)}, bf16[1,32,2816]{2,1,0:T(8,128)(2,1)S(1)}, u32[]{:S(2)}, u32[]{:S(2)}) %collective-permute-start.3) | collective-permute-done | bytes 180256 | tf_op jit(solution)/shard_map/ppermute | solution.py:452
  101.2 9.6 convolution_convert_fusion.12
  148.2 15.5 %collective-permute-start.15 = (bf16[384,1408]{1,0:T(8,128)(2,1)}, bf16[384,1408]{1,0:T(8,128)(2,1)}, u32[]{:S(2)}, u32[]{:S(2)}) collective-permute-start(bf16[384,1408]{1,0:T(8,128)(2,1)} %add_convert_fusion.8), channel_id=1, source_target_pairs={{0,1},{1,0},{2,3},{3,2},{4,5},{5,4},{6,7},{7,6},{8,9},{9,8},{10,11... | collective-permute-start | bytes 3244040 | tf_op jit(solution)/shard_map/ppermute | solution.py:452
  163.7 11.0 %collective-permute-start.17 = (bf16[384,1408]{1,0:T(8,128)(2,1)}, bf16[384,1408]{1,0:T(8,128)(2,1)}, u32[]{:S(2)}, u32[]{:S(2)}) collective-permute-start(bf16[384,1408]{1,0:T(8,128)(2,1)} %collective-permute-done.16), channel_id=1, source_target_pairs={{0,1},{1,0},{2,3},{3,2},{4,5},{5,4},{6,7},{7,6},{8,9},{9,8},{10,11... | collective-permute-start | bytes 3244040 | tf_op jit(solution)/shard_map/ppermute | solution.py:452
  175.4 10.8 %collective-permute-start.19 = (bf16[1,2,32,2816]{3,2,1,0:T(8,128)(2,1)S(1)}, bf16[1,2,32,2816]{3,2,1,0:T(8,128)(2,1)S(1)}, u32[]{:S(2)}, u32[]{:S(2)}) collective-permute-start(bf16[1,2,32,2816]{3,2,1,0:T(8,128)(2,1)S(1)} %get-tuple-element.342), channel_id=1, source_target_pairs={{0,16},{4,20},{8,24},{12,28},{16,0},{20,4},{24,8},{28,12},{1,17},{... | collective-permute-start | bytes 1081352 | tf_op jit(solution)/shard_map/ppermute | solution.py:452
  188.6 14.2 %collective-permute-done.19 = bf16[1,2,32,2816]{3,2,1,0:T(8,128)(2,1)S(1)} collective-permute-done((bf16[1,2,32,2816]{3,2,1,0:T(8,128)(2,1)S(1)}, bf16[1,2,32,2816]{3,2,1,0:T(8,128)(2,1)S(1)}, u32[]{:S(2)}, u32[]{:S(2)}) %collective-permute-start.19) | collective-permute-done | bytes 360480 | tf_op jit(solution)/shard_map/ppermute | solution.py:452
  217.4 12.8 %fusion.90.pre_ref = f32[1536,1536]{1,0:T(8,128)} fusion(bf16[1536,1408]{1,0:T(8,128)(2,1)} %constant_dynamic-update-slice_fusion, bf16[1408,1536]{1,0:T(8,128)(2,1)} %all-gather.7.cloned.1.call-done), kind=kOutput, calls=%fused_computation.282 | convolution fusion | flops 6643777536 | bytes 18087936 | tf_op jit(solution)/shard_map/dot_general | solution.py:35
  230.2 15.3 %shard_map.389.q_ref.k_ref.v_ref = bf16[1536,1536]{1,0:T(8,128)(2,1)} custom-call(f32[1536,1536]{1,0:T(8,128)} %fusion.90.pre_ref, f32[1536,128]{1,0:T(8,128)} %get-tuple-element.169.cos_ref, f32[1536,128]{1,0:T(8,128)} %get-tuple-element.170.sa_ref, f32[1536,128]{1,0:T(8,128)} %get-tuple-element.171.sb_ref, s32[1536,1]{1,0:T(8,128)} %copy.90.seg_ref, ...), custom_call_target="tpu_custom_call" | custom-call | flops 47185920 | bytes 18874368 | tf_op jit(solution)/shard_map/pallas_call | solution.py:94
  245.5 18.7 %shard_map.390 = (bf16[1536,352]{1,0:T(8,128)(2,1)}, f32[4,1536]{1,0:T(4,128)}) custom-call(bf16[1536,1536]{1,0:T(8,128)(2,1)} %shard_map.389.q_ref.k_ref.v_ref, bf16[1536,1536]{1,0:T(8,128)(2,1)} %shard_map.389.q_ref.k_ref.v_ref, bf16[1536,1536]{1,0:T(8,128)(2,1)} %shard_map.389.q_ref.k_ref.v_ref), custom_call_target="tpu_custom_call" | custom-call | flops 4831838208 | bytes 6291456 | tf_op jit(solution)/shard_map/pallas_call | solution.py:140
  264.2 14.7 %collective-permute-done.21.refs_2_ = bf16[8,144,1408]{2,1,0:T(8,128)(2,1)} collective-permute-done((bf16[8,144,1408]{2,1,0:T(8,128)(2,1)}, bf16[8,144,1408]{2,1,0:T(8,128)(2,1)}, u32[]{:S(2)}, u32[]{:S(2)}) %collective-permute-start.21) | collective-permute-done | bytes 3244064 | tf_op jit(solution)/shard_map/ppermute | solution.py:452
  302.5 21.7 %collective-permute-done.27 = bf16[4,2,32,2816]{3,2,1,0:T(8,128)(2,1)} collective-permute-done((bf16[4,2,32,2816]{3,2,1,0:T(8,128)(2,1)}, bf16[4,2,32,2816]{3,2,1,0:T(8,128)(2,1)}, u32[]{:S(2)}, u32[]{:S(2)}) %collective-permute-start.27) | collective-permute-done | bytes 1441824 | tf_op jit(solution)/shard_map/ppermute | solution.py:452
  329.8 12.3 %shard_map.392 = (bf16[1408,1408]{1,0:T(8,128)(2,1)}, bf16[1408,1408]{1,0:T(8,128)(2,1)}, bf16[1408,1408]{1,0:T(8,128)(2,1)}) custom-call(s32[2]{0:T(128)} %pad_add_fusion.ranks_ref, bf16[8,144,1408]{2,1,0:T(8,128)(2,1)} %pad_maximum_fusion.3.refs_0_, bf16[8,144,1408]{2,1,0:T(8,128)(2,1)} %collective-permute-done.20.refs_1_, ...), custom_call_target="tpu_custom_call" | custom-call | bytes 23789568 | tf_op jit(solution)/shard_map/pallas_call | solution.py:617
  364.4 9.8 collective-permute-done.30
  375.1 10.5 %convolution_convert_fusion.10.kv_ref = bf16[1008,2816]{1,0:T(8,128)(2,1)} fusion(bf16[1008,1024]{1,0:T(8,128)(2,1)S(1)} %bitcast.185, bf16[1024,2816]{1,0:T(8,128)(2,1)} %shard_map.393), kind=kOutput, calls=%fused_computation.31 | convolution fusion | flops 5816143872 | bytes 13508608 | tf_op jit(solution)/shard_map/dot_general | solution.py:35
  388.5 11.1 %shard_map.394 = (bf16[384,1408]{1,0:T(8,128)(2,1)}, f32[16,384]{1,0:T(8,128)}, f32[16,384]{1,0:T(8,128)}) custom-call(s32[2]{0:T(128)} %pad_add_fusion.1.span_ref, bf16[384,1408]{1,0:T(8,128)(2,1)} %convolution_convert_fusion.15.q_ref, bf16[1008,2816]{1,0:T(8,128)(2,1)} %convolution_convert_fusion.10.kv_ref, bf16[1008,1]{1,0:T(8,128)(2,1)} %copy.91.pen_ref, ...), custom_call_target="tpu_custom_call" | custom-call | flops 2113929216 | bytes 10002432 | tf_op jit(solution)/shard_map/pallas_call | solution.py:336
  412.7 23.8 %collective-permute-done.33 = bf16[384,1408]{1,0:T(8,128)(2,1)} collective-permute-done((bf16[384,1408]{1,0:T(8,128)(2,1)}, bf16[384,1408]{1,0:T(8,128)(2,1)}, u32[]{:S(2)}, u32[]{:S(2)}) %collective-permute-start.33) | collective-permute-done | bytes 1081376 | tf_op jit(solution)/shard_map/ppermute | solution.py:452
  460.3 14.1 %fusion.91 = f32[1536,1536]{1,0:T(8,128)} fusion(bf16[1536,1408]{1,0:T(8,128)(2,1)S(1)} %constant_dynamic-update-slice_fusion.4, bf16[1408,1536]{1,0:T(8,128)(2,1)} %all-gather.9.cloned.1.call-done), kind=kOutput, calls=%fused_computation.283 | convolution fusion | flops 6643777536 | bytes 18087936 | tf_op jit(solution)/shard_map/dot_general | solution.py:35
  474.4 16.6 %fusion.4 = bf16[1536,1536]{1,0:T(8,128)(2,1)} fusion(f32[1536,1536]{1,0:T(8,128)} %fusion.91, bf16[1536,1408]{1,0:T(8,128)(2,1)S(1)} %bitcast.176, bf16[1536,1408]{1,0:T(8,128)(2,1)S(1)} %bitcast.196), kind=kOutput, calls=%fused_computation.14 | convolution fusion | flops 6700400640 | bytes 22806528 | tf_op jit(solution)/shard_map/dot_general | solution.py:35
  498.6 11.0 %convolution_convert_fusion.5 = bf16[1536,1408]{1,0:T(8,128)(2,1)S(1)} fusion(bf16[1536,1536]{1,0:T(8,128)(2,1)} %fusion.4, bf16[1408,1536]{1,0:T(8,128)(2,1)} %all-gather.9.cloned.1.call-done), kind=kOutput, calls=%fused_computation.24 | convolution fusion | flops 6645940224 | bytes 13369344 | tf_op jit(solution)/shard_map/dot_general | solution.py:35
  513.7 9.6 convolution_convert_fusion.3
  528.1 11.6 %convolution_convert_fusion.4 = bf16[1408,1536]{1,0:T(8,128)(2,1)} fusion(bf16[1536,1408]{1,0:T(8,128)(2,1)} %copy-done.87, bf16[1536,1536]{1,0:T(8,128)(2,1)} %fusion.4), kind=kOutput, calls=%fused_computation.23 | convolution fusion | flops 6645940224 | bytes 13369344 | tf_op jit(solution)/shard_map/dot_general | solution.py:35
  540.3 12.2 %collective-permute-done.40 = bf16[384,1408]{1,0:T(8,128)(2,1)} collective-permute-done((bf16[384,1408]{1,0:T(8,128)(2,1)}, bf16[384,1408]{1,0:T(8,128)(2,1)}, u32[]{:S(2)}, u32[]{:S(2)}) %collective-permute-start.40) | collective-permute-done | bytes 1081376 | tf_op jit(solution)/shard_map/ppermute | solution.py:452
  569.0 15.4 %shard_map.395 = (bf16[384,1408]{1,0:T(8,128)(2,1)}, bf16[1008,2816]{1,0:T(8,128)(2,1)}) custom-call(s32[2]{0:T(128)} %pad_add_fusion.1.span_ref, bf16[384,1408]{1,0:T(8,128)(2,1)} %convolution_convert_fusion.15.q_ref, bf16[1008,2816]{1,0:T(8,128)(2,1)} %convolution_convert_fusion.10.kv_ref, bf16[1008,1]{1,0:T(8,128)(2,1)} %copy.91.pen_ref, ...), custom_call_target="tpu_custom_call" | custom-call | flops 5284823040 | bytes 15679488 | tf_op jit(solution)/shard_map/pallas_call | solution.py:398
  613.4 11.9 %convolution_convert_fusion.2 = bf16[1536,1408]{1,0:T(8,128)(2,1)} fusion(bf16[1536,1408]{1,0:T(8,128)(2,1)S(1)} %bitcast.198, f32[1536,1536]{1,0:T(8,128)} %fusion.91), kind=kOutput, calls=%fused_computation.21 | convolution fusion | flops 6667173888 | bytes 18087936 | tf_op jit(solution)/shard_map/dot_general | solution.py:35
  684.7 37.8 %shard_map.397 = (bf16[1536,512]{1,0:T(8,128)(2,1)}, bf16[1536,512]{1,0:T(8,128)(2,1)}, bf16[1536,512]{1,0:T(8,128)(2,1)}) custom-call(bf16[1536,1536]{1,0:T(8,128)(2,1)} %shard_map.389.q_ref.k_ref.v_ref, bf16[1536,1536]{1,0:T(8,128)(2,1)} %shard_map.389.q_ref.k_ref.v_ref, bf16[1536,1536]{1,0:T(8,128)(2,1)} %shard_map.389.q_ref.k_ref.v_ref, ...), custom_call_target="tpu_custom_call" | custom-call | flops 12079595520 | bytes 11010048 | tf_op jit(solution)/shard_map/pallas_call | solution.py:197
  731.0 18.0 %shard_map.398 = (bf16[1536,1536]{1,0:T(8,128)(2,1)}, f32[2,128]{1,0:T(2,128)}, f32[2,128]{1,0:T(2,128)}) custom-call(f32[1536,1536]{1,0:T(8,128)} %fusion.90.pre_ref, bf16[1536,512]{1,0:T(8,128)(2,1)} %get-tuple-element.227.dq_ref, bf16[1536,512]{1,0:T(8,128)(2,1)} %get-tuple-element.228.dk_ref, bf16[1536,512]{1,0:T(8,128)(2,1)} %get-tuple-element.229.dv_ref, ...), custom_call_target="tpu_custom_call" | custom-call | flops 47185920 | bytes 23592960 | tf_op jit(solution)/shard_map/pallas_call | solution.py:256
  749.0 10.8 %convolution_convert_fusion.1 = bf16[1536,1408]{1,0:T(8,128)(2,1)S(1)} fusion(bf16[1536,1536]{1,0:T(8,128)(2,1)} %get-tuple-element.230, bf16[1408,1536]{1,0:T(8,128)(2,1)} %all-gather.7.cloned.1.call-done), kind=kOutput, calls=%fused_computation.20 | convolution fusion | flops 6645940224 | bytes 13369344 | tf_op jit(solution)/shard_map/dot_general | solution.py:35
  763.0 11.0 %convolution_convert_fusion = bf16[1408,1536]{1,0:T(8,128)(2,1)} fusion(bf16[1536,1408]{1,0:T(8,128)(2,1)} %constant_dynamic-update-slice_fusion, bf16[1536,1536]{1,0:T(8,128)(2,1)S(1)} %copy-done.142), kind=kOutput, calls=%fused_computation.19 | convolution fusion | flops 6645940224 | bytes 13369344 | tf_op jit(solution)/shard_map/dot_general | solution.py:35
  794.6 15.9 %collective-permute-done.54 = bf16[384,1408]{1,0:T(8,128)(2,1)} collective-permute-done((bf16[384,1408]{1,0:T(8,128)(2,1)}, bf16[384,1408]{1,0:T(8,128)(2,1)}, u32[]{:S(2)}, u32[]{:S(2)}) %collective-permute-start.54) | collective-permute-done | bytes 1081376 | tf_op jit(solution)/shard_map/ppermute | solution.py:452
  814.1 19.6 %collective-permute-done.55 = bf16[384,1408]{1,0:T(8,128)(2,1)} collective-permute-done((bf16[384,1408]{1,0:T(8,128)(2,1)}, bf16[384,1408]{1,0:T(8,128)(2,1)}, u32[]{:S(2)}, u32[]{:S(2)}) %collective-permute-start.55) | collective-permute-done | bytes 1081376 | tf_op jit(solution)/shard_map/ppermute | solution.py:452
  924.5 11.5 %collective-permute-done.68.refs_1_.refs_3_ = bf16[2,352,352]{2,1,0:T(8,128)(2,1)S(1)} collective-permute-done((bf16[2,352,352]{2,1,0:T(8,128)(2,1)}, bf16[2,352,352]{2,1,0:T(8,128)(2,1)S(1)}, u32[]{:S(2)}, u32[]{:S(2)}) %collective-permute-start.68) | collective-permute-done | bytes 495648 | tf_op jit(solution)/shard_map/ppermute | solution.py:452
  952.8 25.1 %collective-permute-done.78 = bf16[1,352,352]{2,1,0:T(8,128)(2,1)} collective-permute-done((bf16[1,352,352]{2,1,0:T(8,128)(2,1)}, bf16[1,352,352]{2,1,0:T(8,128)(2,1)}, u32[]{:S(2)}, u32[]{:S(2)}) %collective-permute-start.78) | collective-permute-done | bytes 247840 | tf_op jit(solution)/shard_map/ppermute | solution.py:452
  (753 shorter events, 537.3 us)
Async XLA Ops:
  7.2 94.0 %all-gather.5.cloned.1.call-start = ((), (), s32[]{:S(2)}) async-start(), calls=%async_computation.3 | async-start | bytes 2433024 | tf_op jit(solution)/shard_map/all_gather | solution.py:982
  9.3 208.0 %all-gather.7.cloned.1.call-start = ((), (), s32[]{:S(2)}) async-start(), calls=%async_computation.4 | async-start | bytes 4866048 | tf_op jit(solution)/shard_map/all_gather | solution.py:984
  21.8 54.2 %collective-permute-start = (bf16[384,2816]{1,0:T(8,128)(2,1)}, bf16[384,2816]{1,0:T(8,128)(2,1)}, u32[]{:S(2)}, u32[]{:S(2)}) collective-permute-start(bf16[384,2816]{1,0:T(8,128)(2,1)} %fusion.16), channel_id=1, source_target_pairs={{0,1},{1,0},{2,3},{3,2},{4,5},{5,4},{6,7},{7,6},{8,9},{9,8},{10,11... | collective-permute-start | bytes 6488072 | tf_op jit(solution)/shard_map/ppermute | solution.py:452
  21.8 54.2 %collective-permute-start.1 = (bf16[384,2816]{1,0:T(8,128)(2,1)}, bf16[384,2816]{1,0:T(8,128)(2,1)}, u32[]{:S(2)}, u32[]{:S(2)}) collective-permute-start(bf16[384,2816]{1,0:T(8,128)(2,1)} %fusion.16), channel_id=1, source_target_pairs={{0,2},{1,3},{2,0},{3,1},{4,6},{5,7},{6,4},{7,5},{8,10},{9,11},{10,... | collective-permute-start | bytes 6488072 | tf_op jit(solution)/shard_map/ppermute | solution.py:452
  24.6 51.4 %collective-permute-start.2 = (bf16[1,144,1408]{2,1,0:T(8,128)(2,1)}, bf16[1,144,1408]{2,1,0:T(8,128)(2,1)S(1)}, u32[]{:S(2)}, u32[]{:S(2)}) collective-permute-start(bf16[1,144,1408]{2,1,0:T(8,128)(2,1)} %bitcast.7), channel_id=1, source_target_pairs={{0,16},{4,20},{8,24},{12,28},{16,0},{20,4},{24,8},{28,12},{1,17},{... | collective-permute-start | bytes 1216520 | tf_op jit(solution)/shard_map/ppermute | solution.py:452
  26.9 49.1 %collective-permute-start.3 = (bf16[1,32,2816]{2,1,0:T(8,128)(2,1)S(1)}, bf16[1,32,2816]{2,1,0:T(8,128)(2,1)S(1)}, u32[]{:S(2)}, u32[]{:S(2)}) collective-permute-start(bf16[1,32,2816]{2,1,0:T(8,128)(2,1)S(1)} %bitcast.187), channel_id=1, source_target_pairs={{0,2},{1,3},{2,0},{3,1},{4,6},{5,7},{6,4},{7,5},{8,10},{9,11},{10,... | collective-permute-start | bytes 540680 | tf_op jit(solution)/shard_map/ppermute | solution.py:452
  28.3 371.3 %all-gather.9.cloned.1.call-start = ((), (), s32[]{:S(2)}) async-start(), calls=%async_computation.5 | async-start | bytes 4866048 | tf_op jit(solution)/shard_map/all_gather | solution.py:1055
  35.4 41.3 %collective-permute-start.9 = (bf16[6,1408]{1,0:T(8,128)(2,1)S(1)}, bf16[6,1408]{1,0:T(8,128)(2,1)S(1)}, u32[]{:S(2)}, u32[]{:S(2)}) collective-permute-start(bf16[6,1408]{1,0:T(8,128)(2,1)S(1)} %pad_maximum_fusion.19), channel_id=1, source_target_pairs={{0,8},{4,12},{8,0},{12,4},{16,24},{20,28},{24,16},{28,20},{1,9},{5... | collective-permute-start | bytes 50696 | tf_op jit(solution)/shard_map/ppermute | solution.py:452
  148.2 54.6 %collective-permute-start.18 = (bf16[4,144,1408]{2,1,0:T(8,128)(2,1)}, bf16[4,144,1408]{2,1,0:T(8,128)(2,1)}, u32[]{:S(2)}, u32[]{:S(2)}) collective-permute-start(bf16[4,144,1408]{2,1,0:T(8,128)(2,1)} %pad_maximum_fusion.7), channel_id=1, source_target_pairs={{0,4},{4,0},{8,12},{12,8},{16,20},{20,16},{24,28},{28,24},{1,5},{5... | collective-permute-start | bytes 4866056 | tf_op jit(solution)/shard_map/ppermute | solution.py:452
  148.2 54.6 %collective-permute-start.15 = (bf16[384,1408]{1,0:T(8,128)(2,1)}, bf16[384,1408]{1,0:T(8,128)(2,1)}, u32[]{:S(2)}, u32[]{:S(2)}) collective-permute-start(bf16[384,1408]{1,0:T(8,128)(2,1)} %add_convert_fusion.8), channel_id=1, source_target_pairs={{0,1},{1,0},{2,3},{3,2},{4,5},{5,4},{6,7},{7,6},{8,9},{9,8},{10,11... | collective-permute-start | bytes 3244040 | tf_op jit(solution)/shard_map/ppermute | solution.py:452
  206.2 58.0 %collective-permute-start.20 = (bf16[8,144,1408]{2,1,0:T(8,128)(2,1)}, bf16[8,144,1408]{2,1,0:T(8,128)(2,1)}, u32[]{:S(2)}, u32[]{:S(2)}) collective-permute-start(bf16[8,144,1408]{2,1,0:T(8,128)(2,1)} %pad_maximum_fusion.3.refs_0_), channel_id=1, source_target_pairs={{0,1},{1,0},{2,3},{3,2},{4,5},{5,4},{6,7},{7,6},{8,9},{9,8},{10,11... | collective-permute-start | bytes 9732104 | tf_op jit(solution)/shard_map/ppermute | solution.py:452
  206.8 72.2 %collective-permute-start.21 = (bf16[8,144,1408]{2,1,0:T(8,128)(2,1)}, bf16[8,144,1408]{2,1,0:T(8,128)(2,1)}, u32[]{:S(2)}, u32[]{:S(2)}) collective-permute-start(bf16[8,144,1408]{2,1,0:T(8,128)(2,1)} %pad_maximum_fusion.3.refs_0_), channel_id=1, source_target_pairs={{0,2},{1,3},{2,0},{3,1},{4,6},{5,7},{6,4},{7,5},{8,10},{9,11},{10,... | collective-permute-start | bytes 9732104 | tf_op jit(solution)/shard_map/ppermute | solution.py:452
  207.7 56.5 %collective-permute-start.22 = (bf16[2,2,32,2816]{3,2,1,0:T(8,128)(2,1)}, bf16[2,2,32,2816]{3,2,1,0:T(8,128)(2,1)S(1)}, u32[]{:S(2)}, u32[]{:S(2)}) collective-permute-start(bf16[2,2,32,2816]{3,2,1,0:T(8,128)(2,1)} %pad_maximum_fusion.13), channel_id=1, source_target_pairs={{0,8},{4,12},{8,0},{12,4},{16,24},{20,28},{24,16},{28,20},{1,9},{5... | collective-permute-start | bytes 2162696 | tf_op jit(solution)/shard_map/ppermute | solution.py:452
  279.0 169.8 %all-gather.11.cloned.1.call-start = ((), (), s32[]{:S(2)}) async-start(), calls=%async_computation.6 | async-start | bytes 4866048 | tf_op jit(solution)/shard_map/all_gather | solution.py:1049
  279.0 45.2 %collective-permute-start.26 = (bf16[8,144,1408]{2,1,0:T(8,128)(2,1)}, bf16[8,144,1408]{2,1,0:T(8,128)(2,1)}, u32[]{:S(2)}, u32[]{:S(2)}) collective-permute-start(bf16[8,144,1408]{2,1,0:T(8,128)(2,1)} %collective-permute-done.21.refs_2_), channel_id=1, source_target_pairs={{0,1},{1,0},{2,3},{3,2},{4,5},{5,4},{6,7},{7,6},{8,9},{9,8},{10,11... | collective-permute-start | bytes 9732104 | tf_op jit(solution)/shard_map/ppermute | solution.py:452
  282.1 42.1 %collective-permute-start.27 = (bf16[4,2,32,2816]{3,2,1,0:T(8,128)(2,1)}, bf16[4,2,32,2816]{3,2,1,0:T(8,128)(2,1)}, u32[]{:S(2)}, u32[]{:S(2)}) collective-permute-start(bf16[4,2,32,2816]{3,2,1,0:T(8,128)(2,1)} %pad_maximum_fusion.10), channel_id=1, source_target_pairs={{0,4},{4,0},{8,12},{12,8},{16,20},{20,16},{24,28},{28,24},{1,5},{5... | collective-permute-start | bytes 4325384 | tf_op jit(solution)/shard_map/ppermute | solution.py:452
  329.7 392.7 %reduce-scatter.4.cloned.1.call-start = ((), (), s32[]{:S(2)}) async-start(), calls=%async_computation.7 | async-start | bytes 4866048 | tf_op jit(solution)/shard_map/reduce_scatter | solution.py:1114
  355.6 44.0 %collective-permute-start.29 = (bf16[384,1408]{1,0:T(8,128)(2,1)S(1)}, bf16[384,1408]{1,0:T(8,128)(2,1)}, u32[]{:S(2)}, u32[]{:S(2)}) collective-permute-start(bf16[384,1408]{1,0:T(8,128)(2,1)S(1)} %copy-done.22), channel_id=1, source_target_pairs={{0,1},{1,0},{2,3},{3,2},{4,5},{5,4},{6,7},{7,6},{8,9},{9,8},{10,11... | collective-permute-start | bytes 3244040 | tf_op jit(solution)/shard_map/ppermute | solution.py:452
  452.8 45.0 %collective-permute-start.36 = (bf16[2816,352]{0,1:T(8,128)(2,1)}, bf16[2816,352]{0,1:T(8,128)(2,1)S(1)}, u32[]{:S(2)}, u32[]{:S(2)}) collective-permute-start(bf16[2816,352]{0,1:T(8,128)(2,1)} %copy.92), channel_id=1, source_target_pairs={{0,2},{1,3},{2,0},{3,1},{4,6},{5,7},{6,4},{7,5},{8,10},{9,11},{10,... | collective-permute-start | bytes 5947400 | tf_op jit(solution)/shard_map/ppermute | solution.py:452
  454.3 55.4 %collective-permute-start.35 = (bf16[2816,352]{0,1:T(8,128)(2,1)}, bf16[2816,352]{0,1:T(8,128)(2,1)S(1)}, u32[]{:S(2)}, u32[]{:S(2)}) collective-permute-start(bf16[2816,352]{0,1:T(8,128)(2,1)} %copy.92), channel_id=1, source_target_pairs={{0,1},{1,0},{2,3},{3,2},{4,5},{5,4},{6,7},{7,6},{8,9},{9,8},{10,11... | collective-permute-start | bytes 5947400 | tf_op jit(solution)/shard_map/ppermute | solution.py:452
  539.7 274.4 %reduce-scatter.6.cloned.1.call-start = ((), (), s32[]{:S(2)}) async-start(), calls=%async_computation.8 | async-start | bytes 4866048 | tf_op jit(solution)/shard_map/reduce_scatter | solution.py:1109
  604.4 59.5 %collective-permute-start.46 = (bf16[8,2,112,1408]{3,2,1,0:T(8,128)(2,1)}, bf16[8,2,112,1408]{3,2,1,0:T(8,128)(2,1)}, u32[]{:S(2)}, u32[]{:S(2)}) collective-permute-start(bf16[8,2,112,1408]{3,2,1,0:T(8,128)(2,1)} %dynamic-slice_bitcast_fusion), channel_id=1, source_target_pairs={{0,1},{1,0},{2,3},{3,2},{4,5},{5,4},{6,7},{7,6},{8,9},{9,8},{10,11... | collective-permute-start | bytes 15138824 | tf_op jit(solution)/shard_map/ppermute | solution.py:452
  625.3 372.7 %reduce-scatter.8.cloned.1.call-start = ((), (), s32[]{:S(2)}) async-start(), calls=%async_computation.9 | async-start | bytes 4866048 | tf_op jit(solution)/shard_map/reduce_scatter | solution.py:1152
  673.5 54.8 %collective-permute-start.48 = (bf16[8,1,112,1408]{3,2,1,0:T(8,128)(2,1)}, bf16[8,1,112,1408]{3,2,1,0:T(8,128)(2,1)}, u32[]{:S(2)}, u32[]{:S(2)}) collective-permute-start(bf16[8,1,112,1408]{3,2,1,0:T(8,128)(2,1)} %constant_dynamic-slice_fusion.6), channel_id=1, source_target_pairs={{0,2},{1,3},{2,0},{3,1},{4,6},{5,7},{6,4},{7,5},{8,10},{9,11},{10,... | collective-permute-start | bytes 7569416 | tf_op jit(solution)/shard_map/ppermute | solution.py:452
  675.0 47.5 %collective-permute-start.49 = (bf16[8,2,48,1408]{3,2,1,0:T(8,128)(2,1)}, bf16[8,2,48,1408]{3,2,1,0:T(8,128)(2,1)}, u32[]{:S(2)}, u32[]{:S(2)}) collective-permute-start(bf16[8,2,48,1408]{3,2,1,0:T(8,128)(2,1)} %dynamic-slice_bitcast_fusion.1), channel_id=1, source_target_pairs={{0,1},{1,0},{2,3},{3,2},{4,5},{5,4},{6,7},{7,6},{8,9},{9,8},{10,11... | collective-permute-start | bytes 6488072 | tf_op jit(solution)/shard_map/ppermute | solution.py:452
  681.1 41.4 %collective-permute-start.47 = (bf16[2,2,48,1408]{3,2,1,0:T(8,128)(2,1)}, bf16[2,2,48,1408]{3,2,1,0:T(8,128)(2,1)}, u32[]{:S(2)}, u32[]{:S(2)}) collective-permute-start(bf16[2,2,48,1408]{3,2,1,0:T(8,128)(2,1)} %dynamic-slice_bitcast_fusion.8), channel_id=1, source_target_pairs={{0,8},{4,12},{8,0},{12,4},{16,24},{20,28},{24,16},{28,20},{1,9},{5... | collective-permute-start | bytes 1622024 | tf_op jit(solution)/shard_map/ppermute | solution.py:452
  728.3 85.8 %collective-permute-start.56 = (bf16[176,1536]{1,0:T(8,128)(2,1)}, bf16[176,1536]{1,0:T(8,128)(2,1)}, u32[]{:S(2)}, u32[]{:S(2)}) collective-permute-start(bf16[176,1536]{1,0:T(8,128)(2,1)} %reduce-scatter.4.cloned.1.call-done.refs_0_), channel_id=1, source_target_pairs={{0,1},{1,0},{2,3},{3,2},{4,5},{5,4},{6,7},{7,6},{8,9},{9,8},{10,11... | collective-permute-start | bytes 1622024 | tf_op jit(solution)/shard_map/ppermute | solution.py:452
  731.0 83.2 %collective-permute-start.57 = (bf16[176,1536]{1,0:T(8,128)(2,1)}, bf16[176,1536]{1,0:T(8,128)(2,1)}, u32[]{:S(2)}, u32[]{:S(2)}) collective-permute-start(bf16[176,1536]{1,0:T(8,128)(2,1)} %reduce-scatter.4.cloned.1.call-done.refs_0_), channel_id=1, source_target_pairs={{0,2},{1,3},{2,0},{3,1},{4,6},{5,7},{6,4},{7,5},{8,10},{9,11},{10,... | collective-permute-start | bytes 1622024 | tf_op jit(solution)/shard_map/ppermute | solution.py:452
  789.0 44.7 %collective-permute-start.55 = (bf16[384,1408]{1,0:T(8,128)(2,1)}, bf16[384,1408]{1,0:T(8,128)(2,1)}, u32[]{:S(2)}, u32[]{:S(2)}) collective-permute-start(bf16[384,1408]{1,0:T(8,128)(2,1)} %add_convert_fusion.3), channel_id=1, source_target_pairs={{0,2},{1,3},{2,0},{3,1},{4,6},{5,7},{6,4},{7,5},{8,10},{9,11},{10,... | collective-permute-start | bytes 3244040 | tf_op jit(solution)/shard_map/ppermute | solution.py:452
  794.5 84.0 %collective-permute-start.63 = (bf16[4,2,48,1408]{3,2,1,0:T(8,128)(2,1)}, bf16[4,2,48,1408]{3,2,1,0:T(8,128)(2,1)}, u32[]{:S(2)}, u32[]{:S(2)}) collective-permute-start(bf16[4,2,48,1408]{3,2,1,0:T(8,128)(2,1)} %dynamic-slice_bitcast_fusion.4), channel_id=1, source_target_pairs={{0,4},{4,0},{8,12},{12,8},{16,20},{20,16},{24,28},{28,24},{1,5},{5... | collective-permute-start | bytes 3244040 | tf_op jit(solution)/shard_map/ppermute | solution.py:452
  810.5 68.0 %collective-permute-start.62 = (bf16[4,1,112,1408]{3,2,0,1:T(8,128)(2,1)}, bf16[4,1,112,1408]{3,2,0,1:T(8,128)(2,1)}, u32[]{:S(2)}, u32[]{:S(2)}) collective-permute-start(bf16[4,1,112,1408]{3,2,0,1:T(8,128)(2,1)} %dynamic-slice_bitcast_fusion.3), channel_id=1, source_target_pairs={{0,4},{4,0},{8,12},{12,8},{16,20},{20,16},{24,28},{28,24},{1,5},{5... | collective-permute-start | bytes 3784712 | tf_op jit(solution)/shard_map/ppermute | solution.py:452
  881.4 41.7 %collective-permute-start.71 = (bf16[2,2,48,1408]{3,2,1,0:T(8,128)(2,1)}, bf16[2,2,48,1408]{3,2,1,0:T(8,128)(2,1)}, u32[]{:S(2)}, u32[]{:S(2)}) collective-permute-start(bf16[2,2,48,1408]{3,2,1,0:T(8,128)(2,1)} %dynamic-slice_bitcast_fusion.7), channel_id=1, source_target_pairs={{0,8},{4,12},{8,0},{12,4},{16,24},{20,28},{24,16},{28,20},{1,9},{5... | collective-permute-start | bytes 1622024 | tf_op jit(solution)/shard_map/ppermute | solution.py:452
  (228 other events, 3957.7 us)
Sparse Core Ops, SparseCore 0:
  10.8 61.6 all-gather.4
  75.3 83.3 all-gather.6
  279.1 78.7 all-gather.8
  360.5 73.8 all-gather.10
  539.8 88.9 reduce-scatter.3
  632.7 93.1 reduce-scatter.5
  789.1 124.3 reduce-scatter.7

commit v6 on v5

--- a/solution.py
+++ b/solution.py
@@ -1041,7 +1041,7 @@
     shifts = scatter_small(matmul(cond_rows, w_mod), "dp")
     time_shift = jnp.sum(jnp.where(member[:, :, None], shifts[None], 0.0), axis=1)
 
-    x_one, time_shift = advance((x_one, time_shift), ways[:1])
+    x_one, time_shift = advance((x_one, time_shift), ways)
     n_float, pull_one = jax.vjp(layer_norm, x_one, ln_gains[2], ln_biases[2])
     n_one = (n_float + time_shift).astype(jnp.bfloat16)
     n_one_blocks, w_down = advance((blocks_of(n_one, "seq"), w_down), ways)
@@ -1056,6 +1056,14 @@
     out_blocks = head_out.reshape(seq_count, local_tok, head_cols)
     attn_o = join_columns(exchange([out_blocks[k] for k in seq_range], "seq"), ranks, jnp.bfloat16)
     attn_o = advance(attn_o, ways)
+    if aligned(w_ckv.shape[0]):
+        ckv_rows = w_ckv.shape[0]
+        quarters = [q.reshape(dp_count, -1, w_ckv.shape[1]) for q in ckv_way.finish()]
+        (full_ckv,) = place_quarters(
+            quarters, ranks, [ckv_rows], [share_of(ckv_rows, seq_count)], dp_bits
+        )
+    else:
+        full_ckv = lax.all_gather(w_ckv, "dp", axis=0, tiled=True)
     if aligned(row_count):
         full_out, full_cq, full_co = place_quarters(
             square_way.finish(),
@@ -1071,16 +1079,8 @@
     x_two = x_one + matmul(attn_o, full_out)
     n3_float, pull_three = jax.vjp(layer_norm, x_two, ln_gains[3], ln_biases[3])
     n_three = n3_float.astype(jnp.bfloat16)
-    n_three, cotangent = advance((n_three, cotangent), ways)
+    n_three, cotangent = lax.optimization_barrier((n_three, cotangent))
     cross_q = matmul(n_three, full_cq).astype(jnp.bfloat16)
-    if aligned(w_ckv.shape[0]):
-        ckv_rows = w_ckv.shape[0]
-        quarters = [q.reshape(dp_count, -1, w_ckv.shape[1]) for q in ckv_way.finish()]
-        (full_ckv,) = place_quarters(
-            quarters, ranks, [ckv_rows], [share_of(ckv_rows, seq_count)], dp_bits
-        )
-    else:
-        full_ckv = lax.all_gather(w_ckv, "dp", axis=0, tiled=True)
     text_kv = matmul(caption_rows, full_ckv).astype(jnp.bfloat16)
     seg_row = seg_local[None]
     span = jnp.stack([seg_local[0], seg_local[-1]])
@@ -1092,9 +1092,9 @@
     x_three = x_two + matmul(cross_o, full_co)
     n2_float, pull_two = jax.vjp(layer_norm, x_three, ln_gains[4], ln_biases[4])
     n_two = n2_float.astype(jnp.bfloat16)
-    n_two_blocks, part_skip, part_down, cot_all = lax.optimization_barrier(
-        (blocks_of(n_two, "seq"), part_skip, part_down, cot_all)
-    )
+    n_two_way = Gather(n_two, [("seq", seq_bits, False)])
+    cot_all, part_down = advance((cot_all, part_down), [n_two_way])
+    n_two_blocks, part_skip = lax.optimization_barrier((n_two_way.finish(), part_skip))
     n_two_all = jnp.concatenate(n_two_blocks, axis=0)
     skip_blocks = blocks_of(part_skip, "seq")
     up_proj = matmul(n_two_all, part_up)
@@ -1152,9 +1152,8 @@
     total_qkv = lax.psum_scatter(grad_qkv, "dp", scatter_dimension=0, tiled=True)
     d_n_one = sum_parts([d_one_part[k] for k in seq_range], "seq", jnp.bfloat16)
     d_n_one, total_down = advance(
-        (d_n_one, total_down), [block_way, up_way]
-    )
-    block_out = (x_three + block_way.total()).astype(jnp.bfloat16)
+        (d_n_one, total_down), []
+    )
     down_way = Gather(total_down, [("seq", seq_bits, False)])
     back_one_x, gain_one, bias_one = pull_one(d_n_one)
     d_x_one = d_x_two + back_one_x
@@ -1163,7 +1162,7 @@
     y_cols = jnp.concatenate(exchange(y_blocks, "seq"), axis=0)
     grad_skip_w = matmul(h_all.T, y_cols).astype(jnp.bfloat16)
     grad_skip_w, d_n_one, y_blocks = lax.optimization_barrier((grad_skip_w, d_n_one, y_blocks))
-    moving = scatters + [up_way, down_way]
+    moving = scatters + [up_way, down_way, block_way]
     first_moving = moving
     if aligned(skip_rows):
         skip_scatter = PartScatter(grad_skip_w, ranks)
@@ -1219,6 +1218,7 @@
     grad_down, grad_up = advance((grad_down, grad_up), moving)
     if aligned(skip_rows):
         total_skip = skip_scatter.total()
+    block_out = (x_three + block_way.total()).astype(jnp.bfloat16)
     share, ckv_share = share_of(row_count, seq_count), share_of(w_ckv.shape[0], seq_count)
     square = (row_count, model_width)
     grad_co, grad_cq, grad_ckv, grad_out = put_rows(

time: 1060 us -> 1040 us (0.981)
  starting transfers between devices: 138 us -> 116 us
  waiting for transfers between devices: 293 us -> 304 us
    all_gather x1, waiting for transfers between devices: 0.01 us -> 38.8 us  [shards(): part_down = lax.all_gather(own_down, 'dp', axis=0, tiled=True)]
    ppermute x91, waiting for transfers between devices: 293 us -> 265 us  [swap(): lax.ppermute(value, axis, [(rank, rank ^ mask) for rank in range(count)])]
    ppermute x91, starting transfers between devices: 137 us -> 115 us  [swap(): lax.ppermute(value, axis, [(rank, rank ^ mask) for rank in range(count)])]
    unnamed x331 -> x315, local copies, waits for them, and re-layouts: 32.9 us -> 32.7 us
  transfers between devices with their start and end apart: 98 -> 98, of which waited for: 33 -> 33; matrix products, arithmetic and copies ran while one was open for 37% -> 37% of each run, Pallas kernels for 17% -> 18%
where the time goes in v6:
time: 1040 us; the launch traced here: 1030 us
  waiting for transfers between devices  304 us (29%)
  Pallas kernels  186 us (18%)
  matrix products  184 us (18%)
  other arithmetic  119 us (11%)
  starting transfers between devices  116 us (11%)
  local copies, waits for them, and re-layouts  106 us (10%)
  between operations  16.4 us (2%)
    ppermute x91, waiting for transfers between devices, swap(): lax.ppermute(value, axis, [(rank, rank ^ mask) for rank in range(count)])  265 us
    dot_general x24, matrix products, matmul(): return jnp.dot(left, right, preferred_element_type=jnp.float32)  175 us
    ppermute x91, starting transfers between devices, swap(): lax.ppermute(value, axis, [(rank, rank ^ mask) for rank in range(count)])  115 us
    all_gather x1, waiting for transfers between devices, shards(): part_down = lax.all_gather(own_down, 'dp', axis=0, tiled=True)  38.8 us
    pallas_call x1, Pallas kernels, self_backward(): pl.pallas_call(functools.partial(self_backward_kernel, heads, blocks), gr...  37.8 us
    unnamed x315, local copies, waits for them, and re-layouts  32.7 us
    convert_element_type x12, other arithmetic, step(): self.held, self.came = (total.astype(jnp.bfloat16), None)  25.6 us
    pallas_call x2, Pallas kernels, place_quarters(): pl.pallas_call(functools.partial(quarter_kernel, row_counts, shares), gri...  21.1 us
  transfers between devices with their start and end apart: 98, of which 33 were waited for; matrix products, arithmetic and copies ran while one was open for 37% of the time, Pallas kernels for 18%

profile of v6, /device:TPU:1, one launch (start us, length us, event | category | flops | bytes accessed | tf_op | source)
XLA Modules:
  0.0 1030.6 jit_solution(1830170486315878210)
XLA Ops:
  54.6 21.3 %collective-permute-done.3 = bf16[1,32,2816]{2,1,0:T(8,128)(2,1)S(1)} collective-permute-done((bf16[1,32,2816]{2,1,0:T(8,128)(2,1)S(1)}, bf16[1,32,2816]{2,1,0:T(8,128)(2,1)S(1)}, u32[]{:S(2)}, u32[]{:S(2)}) %collective-permute-start.3) | collective-permute-done | bytes 180256 | tf_op jit(solution)/shard_map/ppermute | solution.py:452
  102.9 9.6 convolution_convert_fusion.12
  153.7 13.6 %collective-permute-done.17 = bf16[384,1408]{1,0:T(8,128)(2,1)} collective-permute-done((bf16[384,1408]{1,0:T(8,128)(2,1)}, bf16[384,1408]{1,0:T(8,128)(2,1)}, u32[]{:S(2)}, u32[]{:S(2)}) %collective-permute-start.17) | collective-permute-done | bytes 1081376 | tf_op jit(solution)/shard_map/ppermute | solution.py:452
  174.7 15.7 %collective-permute-done.20 = bf16[2,2,32,2816]{3,2,1,0:T(8,128)(2,1)S(1)} collective-permute-done((bf16[2,2,32,2816]{3,2,1,0:T(8,128)(2,1)}, bf16[2,2,32,2816]{3,2,1,0:T(8,128)(2,1)S(1)}, u32[]{:S(2)}, u32[]{:S(2)}) %collective-permute-start.20) | collective-permute-done | bytes 720928 | tf_op jit(solution)/shard_map/ppermute | solution.py:452
  207.3 12.8 %fusion.90.pre_ref = f32[1536,1536]{1,0:T(8,128)} fusion(bf16[1536,1408]{1,0:T(8,128)(2,1)} %constant_dynamic-update-slice_fusion, bf16[1408,1536]{1,0:T(8,128)(2,1)} %all-gather.7.cloned.1.call-done), kind=kOutput, calls=%fused_computation.282 | convolution fusion | flops 6643777536 | bytes 18087936 | tf_op jit(solution)/shard_map/dot_general | solution.py:35
  220.1 15.3 %shard_map.389.q_ref.k_ref.v_ref = bf16[1536,1536]{1,0:T(8,128)(2,1)} custom-call(f32[1536,1536]{1,0:T(8,128)} %fusion.90.pre_ref, f32[1536,128]{1,0:T(8,128)} %get-tuple-element.172.cos_ref, f32[1536,128]{1,0:T(8,128)} %get-tuple-element.173.sa_ref, f32[1536,128]{1,0:T(8,128)} %get-tuple-element.174.sb_ref, s32[1536,1]{1,0:T(8,128)} %copy.90.seg_ref, ...), custom_call_target="tpu_custom_call" | custom-call | flops 47185920 | bytes 18874368 | tf_op jit(solution)/shard_map/pallas_call | solution.py:94
  235.4 18.7 %shard_map.390 = (bf16[1536,352]{1,0:T(8,128)(2,1)}, f32[4,1536]{1,0:T(4,128)}) custom-call(bf16[1536,1536]{1,0:T(8,128)(2,1)} %shard_map.389.q_ref.k_ref.v_ref, bf16[1536,1536]{1,0:T(8,128)(2,1)} %shard_map.389.q_ref.k_ref.v_ref, bf16[1536,1536]{1,0:T(8,128)(2,1)} %shard_map.389.q_ref.k_ref.v_ref), custom_call_target="tpu_custom_call" | custom-call | flops 4831838208 | bytes 6291456 | tf_op jit(solution)/shard_map/pallas_call | solution.py:140
  254.1 12.7 %collective-permute-done.22.refs_2_ = bf16[8,144,1408]{2,1,0:T(8,128)(2,1)} collective-permute-done((bf16[8,144,1408]{2,1,0:T(8,128)(2,1)}, bf16[8,144,1408]{2,1,0:T(8,128)(2,1)}, u32[]{:S(2)}, u32[]{:S(2)}) %collective-permute-start.22) | collective-permute-done | bytes 3244064 | tf_op jit(solution)/shard_map/ppermute | solution.py:452
  290.9 12.4 %shard_map.392 = (bf16[1408,1408]{1,0:T(8,128)(2,1)}, bf16[1408,1408]{1,0:T(8,128)(2,1)}, bf16[1408,1408]{1,0:T(8,128)(2,1)}) custom-call(s32[2]{0:T(128)} %pad_add_fusion.ranks_ref, bf16[8,144,1408]{2,1,0:T(8,128)(2,1)} %pad_maximum_fusion.3.refs_0_, bf16[8,144,1408]{2,1,0:T(8,128)(2,1)} %collective-permute-done.21.refs_1_, ...), custom_call_target="tpu_custom_call" | custom-call | bytes 23789568 | tf_op jit(solution)/shard_map/pallas_call | solution.py:617
  318.0 8.8 shard_map.393
  336.3 10.5 %convolution_convert_fusion.10.kv_ref = bf16[1008,2816]{1,0:T(8,128)(2,1)} fusion(bf16[1008,1024]{1,0:T(8,128)(2,1)S(1)} %bitcast.187, bf16[1024,2816]{1,0:T(8,128)(2,1)} %shard_map.393), kind=kOutput, calls=%fused_computation.31 | convolution fusion | flops 5816143872 | bytes 13508608 | tf_op jit(solution)/shard_map/dot_general | solution.py:35
  349.7 11.1 %shard_map.394 = (bf16[384,1408]{1,0:T(8,128)(2,1)}, f32[16,384]{1,0:T(8,128)}, f32[16,384]{1,0:T(8,128)}) custom-call(s32[2]{0:T(128)} %pad_add_fusion.1.span_ref, bf16[384,1408]{1,0:T(8,128)(2,1)} %convolution_convert_fusion.15.q_ref, bf16[1008,2816]{1,0:T(8,128)(2,1)} %convolution_convert_fusion.10.kv_ref, bf16[1008,1]{1,0:T(8,128)(2,1)} %copy.91.pen_ref, ...), custom_call_target="tpu_custom_call" | custom-call | flops 2113929216 | bytes 10002432 | tf_op jit(solution)/shard_map/pallas_call | solution.py:336
  382.9 38.8 %all-gather.11.cloned.1.call-done = bf16[1536,1408]{1,0:T(8,128)(2,1)} async-done(((bf16[192,1408]{1,0:T(8,128)(2,1)}), bf16[1536,1408]{1,0:T(8,128)(2,1)}) %all-gather.11.cloned.1.call-update) | async-done | bytes 4325392 | tf_op jit(solution)/shard_map/all_gather | solution.py:1049
  437.9 14.1 %fusion.91 = f32[1536,1536]{1,0:T(8,128)} fusion(bf16[1536,1408]{1,0:T(8,128)(2,1)S(1)} %constant_dynamic-update-slice_fusion.4, bf16[1408,1536]{1,0:T(8,128)(2,1)} %all-gather.9.cloned.1.call-done), kind=kOutput, calls=%fused_computation.283 | convolution fusion | flops 6643777536 | bytes 18087936 | tf_op jit(solution)/shard_map/dot_general | solution.py:35
  452.1 16.6 %fusion.4 = bf16[1536,1536]{1,0:T(8,128)(2,1)} fusion(f32[1536,1536]{1,0:T(8,128)} %fusion.91, bf16[1536,1408]{1,0:T(8,128)(2,1)S(1)} %bitcast.178, bf16[1536,1408]{1,0:T(8,128)(2,1)S(1)} %bitcast.198), kind=kOutput, calls=%fused_computation.14 | convolution fusion | flops 6700400640 | bytes 22806528 | tf_op jit(solution)/shard_map/dot_general | solution.py:35
  476.3 11.0 %convolution_convert_fusion.5 = bf16[1536,1408]{1,0:T(8,128)(2,1)S(1)} fusion(bf16[1536,1536]{1,0:T(8,128)(2,1)} %fusion.4, bf16[1408,1536]{1,0:T(8,128)(2,1)} %all-gather.9.cloned.1.call-done), kind=kOutput, calls=%fused_computation.24 | convolution fusion | flops 6645940224 | bytes 13369344 | tf_op jit(solution)/shard_map/dot_general | solution.py:35
  491.4 9.6 convolution_convert_fusion.3
  505.6 11.6 %convolution_convert_fusion.4 = bf16[1408,1536]{1,0:T(8,128)(2,1)} fusion(bf16[1536,1408]{1,0:T(8,128)(2,1)} %copy-done.89, bf16[1536,1536]{1,0:T(8,128)(2,1)} %fusion.4), kind=kOutput, calls=%fused_computation.23 | convolution fusion | flops 6645940224 | bytes 13369344 | tf_op jit(solution)/shard_map/dot_general | solution.py:35
  517.7 12.5 %collective-permute-done.40 = bf16[384,1408]{1,0:T(8,128)(2,1)} collective-permute-done((bf16[384,1408]{1,0:T(8,128)(2,1)}, bf16[384,1408]{1,0:T(8,128)(2,1)}, u32[]{:S(2)}, u32[]{:S(2)}) %collective-permute-start.40) | collective-permute-done | bytes 1081376 | tf_op jit(solution)/shard_map/ppermute | solution.py:452
  546.7 15.4 %shard_map.395 = (bf16[384,1408]{1,0:T(8,128)(2,1)}, bf16[1008,2816]{1,0:T(8,128)(2,1)}) custom-call(s32[2]{0:T(128)} %pad_add_fusion.1.span_ref, bf16[384,1408]{1,0:T(8,128)(2,1)} %convolution_convert_fusion.15.q_ref, bf16[1008,2816]{1,0:T(8,128)(2,1)} %convolution_convert_fusion.10.kv_ref, bf16[1008,1]{1,0:T(8,128)(2,1)} %copy.91.pen_ref, ...), custom_call_target="tpu_custom_call" | custom-call | flops 5284823040 | bytes 15679488 | tf_op jit(solution)/shard_map/pallas_call | solution.py:398
  562.2 9.4 convolution_convert_fusion.9
  582.0 9.0 collective-permute-start.46
  591.1 11.9 %convolution_convert_fusion.2 = bf16[1536,1408]{1,0:T(8,128)(2,1)} fusion(bf16[1536,1408]{1,0:T(8,128)(2,1)S(1)} %bitcast.200, f32[1536,1536]{1,0:T(8,128)} %fusion.91), kind=kOutput, calls=%fused_computation.21 | convolution fusion | flops 6667173888 | bytes 18087936 | tf_op jit(solution)/shard_map/dot_general | solution.py:35
  662.9 37.8 %shard_map.397 = (bf16[1536,512]{1,0:T(8,128)(2,1)}, bf16[1536,512]{1,0:T(8,128)(2,1)}, bf16[1536,512]{1,0:T(8,128)(2,1)}) custom-call(bf16[1536,1536]{1,0:T(8,128)(2,1)} %shard_map.389.q_ref.k_ref.v_ref, bf16[1536,1536]{1,0:T(8,128)(2,1)} %shard_map.389.q_ref.k_ref.v_ref, bf16[1536,1536]{1,0:T(8,128)(2,1)} %shard_map.389.q_ref.k_ref.v_ref, ...), custom_call_target="tpu_custom_call" | custom-call | flops 12079595520 | bytes 11010048 | tf_op jit(solution)/shard_map/pallas_call | solution.py:197
  705.7 17.9 %shard_map.398 = (bf16[1536,1536]{1,0:T(8,128)(2,1)}, f32[2,128]{1,0:T(2,128)}, f32[2,128]{1,0:T(2,128)}) custom-call(f32[1536,1536]{1,0:T(8,128)} %fusion.90.pre_ref, bf16[1536,512]{1,0:T(8,128)(2,1)} %get-tuple-element.231.dq_ref, bf16[1536,512]{1,0:T(8,128)(2,1)} %get-tuple-element.232.dk_ref, bf16[1536,512]{1,0:T(8,128)(2,1)} %get-tuple-element.233.dv_ref, ...), custom_call_target="tpu_custom_call" | custom-call | flops 47185920 | bytes 23592960 | tf_op jit(solution)/shard_map/pallas_call | solution.py:256
  723.6 10.7 %convolution_convert_fusion.1 = bf16[1536,1408]{1,0:T(8,128)(2,1)S(1)} fusion(bf16[1536,1536]{1,0:T(8,128)(2,1)} %get-tuple-element.234, bf16[1408,1536]{1,0:T(8,128)(2,1)} %all-gather.7.cloned.1.call-done), kind=kOutput, calls=%fused_computation.20 | convolution fusion | flops 6645940224 | bytes 13369344 | tf_op jit(solution)/shard_map/dot_general | solution.py:35
  741.5 11.0 %convolution_convert_fusion = bf16[1408,1536]{1,0:T(8,128)(2,1)} fusion(bf16[1536,1408]{1,0:T(8,128)(2,1)} %constant_dynamic-update-slice_fusion, bf16[1536,1536]{1,0:T(8,128)(2,1)S(1)} %copy-done.133), kind=kOutput, calls=%fused_computation.19 | convolution fusion | flops 6645940224 | bytes 13369344 | tf_op jit(solution)/shard_map/dot_general | solution.py:35
  770.3 18.6 %collective-permute-done.54 = bf16[384,1408]{1,0:T(8,128)(2,1)S(1)} collective-permute-done((bf16[384,1408]{1,0:T(8,128)(2,1)S(1)}, bf16[384,1408]{1,0:T(8,128)(2,1)S(1)}, u32[]{:S(2)}, u32[]{:S(2)}) %collective-permute-start.54) | collective-permute-done | bytes 1081376 | tf_op jit(solution)/shard_map/ppermute | solution.py:452
  840.0 10.1 collective-permute-done.65
  850.1 22.5 %collective-permute-done.59 = bf16[4,1,112,1408]{3,2,0,1:T(8,128)(2,1)} collective-permute-done((bf16[4,1,112,1408]{3,2,0,1:T(8,128)(2,1)S(1)}, bf16[4,1,112,1408]{3,2,0,1:T(8,128)(2,1)}, u32[]{:S(2)}, u32[]{:S(2)}) %collective-permute-start.59) | collective-permute-done | bytes 1261600 | tf_op jit(solution)/shard_map/ppermute | solution.py:452
  910.0 9.5 collective-permute-done.67.refs_1_.refs_3_
  938.7 22.6 %collective-permute-done.78 = bf16[1,352,352]{2,1,0:T(8,128)(2,1)} collective-permute-done((bf16[1,352,352]{2,1,0:T(8,128)(2,1)}, bf16[1,352,352]{2,1,0:T(8,128)(2,1)}, u32[]{:S(2)}, u32[]{:S(2)}) %collective-permute-start.78) | collective-permute-done | bytes 247840 | tf_op jit(solution)/shard_map/ppermute | solution.py:452
  (738 shorter events, 531.2 us)
Async XLA Ops:
  7.2 95.6 %all-gather.5.cloned.1.call-start = ((), (), s32[]{:S(2)}) async-start(), calls=%async_computation.3 | async-start | bytes 2433024 | tf_op jit(solution)/shard_map/all_gather | solution.py:982
  9.3 198.0 %all-gather.7.cloned.1.call-start = ((), (), s32[]{:S(2)}) async-start(), calls=%async_computation.4 | async-start | bytes 4866048 | tf_op jit(solution)/shard_map/all_gather | solution.py:984
  21.8 54.2 %collective-permute-start = (bf16[384,2816]{1,0:T(8,128)(2,1)}, bf16[384,2816]{1,0:T(8,128)(2,1)}, u32[]{:S(2)}, u32[]{:S(2)}) collective-permute-start(bf16[384,2816]{1,0:T(8,128)(2,1)} %fusion.16), channel_id=1, source_target_pairs={{0,1},{1,0},{2,3},{3,2},{4,5},{5,4},{6,7},{7,6},{8,9},{9,8},{10,11... | collective-permute-start | bytes 6488072 | tf_op jit(solution)/shard_map/ppermute | solution.py:452
  21.8 54.2 %collective-permute-start.1 = (bf16[384,2816]{1,0:T(8,128)(2,1)}, bf16[384,2816]{1,0:T(8,128)(2,1)}, u32[]{:S(2)}, u32[]{:S(2)}) collective-permute-start(bf16[384,2816]{1,0:T(8,128)(2,1)} %fusion.16), channel_id=1, source_target_pairs={{0,2},{1,3},{2,0},{3,1},{4,6},{5,7},{6,4},{7,5},{8,10},{9,11},{10,... | collective-permute-start | bytes 6488072 | tf_op jit(solution)/shard_map/ppermute | solution.py:452
  24.6 51.4 %collective-permute-start.2 = (bf16[1,144,1408]{2,1,0:T(8,128)(2,1)}, bf16[1,144,1408]{2,1,0:T(8,128)(2,1)S(1)}, u32[]{:S(2)}, u32[]{:S(2)}) collective-permute-start(bf16[1,144,1408]{2,1,0:T(8,128)(2,1)} %bitcast.7), channel_id=1, source_target_pairs={{0,16},{4,20},{8,24},{12,28},{16,0},{20,4},{24,8},{28,12},{1,17},{... | collective-permute-start | bytes 1216520 | tf_op jit(solution)/shard_map/ppermute | solution.py:452
  26.9 49.1 %collective-permute-start.3 = (bf16[1,32,2816]{2,1,0:T(8,128)(2,1)S(1)}, bf16[1,32,2816]{2,1,0:T(8,128)(2,1)S(1)}, u32[]{:S(2)}, u32[]{:S(2)}) collective-permute-start(bf16[1,32,2816]{2,1,0:T(8,128)(2,1)S(1)} %bitcast.189), channel_id=1, source_target_pairs={{0,2},{1,3},{2,0},{3,1},{4,6},{5,7},{6,4},{7,5},{8,10},{9,11},{10,... | collective-permute-start | bytes 540680 | tf_op jit(solution)/shard_map/ppermute | solution.py:452
  28.3 332.5 %all-gather.9.cloned.1.call-start = ((), (), s32[]{:S(2)}) async-start(), calls=%async_computation.5 | async-start | bytes 4866048 | tf_op jit(solution)/shard_map/all_gather | solution.py:1055
  96.2 41.3 %collective-permute-start.14 = (bf16[2,144,1408]{2,1,0:T(8,128)(2,1)}, bf16[2,144,1408]{2,1,0:T(8,128)(2,1)}, u32[]{:S(2)}, u32[]{:S(2)}) collective-permute-start(bf16[2,144,1408]{2,1,0:T(8,128)(2,1)} %pad_maximum_fusion.12), channel_id=1, source_target_pairs={{0,8},{4,12},{8,0},{12,4},{16,24},{20,28},{24,16},{28,20},{1,9},{5... | collective-permute-start | bytes 2433032 | tf_op jit(solution)/shard_map/ppermute | solution.py:452
  148.5 41.9 %collective-permute-start.19 = (bf16[4,144,1408]{2,1,0:T(8,128)(2,1)}, bf16[4,144,1408]{2,1,0:T(8,128)(2,1)}, u32[]{:S(2)}, u32[]{:S(2)}) collective-permute-start(bf16[4,144,1408]{2,1,0:T(8,128)(2,1)} %pad_maximum_fusion.7), channel_id=1, source_target_pairs={{0,4},{4,0},{8,12},{12,8},{16,20},{20,16},{24,28},{28,24},{1,5},{5... | collective-permute-start | bytes 4866056 | tf_op jit(solution)/shard_map/ppermute | solution.py:452
  193.9 60.2 %collective-permute-start.21 = (bf16[8,144,1408]{2,1,0:T(8,128)(2,1)}, bf16[8,144,1408]{2,1,0:T(8,128)(2,1)}, u32[]{:S(2)}, u32[]{:S(2)}) collective-permute-start(bf16[8,144,1408]{2,1,0:T(8,128)(2,1)} %pad_maximum_fusion.3.refs_0_), channel_id=1, source_target_pairs={{0,1},{1,0},{2,3},{3,2},{4,5},{5,4},{6,7},{7,6},{8,9},{9,8},{10,11... | collective-permute-start | bytes 9732104 | tf_op jit(solution)/shard_map/ppermute | solution.py:452
  194.7 72.2 %collective-permute-start.22 = (bf16[8,144,1408]{2,1,0:T(8,128)(2,1)}, bf16[8,144,1408]{2,1,0:T(8,128)(2,1)}, u32[]{:S(2)}, u32[]{:S(2)}) collective-permute-start(bf16[8,144,1408]{2,1,0:T(8,128)(2,1)} %pad_maximum_fusion.3.refs_0_), channel_id=1, source_target_pairs={{0,2},{1,3},{2,0},{3,1},{4,6},{5,7},{6,4},{7,5},{8,10},{9,11},{10,... | collective-permute-start | bytes 9732104 | tf_op jit(solution)/shard_map/ppermute | solution.py:452
  197.0 57.1 %collective-permute-start.23 = (bf16[4,2,32,2816]{3,2,1,0:T(8,128)(2,1)}, bf16[4,2,32,2816]{3,2,1,0:T(8,128)(2,1)}, u32[]{:S(2)}, u32[]{:S(2)}) collective-permute-start(bf16[4,2,32,2816]{3,2,1,0:T(8,128)(2,1)} %pad_maximum_fusion.10), channel_id=1, source_target_pairs={{0,4},{4,0},{8,12},{12,8},{16,20},{20,16},{24,28},{28,24},{1,5},{5... | collective-permute-start | bytes 4325384 | tf_op jit(solution)/shard_map/ppermute | solution.py:452
  266.9 154.8 %all-gather.11.cloned.1.call-start = ((), (), s32[]{:S(2)}) async-start(), calls=%async_computation.6 | async-start | bytes 4866048 | tf_op jit(solution)/shard_map/all_gather | solution.py:1049
  274.7 426.1 %reduce-scatter.4.cloned.1.call-start = ((), (), s32[]{:S(2)}) async-start(), calls=%async_computation.7 | async-start | bytes 4866048 | tf_op jit(solution)/shard_map/reduce_scatter | solution.py:1114
  317.8 43.0 %collective-permute-start.29 = (bf16[384,1408]{1,0:T(8,128)(2,1)S(1)}, bf16[384,1408]{1,0:T(8,128)(2,1)}, u32[]{:S(2)}, u32[]{:S(2)}) collective-permute-start(bf16[384,1408]{1,0:T(8,128)(2,1)S(1)} %copy-done.22), channel_id=1, source_target_pairs={{0,1},{1,0},{2,3},{3,2},{4,5},{5,4},{6,7},{7,6},{8,9},{9,8},{10,11... | collective-permute-start | bytes 3244040 | tf_op jit(solution)/shard_map/ppermute | solution.py:452
  367.8 53.9 %collective-permute-start.32 = (bf16[384,1408]{1,0:T(8,128)(2,1)}, bf16[384,1408]{1,0:T(8,128)(2,1)}, u32[]{:S(2)}, u32[]{:S(2)}) collective-permute-start(bf16[384,1408]{1,0:T(8,128)(2,1)} %add_convert_fusion.6), channel_id=1, source_target_pairs={{0,1},{1,0},{2,3},{3,2},{4,5},{5,4},{6,7},{7,6},{8,9},{9,8},{10,11... | collective-permute-start | bytes 3244040 | tf_op jit(solution)/shard_map/ppermute | solution.py:452
  373.9 47.8 %collective-permute-start.33 = (bf16[384,1408]{1,0:T(8,128)(2,1)}, bf16[384,1408]{1,0:T(8,128)(2,1)}, u32[]{:S(2)}, u32[]{:S(2)}) collective-permute-start(bf16[384,1408]{1,0:T(8,128)(2,1)} %add_convert_fusion.6), channel_id=1, source_target_pairs={{0,2},{1,3},{2,0},{3,1},{4,6},{5,7},{6,4},{7,5},{8,10},{9,11},{10,... | collective-permute-start | bytes 3244040 | tf_op jit(solution)/shard_map/ppermute | solution.py:452
  430.5 44.8 %collective-permute-start.36 = (bf16[2816,352]{0,1:T(8,128)(2,1)}, bf16[2816,352]{0,1:T(8,128)(2,1)S(1)}, u32[]{:S(2)}, u32[]{:S(2)}) collective-permute-start(bf16[2816,352]{0,1:T(8,128)(2,1)} %copy.92), channel_id=1, source_target_pairs={{0,2},{1,3},{2,0},{3,1},{4,6},{5,7},{6,4},{7,5},{8,10},{9,11},{10,... | collective-permute-start | bytes 5947400 | tf_op jit(solution)/shard_map/ppermute | solution.py:452
  431.7 55.7 %collective-permute-start.35 = (bf16[2816,352]{0,1:T(8,128)(2,1)}, bf16[2816,352]{0,1:T(8,128)(2,1)S(1)}, u32[]{:S(2)}, u32[]{:S(2)}) collective-permute-start(bf16[2816,352]{0,1:T(8,128)(2,1)} %copy.92), channel_id=1, source_target_pairs={{0,1},{1,0},{2,3},{3,2},{4,5},{5,4},{6,7},{7,6},{8,9},{9,8},{10,11... | collective-permute-start | bytes 5947400 | tf_op jit(solution)/shard_map/ppermute | solution.py:452
  517.2 273.3 %reduce-scatter.6.cloned.1.call-start = ((), (), s32[]{:S(2)}) async-start(), calls=%async_computation.8 | async-start | bytes 4866048 | tf_op jit(solution)/shard_map/reduce_scatter | solution.py:1109
  582.0 59.4 %collective-permute-start.46 = (bf16[8,2,112,1408]{3,2,1,0:T(8,128)(2,1)}, bf16[8,2,112,1408]{3,2,1,0:T(8,128)(2,1)}, u32[]{:S(2)}, u32[]{:S(2)}) collective-permute-start(bf16[8,2,112,1408]{3,2,1,0:T(8,128)(2,1)} %dynamic-slice_bitcast_fusion), channel_id=1, source_target_pairs={{0,1},{1,0},{2,3},{3,2},{4,5},{5,4},{6,7},{7,6},{8,9},{9,8},{10,11... | collective-permute-start | bytes 15138824 | tf_op jit(solution)/shard_map/ppermute | solution.py:452
  603.0 377.3 %reduce-scatter.8.cloned.1.call-start = ((), (), s32[]{:S(2)}) async-start(), calls=%async_computation.9 | async-start | bytes 4866048 | tf_op jit(solution)/shard_map/reduce_scatter | solution.py:1152
  651.0 54.7 %collective-permute-start.48 = (bf16[8,1,112,1408]{3,2,1,0:T(8,128)(2,1)}, bf16[8,1,112,1408]{3,2,1,0:T(8,128)(2,1)}, u32[]{:S(2)}, u32[]{:S(2)}) collective-permute-start(bf16[8,1,112,1408]{3,2,1,0:T(8,128)(2,1)} %constant_dynamic-slice_fusion.6), channel_id=1, source_target_pairs={{0,2},{1,3},{2,0},{3,1},{4,6},{5,7},{6,4},{7,5},{8,10},{9,11},{10,... | collective-permute-start | bytes 7569416 | tf_op jit(solution)/shard_map/ppermute | solution.py:452
  652.5 48.3 %collective-permute-start.49 = (bf16[8,2,48,1408]{3,2,1,0:T(8,128)(2,1)}, bf16[8,2,48,1408]{3,2,1,0:T(8,128)(2,1)}, u32[]{:S(2)}, u32[]{:S(2)}) collective-permute-start(bf16[8,2,48,1408]{3,2,1,0:T(8,128)(2,1)} %dynamic-slice_bitcast_fusion.1), channel_id=1, source_target_pairs={{0,1},{1,0},{2,3},{3,2},{4,5},{5,4},{6,7},{7,6},{8,9},{9,8},{10,11... | collective-permute-start | bytes 6488072 | tf_op jit(solution)/shard_map/ppermute | solution.py:452
  657.3 43.5 %collective-permute-start.47 = (bf16[2,2,48,1408]{3,2,1,0:T(8,128)(2,1)}, bf16[2,2,48,1408]{3,2,1,0:T(8,128)(2,1)}, u32[]{:S(2)}, u32[]{:S(2)}) collective-permute-start(bf16[2,2,48,1408]{3,2,1,0:T(8,128)(2,1)} %dynamic-slice_bitcast_fusion.8), channel_id=1, source_target_pairs={{0,8},{4,12},{8,0},{12,4},{16,24},{20,28},{24,16},{28,20},{1,9},{5... | collective-permute-start | bytes 1622024 | tf_op jit(solution)/shard_map/ppermute | solution.py:452
  753.2 51.2 %collective-permute-start.58 = (bf16[1,2,48,1408]{3,2,1,0:T(8,128)(2,1)}, bf16[1,2,48,1408]{3,2,1,0:T(8,128)(2,1)}, u32[]{:S(2)}, u32[]{:S(2)}) collective-permute-start(bf16[1,2,48,1408]{3,2,1,0:T(8,128)(2,1)} %constant_dynamic-slice_fusion.5), channel_id=1, source_target_pairs={{0,16},{4,20},{8,24},{12,28},{16,0},{20,4},{24,8},{28,12},{1,17},{... | collective-permute-start | bytes 811016 | tf_op jit(solution)/shard_map/ppermute | solution.py:452
  756.1 67.7 %collective-permute-start.61 = (bf16[176,1536]{1,0:T(8,128)(2,1)}, bf16[176,1536]{1,0:T(8,128)(2,1)}, u32[]{:S(2)}, u32[]{:S(2)}) collective-permute-start(bf16[176,1536]{1,0:T(8,128)(2,1)} %reduce-scatter.4.cloned.1.call-done.refs_0_), channel_id=1, source_target_pairs={{0,1},{1,0},{2,3},{3,2},{4,5},{5,4},{6,7},{7,6},{8,9},{9,8},{10,11... | collective-permute-start | bytes 1622024 | tf_op jit(solution)/shard_map/ppermute | solution.py:452
  804.5 45.6 %collective-permute-start.65 = (bf16[384,1408]{1,0:T(8,128)(2,1)}, bf16[384,1408]{1,0:T(8,128)(2,1)}, u32[]{:S(2)}, u32[]{:S(2)}) collective-permute-start(bf16[384,1408]{1,0:T(8,128)(2,1)} %add_convert_fusion.2), channel_id=1, source_target_pairs={{0,2},{1,3},{2,0},{3,1},{4,6},{5,7},{6,4},{7,5},{8,10},{9,11},{10,... | collective-permute-start | bytes 3244040 | tf_op jit(solution)/shard_map/ppermute | solution.py:452
  816.2 56.4 %collective-permute-start.59 = (bf16[4,1,112,1408]{3,2,0,1:T(8,128)(2,1)S(1)}, bf16[4,1,112,1408]{3,2,0,1:T(8,128)(2,1)}, u32[]{:S(2)}, u32[]{:S(2)}) collective-permute-start(bf16[4,1,112,1408]{3,2,0,1:T(8,128)(2,1)S(1)} %dynamic-slice_bitcast_fusion.3), channel_id=1, source_target_pairs={{0,4},{4,0},{8,12},{12,8},{16,20},{20,16},{24,28},{28,24},{1,5},{5... | collective-permute-start | bytes 3784712 | tf_op jit(solution)/shard_map/ppermute | solution.py:452
  823.8 48.7 %collective-permute-start.63 = (bf16[192,1408]{1,0:T(8,128)(2,1)}, bf16[192,1408]{1,0:T(8,128)(2,1)}, u32[]{:S(2)}, u32[]{:S(2)}) collective-permute-start(bf16[192,1408]{1,0:T(8,128)(2,1)} %reduce-scatter.6.cloned.1.call-done.refs_0_), channel_id=1, source_target_pairs={{0,1},{1,0},{2,3},{3,2},{4,5},{5,4},{6,7},{7,6},{8,9},{9,8},{10,11... | collective-permute-start | bytes 1622024 | tf_op jit(solution)/shard_map/ppermute | solution.py:452
  826.9 45.6 %collective-permute-start.64 = (bf16[192,1408]{1,0:T(8,128)(2,1)}, bf16[192,1408]{1,0:T(8,128)(2,1)}, u32[]{:S(2)}, u32[]{:S(2)}) collective-permute-start(bf16[192,1408]{1,0:T(8,128)(2,1)} %reduce-scatter.6.cloned.1.call-done.refs_0_), channel_id=1, source_target_pairs={{0,2},{1,3},{2,0},{3,1},{4,6},{5,7},{6,4},{7,5},{8,10},{9,11},{10,... | collective-permute-start | bytes 1622024 | tf_op jit(solution)/shard_map/ppermute | solution.py:452
  850.1 45.6 %collective-permute-start.66 = (bf16[4,352,352]{2,1,0:T(8,128)(2,1)}, bf16[4,352,352]{2,1,0:T(8,128)(2,1)S(1)}, u32[]{:S(2)}, u32[]{:S(2)}) collective-permute-start(bf16[4,352,352]{2,1,0:T(8,128)(2,1)} %get-tuple-element.260), channel_id=1, source_target_pairs={{0,4},{4,0},{8,12},{12,8},{16,20},{20,16},{24,28},{28,24},{1,5},{5... | collective-permute-start | bytes 2973704 | tf_op jit(solution)/shard_map/ppermute | solution.py:452
  (220 other events, 3652.5 us)
Sparse Core Ops, SparseCore 0:
  10.8 61.6 all-gather.4
  74.7 91.7 all-gather.6
  267.0 78.7 all-gather.8
  348.4 73.2 all-gather.10
  517.3 86.8 reduce-scatter.3
  608.1 93.0 reduce-scatter.5
  757.0 100.1 reduce-scatter.7
